TPU v7x, 128 devices: a whole 4x4x4 slice. The times are simulated.
128 devices in a mesh: lon: 16 (over z_lo, x, core), lat: 8 (over y, z_hi).
Axes of the slice: x: 4, y: 4, z: 4 (z_hi: 2, z_lo: 2; z = z_hi * 2 + z_lo), core: 2. Of those that a mesh axis runs over, the one named last changes fastest.
Arguments:
- final_cotangent: float32 [4, 256, 256, 256], P(None, 'lon', 'lat'), may hold values from -6 to 6
- saved_start: bfloat16 [4, 256, 256, 256], P(None, 'lon', 'lat'), may hold values from 0.049804688 to 2
- saved_middle: bfloat16 [4, 256, 256, 256], P(None, 'lon', 'lat'), may hold values from 0.049804688 to 2
- residuals: float32 [2, 4096], P(None, ('lon', 'lat')), may hold values from -6 to 6
- row_cells: int32 [4096, 16], P(('lon', 'lat')), may hold values from 0 to 65535, as said below
- row_count: int32 [4096], P(('lon', 'lat')), may hold values from 1 to 16, as said below
- ocean_mask: int32 [256, 256], P('lon', 'lat'), may hold values 0 or 1
- cell_eez: int32 [256, 256], P('lon', 'lat'), may hold values from 0 to 63
- effort: float32 [64], replicated, may hold values from 0.1 to 2
- kernel: bfloat16 [4, 256, 256], replicated, may hold values from 0.00038909912 to 0.015625
- mix: float32 [4, 4], replicated, may hold values from 0.1 to 1
- assim: float32 [4], replicated, may hold values from 0.2 to 0.8
- mortality: float32 [4, 256], replicated, may hold values from 0.02 to 0.5
- select: float32 [4, 256], replicated, may hold values from 0.05 to 1
- weight: float32 [256], replicated, may hold values from 0.1 to 4
- spread: float32 [256], replicated, may hold values from 0.01 to 0.2
Outputs:
- start_cotangent: float32 [4, 256, 256, 256], P(None, 'lon', 'lat')
- kernel_grad: float32 [4, 256, 256], replicated
- effort_grad: float32 [64], replicated
Inputs may be any that keep to these rules, and one draw needn't show every extreme that they name: `row_cells`: all 16 entries of a row, counted or not, name cells. Of the 512 entries of the rows of one device, at most 8 name cells of one device's tile, and on every device some tile is named by exactly 8 of them. `row_count`: on every device some row uses all 16 cells.
All inputs are finite; a program needn't handle non-finite values. No bound on the sum of `ocean_mask` on one device may be relied on, other than what follows from the above.
Results may differ from a plain program's by a relative error of at most 0.0035.
Values sent between devices are 32-bit elements; how exact they have to be, the bound alone decides.
No kernel may reach another device: no remote copies, remote signals or barrier semaphores. Data moves between devices by JAX's collectives and lax.ppermute only.
A program may use at most 128 MiB of HBM per device.

v0:
```python
import jax
import jax.numpy as jnp
from jax import lax
from jax.sharding import PartitionSpec as P

EEZS = 64


step_length = 0.5


def with_halo(cells, sides, width, closed):
    for axis, dim in sides:
        count = lax.axis_size(axis)
        ends = count if closed else count - 1
        head = lax.slice_in_dim(cells, 0, width, axis=dim)
        tail = lax.slice_in_dim(cells, cells.shape[dim] - width, cells.shape[dim], axis=dim)
        cells = jnp.concatenate(
            [
                lax.ppermute(tail, axis, [(i, (i + 1) % count) for i in range(ends)]),
                cells,
                lax.ppermute(head, axis, [((i + 1) % count, i) for i in range(ends)]),
            ],
            axis=dim,
        )
    return cells


def mix_groups(matrix, field):
    total = matrix[:, 0][:, None, None, None] * field[0]
    for source in range(1, field.shape[0]):
        total = total + matrix[:, source][:, None, None, None] * field[source]
    return total


def with_rims(field):
    cycle = with_halo(field, (("lon", 1),), 1, True)
    band = with_halo(field, (("lat", 2),), 1, False)
    return (cycle, band)


def move_back(cotan, ocean, ocean_cycle, ocean_band, spread):
    cycle, band = with_rims(cotan)
    flux = ocean_cycle[:, 2:] * (cycle[:, 2:] - cotan) + ocean_cycle[:, :-2] * (
        cycle[:, :-2] - cotan
    )
    flux = (
        flux
        + ocean_band[:, :, 2:] * (band[:, :, 2:] - cotan)
        + ocean_band[:, :, :-2] * (band[:, :, :-2] - cotan)
    )
    return cotan + spread * ocean * flux


def local_adjoint(
    back, saved, ocean, effort_cell, catch_cot, kernel, mix, assim, mortality, select, weight
):
    state = saved.astype(jnp.float32)
    prey = mix_groups(mix, state).astype(jnp.bfloat16)
    encounter = jnp.einsum("gxyz,gwz->gxyw", prey, kernel, preferred_element_type=jnp.float32)
    feed = encounter / (encounter + 1.0)
    eaten = (state * feed).astype(jnp.bfloat16)
    removal = jnp.einsum("gxyw,gwz->gxyz", eaten, kernel, preferred_element_type=jnp.float32)
    loss_rate = mix_groups(mix.T, removal)
    rate = (
        assim[:, None, None, None] * feed
        - mortality[:, None, None, :]
        - loss_rate
        - select[:, None, None, :] * effort_cell
    )
    masked = ocean * back
    grad_rate = step_length * masked * state
    grad_removal = mix_groups(mix, -grad_rate).astype(jnp.bfloat16)
    grad_eaten = jnp.einsum(
        "gxyz,gwz->gxyw", grad_removal, kernel, preferred_element_type=jnp.float32
    )
    grad_feed = assim[:, None, None, None] * grad_rate + grad_eaten * state
    grad_enc = (grad_feed / ((encounter + 1.0) * (encounter + 1.0))).astype(jnp.bfloat16)
    grad_prey = jnp.einsum("gxyw,gwz->gxyz", grad_enc, kernel, preferred_element_type=jnp.float32)
    catch_gain = (select * weight[None, :])[:, None, None, :]
    grad_state = (
        masked * (1.0 + step_length * rate) + grad_eaten * feed + mix_groups(mix.T, grad_prey)
    )
    grad_state = grad_state + step_length * ocean * effort_cell * catch_gain * catch_cot
    kernel_part = jnp.einsum(
        "gxyw,gxyz->gwz", eaten, grad_removal, preferred_element_type=jnp.float32
    )
    kernel_part = kernel_part + jnp.einsum(
        "gxyw,gxyz->gwz", grad_enc, prey, preferred_element_type=jnp.float32
    )
    cell_part = -jnp.sum(select[:, None, None, :] * grad_rate, axis=(0, 3), keepdims=True)
    cell_part = cell_part + step_length * ocean * catch_cot * jnp.sum(
        catch_gain * state, axis=(0, 3), keepdims=True
    )
    return (grad_state, kernel_part, cell_part)


def body(
    final_cotangent,
    saved_start,
    saved_middle,
    residuals,
    row_cells,
    row_count,
    ocean_mask,
    cell_eez,
    effort,
    kernel,
    mix,
    assim,
    mortality,
    select,
    weight,
    spread,
):
    width_lon = final_cotangent.shape[1]
    width_lat = final_cotangent.shape[2]
    n_lon = lax.axis_size("lon")
    n_lat = lax.axis_size("lat")
    devices_all = n_lon * n_lat
    cells_dev = width_lon * width_lat
    ocean = ocean_mask.astype(jnp.float32)[None, :, :, None]
    ocean_cycle, ocean_band = with_rims(ocean)
    onehot = cell_eez[:, :, None] == jnp.arange(EEZS, dtype=jnp.int32)[None, None, :]
    effort_cell = jnp.sum(jnp.where(onehot, effort[None, None, :], 0.0), axis=-1)[None, :, :, None]
    total_lat = width_lat * n_lat
    lon_index = row_cells // total_lat
    lat_index = row_cells % total_lat
    owner = lon_index // width_lon * n_lat + lat_index // width_lat
    local = lon_index % width_lon * width_lat + lat_index % width_lat
    entries = row_cells.shape[1]
    valid = jnp.arange(entries, dtype=jnp.int32)[None, :] < row_count[:, None]
    values = jnp.where(valid[None], residuals[:, :, None], 0.0)
    position = owner * cells_dev + local
    field_all = (
        jnp.zeros((2, devices_all * cells_dev), jnp.float32)
        .at[:, position.reshape(-1)]
        .add(values.reshape(2, -1))
    )
    catch_cot = lax.psum_scatter(field_all, ("lon", "lat"), scatter_dimension=1, tiled=True)
    cotan = final_cotangent
    kernel_total = jnp.zeros(kernel.shape, jnp.float32)
    effort_total = jnp.zeros((EEZS,), jnp.float32)
    for step, saved in ((1, saved_middle), (0, saved_start)):
        back = move_back(cotan, ocean, ocean_cycle, ocean_band, spread)
        step_cot = catch_cot[step].reshape(1, width_lon, width_lat, 1)
        cotan, kernel_part, cell_part = local_adjoint(
            back, saved, ocean, effort_cell, step_cot, kernel, mix, assim, mortality, select, weight
        )
        effort_part = jnp.sum(jnp.where(onehot, cell_part[0], 0.0), axis=(0, 1))
        kernel_sum, effort_sum = lax.psum((kernel_part, effort_part), ("lon", "lat"))
        kernel_total = kernel_total + kernel_sum
        effort_total = effort_total + effort_sum
    return (cotan, kernel_total, effort_total)


def solution(mesh):
    placed = (
        P(None, "lon", "lat", None),
        P(None, "lon", "lat", None),
        P(None, "lon", "lat", None),
        P(None, ("lon", "lat")),
        P(("lon", "lat"), None),
        P(("lon", "lat")),
        P("lon", "lat"),
        P("lon", "lat"),
        P(),
        P(),
        P(),
        P(),
        P(),
        P(),
        P(),
        P(),
    )
    return jax.shard_map(
        body,
        mesh=mesh,
        in_specs=placed,
        out_specs=(P(None, "lon", "lat", None), P(), P()),
        check_vma=False,
    )
```

profile of v0, /device:TPU:1, one launch (start us, length us, event | category | flops | bytes accessed | tf_op | source)
XLA Modules:
  0.0 987.9 jit_solution(5171123901016059930)
XLA Ops:
  8.6 6.3 collective-permute-start.7
  17.0 5.5 collective-permute-start.6
  23.5 2.7 collective-permute-start.3
  28.9 15.4 %scatter_custom_fusion = f32[2,65536]{0,1:T(8,128)} fusion(s32[512]{0:T(512)S(1)} %bitcast.137, f32[]{:T(128)} %constant.67.clone.1, f32[2,512]{0,1:T(8,128)S(1)} %bitcast_select_fusion), kind=kCustom, calls=%fused_computation.1 | custom fusion | flops 1024 | bytes 786436 | tf_op jit(solution)/shard_map/scatter-add | solution.py:138
  47.8 1.4 slice_bitcast_fusion.15
  49.6 2.8 collective-permute-start
  53.3 1.5 collective-permute-start.5
  54.9 9.4 collective-permute-done.5
  64.3 2.5 fusion.49
  71.6 2.1 slice_bitcast_fusion.19
  73.6 711.5 %reduce-scatter.2.cloned.1.call-done = f32[2,512]{0,1:T(8,128)} async-done(((f32[2,65536]{0,1:T(8,128)}), f32[2,512]{0,1:T(8,128)}) %reduce-scatter.2.cloned.1.call-update) | async-done | bytes 4112 | tf_op jit(solution)/shard_map/reduce_scatter | solution.py:140
  785.1 1.9 slice_reduce_fusion
  787.3 4.9 fusion.9
  793.7 2.9 collective-permute-start.11
  797.9 6.7 collective-permute-start.8
  804.7 2.2 convolution_bitcast_fusion.3
  808.3 6.8 multiply_reduce_fusion.3
  817.8 1.4 fusion.17
  823.4 1.4 slice_bitcast_fusion.11
  827.1 2.0 fusion.47
  829.5 69.3 %psum.33 = f32[64]{0:T(128)} all-reduce(f32[64]{0:T(128)S(1)} %add.264), channel_id=1, replica_groups=mesh['lon'=16,'lat'=8] {'lon','lat'}, use_global_device_ids=true, to_apply=%region_8.9 | all-reduce | flops 64 | bytes 512 | tf_op jit(solution)/shard_map/psum | solution.py:151
  898.9 5.5 fusion.15
  904.5 74.3 %all-reduce.2.cloned.1.call-done = f32[4,256,256]{2,1,0:T(8,128)} async-done(((f32[4,256,256]{2,1,0:T(8,128)}), f32[4,256,256]{2,1,0:T(8,128)}) %all-reduce.2.cloned.1.call-update) | async-done | bytes 1048592 | tf_op jit(solution)/shard_map/psum | solution.py:151
  978.8 2.3 copy.30
  (232 shorter events, 30.0 us)
Async XLA Ops:
  7.2 777.9 %reduce-scatter.2.cloned.1.call-start = ((), (), s32[]{:S(2)}) async-start(), calls=%async_computation.1 | async-start | bytes 33816576 | tf_op jit(solution)/shard_map/reduce_scatter | solution.py:140
  8.6 46.3 %collective-permute-start.7 = (f32[4,16,1,256]{3,2,1,0:T(1,128)S(1)}, f32[4,16,1,256]{3,2,1,0:T(1,128)S(1)}, u32[]{:S(2)}, u32[]{:S(2)}) collective-permute-start(f32[4,16,1,256]{3,2,1,0:T(1,128)S(1)} %get-tuple-element.59), channel_id=1, source_target_pairs={{0,1},{1,2},{2,3},{3,4},{4,5},{5,6},{6,7},{8,9},{9,10},{10,11},{11... | collective-permute-start | bytes 196616 | tf_op jit(solution)/shard_map/ppermute | solution.py:20
  15.7 33.9 %collective-permute-start.4 = (f32[1,16,1,1]{2,1,3,0:T(8,128)S(1)}, f32[1,16,1,1]{2,1,3,0:T(8,128)S(1)}, u32[]{:S(2)}, u32[]{:S(2)}) collective-permute-start(f32[1,16,1,1]{2,1,3,0:T(8,128)S(1)} %get-tuple-element.70), channel_id=1, source_target_pairs={{1,0},{2,1},{3,2},{4,3},{5,4},{6,5},{7,6},{9,8},{10,9},{11,10},{12... | collective-permute-start | bytes 200 | tf_op jit(solution)/shard_map/ppermute | solution.py:22
  17.0 35.5 %collective-permute-start.6 = (f32[1,16,1,1]{2,1,3,0:T(8,128)S(1)}, f32[1,16,1,1]{2,1,3,0:T(8,128)S(1)}, u32[]{:S(2)}, u32[]{:S(2)}) collective-permute-start(f32[1,16,1,1]{2,1,3,0:T(8,128)S(1)} %get-tuple-element.71), channel_id=1, source_target_pairs={{0,1},{1,2},{2,3},{3,4},{4,5},{5,6},{6,7},{8,9},{9,10},{10,11},{11... | collective-permute-start | bytes 200 | tf_op jit(solution)/shard_map/ppermute | solution.py:20
  23.5 40.8 %collective-permute-start.3 = (f32[4,1,32,256]{3,2,1,0:T(8,128)S(1)}, f32[4,1,32,256]{3,2,1,0:T(8,128)S(1)}, u32[]{:S(2)}, u32[]{:S(2)}) collective-permute-start(f32[4,1,32,256]{3,2,1,0:T(8,128)S(1)} %get-tuple-element.57), channel_id=1, source_target_pairs={{0,8},{8,16},{16,24},{24,32},{32,40},{40,48},{48,56},{56,64},{64,7... | collective-permute-start | bytes 393224 | tf_op jit(solution)/shard_map/ppermute | solution.py:20
  26.2 38.1 %collective-permute-start.1 = (f32[4,1,32,256]{3,2,1,0:T(8,128)S(1)}, f32[4,1,32,256]{3,2,1,0:T(8,128)S(1)}, u32[]{:S(2)}, u32[]{:S(2)}) collective-permute-start(f32[4,1,32,256]{3,2,1,0:T(8,128)S(1)} %get-tuple-element.56), channel_id=1, source_target_pairs={{8,0},{16,8},{24,16},{32,24},{40,32},{48,40},{56,48},{64,56},{72,6... | collective-permute-start | bytes 393224 | tf_op jit(solution)/shard_map/ppermute | solution.py:22
  44.3 934.5 %all-reduce.2.cloned.1.call-start = ((), (), s32[]{:S(2)}) async-start(), calls=%async_computation.2 | async-start | bytes 2097152 | tf_op jit(solution)/shard_map/psum | solution.py:151
  45.6 741.5 %copy-start.37 = (f32[16,32]{1,0:T(8,128)}, f32[16,32]{1,0:T(8,128)S(1)}, u32[]{:S(2)}) copy-start(f32[16,32]{1,0:T(8,128)S(1)} %multiply_multiply_fusion.4) | copy-start | bytes 6148
  47.5 739.6 %copy-start.57 = (f32[4]{0:T(128)}, f32[4]{0:T(128)S(1)}, u32[]{:S(2)}) copy-start(f32[4]{0:T(128)S(1)} %get-tuple-element.72) | copy-start | bytes 52
  47.5 739.6 %copy-start.59 = (f32[4]{0:T(128)}, f32[4]{0:T(128)S(1)}, u32[]{:S(2)}) copy-start(f32[4]{0:T(128)S(1)} %get-tuple-element.73) | copy-start | bytes 52
  47.5 739.6 %copy-start.61 = (f32[4]{0:T(128)}, f32[4]{0:T(128)S(1)}, u32[]{:S(2)}) copy-start(f32[4]{0:T(128)S(1)} %get-tuple-element.74) | copy-start | bytes 52
  47.5 739.6 %copy-start.63 = (f32[4]{0:T(128)}, f32[4]{0:T(128)S(1)}, u32[]{:S(2)}) copy-start(f32[4]{0:T(128)S(1)} %get-tuple-element.75) | copy-start | bytes 52
  49.3 737.8 %copy-start.50 = (f32[4,256]{1,0:T(4,128)}, f32[4,256]{1,0:T(4,128)S(1)}, u32[]{:S(2)}) copy-start(f32[4,256]{1,0:T(4,128)S(1)} %broadcast_multiply_fusion.1) | copy-start | bytes 12292
  49.6 3.6 collective-permute-start
  52.4 2.3 collective-permute-start.2
  53.3 11.0 %collective-permute-start.5 = (f32[4,16,1,256]{3,2,1,0:T(1,128)S(1)}, f32[4,16,1,256]{3,2,1,0:T(1,128)S(1)}, u32[]{:S(2)}, u32[]{:S(2)}) collective-permute-start(f32[4,16,1,256]{3,2,1,0:T(1,128)S(1)} %get-tuple-element.58), channel_id=1, source_target_pairs={{1,0},{2,1},{3,2},{4,3},{5,4},{6,5},{7,6},{9,8},{10,9},{11,10},{12... | collective-permute-start | bytes 196616 | tf_op jit(solution)/shard_map/ppermute | solution.py:22
  71.6 715.6 %copy-start.55 = (f32[4,256]{1,0:T(4,128)S(1)}, f32[4,256]{1,0:T(4,128)}, u32[]{:S(2)}) copy-start(f32[4,256]{1,0:T(4,128)} %param.28) | copy-start | bytes 12292
  793.7 14.6 %collective-permute-start.11 = (f32[4,16,1,256]{3,2,1,0:T(1,128)}, f32[4,16,1,256]{3,2,1,0:T(1,128)}, u32[]{:S(2)}, u32[]{:S(2)}) collective-permute-start(f32[4,16,1,256]{3,2,1,0:T(1,128)} %get-tuple-element.39), channel_id=1, source_target_pairs={{0,1},{1,2},{2,3},{3,4},{4,5},{5,6},{6,7},{8,9},{9,10},{10,11},{11... | collective-permute-start | bytes 196616 | tf_op jit(solution)/shard_map/ppermute | solution.py:20
  796.6 11.7 %collective-permute-start.10 = (f32[4,16,1,256]{3,2,1,0:T(1,128)}, f32[4,16,1,256]{3,2,1,0:T(1,128)}, u32[]{:S(2)}, u32[]{:S(2)}) collective-permute-start(f32[4,16,1,256]{3,2,1,0:T(1,128)} %get-tuple-element.38), channel_id=1, source_target_pairs={{1,0},{2,1},{3,2},{4,3},{5,4},{6,5},{7,6},{9,8},{10,9},{11,10},{12... | collective-permute-start | bytes 196616 | tf_op jit(solution)/shard_map/ppermute | solution.py:22
  797.8 10.5 %collective-permute-start.9 = (f32[4,1,32,256]{3,2,1,0:T(8,128)}, f32[4,1,32,256]{3,2,1,0:T(8,128)S(1)}, u32[]{:S(2)}, u32[]{:S(2)}) collective-permute-start(f32[4,1,32,256]{3,2,1,0:T(8,128)} %get-tuple-element.37), channel_id=1, source_target_pairs={{0,8},{8,16},{16,24},{24,32},{32,40},{40,48},{48,56},{56,64},{64,7... | collective-permute-start | bytes 393224 | tf_op jit(solution)/shard_map/ppermute | solution.py:20
  797.9 10.4 %collective-permute-start.8 = (f32[4,1,32,256]{3,2,1,0:T(8,128)S(1)}, f32[4,1,32,256]{3,2,1,0:T(8,128)S(1)}, u32[]{:S(2)}, u32[]{:S(2)}) collective-permute-start(f32[4,1,32,256]{3,2,1,0:T(8,128)S(1)} %get-tuple-element.36), channel_id=1, source_target_pairs={{8,0},{16,8},{24,16},{32,24},{40,32},{48,40},{56,48},{64,56},{72,6... | collective-permute-start | bytes 393224 | tf_op jit(solution)/shard_map/ppermute | solution.py:22
  827.1 71.8 %copy-start.2 = (f32[4,16,32,256]{3,2,1,0:T(8,128)S(1)}, f32[4,16,32,256]{3,2,1,0:T(8,128)}, u32[]{:S(2)}) copy-start(f32[4,16,32,256]{3,2,1,0:T(8,128)} %copy-done.1) | copy-start | bytes 6291460
  827.1 71.8 %copy-start.38 = (f32[16,32]{1,0:T(8,128)S(1)}, f32[16,32]{1,0:T(8,128)}, u32[]{:S(2)}) copy-start(f32[16,32]{1,0:T(8,128)} %copy-done.37) | copy-start | bytes 6148
  827.1 71.8 %copy-start.49 = (f32[4,256]{1,0:T(4,128)S(1)}, f32[4,256]{1,0:T(4,128)}, u32[]{:S(2)}) copy-start(f32[4,256]{1,0:T(4,128)} %param.29) | copy-start | bytes 12292
  (73 other events, 991.8 us)
Sparse Core Ops, SparseCore 0:
  44.5 740.6 reduce-scatter.1
  829.3 149.4 all-reduce.1
where the time goes:
time: 989 us; the launch traced here: 988 us
  waiting for transfers between devices  796 us (80%)
  blocking collectives  69.3 us (7%)
  other arithmetic  38.4 us (4%)
  starting transfers between devices  31.1 us (3%)
  local copies, waits for them, and re-layouts  25.3 us (3%)
  between operations  15.2 us (2%)
  matrix products  12.5 us (1%)
    reduce_scatter x1, waiting for transfers between devices, body(): lax.psum_scatter(field_all, ('lon', 'lat'), scatter_dimension=1, tiled=True)  711 us
    psum x1, waiting for transfers between devices, body(): lax.psum((kernel_part, effort_part), ('lon', 'lat'))  74.3 us
    psum x1, blocking collectives, body(): lax.psum((kernel_part, effort_part), ('lon', 'lat'))  69.3 us
  transfers between devices with their start and end apart: 14, of which 4 were waited for; matrix products, arithmetic and copies ran while one was open for 4% of the time, Pallas kernels for 0%

commit v1 on v0

v1 whole, which is shorter than its diff:
```python
import functools

import jax
import jax.numpy as jnp
from jax import lax
from jax.experimental import pallas as pl
from jax.experimental.pallas import tpu as pltpu
from jax.sharding import Mesh, PartitionSpec as P

G, Z = 4, 256
CI, CJ = 16, 32
N = CI * CJ
EEZS = 64
H = 0.5
SLOTS = 8
F32, BF16 = jnp.float32, jnp.bfloat16
LON, LAT = ("zl", "x", "c"), ("y", "zh")
ALL = LON + LAT
CHIPS = ("zl", "x", "y", "zh")
NCHIP = 64
MIB = 1024 * 1024
HI = lax.Precision.HIGHEST

LON_A = [(i, i ^ 1) for i in range(16)]
LON_B = [(i, (i + 1) % 16 if i % 2 else (i - 1) % 16) for i in range(16)]
LAT_A = [(i, i ^ 1) for i in range(8)]
LAT_B = [(i, i + 1 if i % 2 else i - 1) for i in range(1, 7)]
CORE = [(0, 1), (1, 0)]


def sds(shape, dtype=F32):
    return jax.ShapeDtypeStruct(shape, dtype)


def vm():
    return pl.BlockSpec(memory_space=pltpu.VMEM)


def sm():
    return pl.BlockSpec(memory_space=pltpu.SMEM)


def call(body, outs, ins, scratch=(), flops=0, nbytes=0, vmem=60):
    return pl.pallas_call(
        body,
        out_shape=outs,
        in_specs=ins,
        out_specs=jax.tree.map(lambda _: vm(), outs),
        scratch_shapes=list(scratch),
        compiler_params=pltpu.CompilerParams(vmem_limit_bytes=vmem * MIB),
        cost_estimate=pl.CostEstimate(flops=flops, bytes_accessed=nbytes, transcendentals=0),
    )


def nt(a, b, **kw):
    return lax.dot_general(a, b, (((1,), (1,)), ((), ())), preferred_element_type=F32, **kw)


def nn(a, b, **kw):
    return lax.dot_general(a, b, (((1,), (0,)), ((), ())), preferred_element_type=F32, **kw)


def tn(a, b, **kw):
    return lax.dot_general(a, b, (((0,), (0,)), ((), ())), preferred_element_type=F32, **kw)


def split(x):
    hi = x.astype(BF16).astype(F32)
    return hi, x - hi


def two(x):
    return jnp.concatenate([x, x], axis=1)


def column(row, n, width):
    eye = lax.broadcasted_iota(jnp.int32, (n, n), 0) == lax.broadcasted_iota(jnp.int32, (n, n), 1)
    col = jnp.sum(jnp.where(eye, jnp.broadcast_to(row, (n, n)), 0.0), axis=1, keepdims=True)
    return jnp.broadcast_to(col, (n, width))


def prep_body(c, ocean, cells, count, resid, la, lb, ta, tb, pay):
    par_i, par_j = lax.axis_index("c"), lax.axis_index("zh")
    oc = ocean[...].astype(F32)
    first_i = column(oc[0:1, :], CJ, Z)
    last_i = column(oc[CI - 1 : CI, :], CJ, Z)
    first_j = jnp.broadcast_to(oc[:, 0:1], (CI, Z))
    last_j = jnp.broadcast_to(oc[:, CJ - 1 : CJ], (CI, Z))

    def lon_rims(hi, lo):
        for g in range(G):
            hi[g] = c[g, CI - 1] * last_i
            lo[g] = c[g, 0] * first_i
        hi[G] = last_i
        lo[G] = first_i

    def lat_rims(hi, lo):
        for g in range(G):
            hi[g] = c[g, :, CJ - 1, :] * last_j
            lo[g] = c[g, :, 0, :] * first_j
        hi[G] = last_j
        lo[G] = first_j

    pl.when(par_i == 0)(lambda: lon_rims(la, lb))
    pl.when(par_i == 1)(lambda: lon_rims(lb, la))
    pl.when(par_j == 0)(lambda: lat_rims(ta, tb))
    pl.when(par_j == 1)(lambda: lat_rims(tb, ta))

    rows, ents = cells.shape
    ne = rows * ents
    devices = pay.shape[0]
    tile_e = lax.broadcasted_iota(jnp.int32, (ents, ne), 1) % ents == lax.broadcasted_iota(
        jnp.int32, (ents, ne), 0
    )
    tile_r = lax.broadcasted_iota(jnp.int32, (rows, ne), 1) // ents == lax.broadcasted_iota(
        jnp.int32, (rows, ne), 0
    )
    tile_ef, tile_rf = tile_e.astype(F32), tile_r.astype(F32)
    lon_i = (cells[...] // 256).astype(F32)
    lat_i = (cells[...] % 256).astype(F32)

    def flat(x):
        spread_out = nn(x, tile_ef, precision=HI)
        return jnp.sum(jnp.where(tile_r, spread_out, 0.0), axis=0, keepdims=True)

    i_row = flat(lon_i).astype(jnp.int32)
    j_row = flat(lat_i).astype(jnp.int32)
    n_row = nn(count[...].astype(F32), tile_rf, precision=HI)
    r_row = nn(resid[...], tile_rf, precision=HI)
    entry = (lax.broadcasted_iota(jnp.int32, (1, ne), 1) % ents).astype(F32)
    vals = jnp.where(entry < n_row, r_row, 0.0)
    owner = (i_row // CI) * 8 + j_row // CJ
    mine = lax.broadcasted_iota(jnp.int32, (devices, ne), 0) == owner
    mine_b = mine.astype(F32).astype(BF16)
    before = (
        lax.broadcasted_iota(jnp.int32, (ne, ne), 0) < lax.broadcasted_iota(jnp.int32, (ne, ne), 1)
    )
    ahead = nn(mine_b, before.astype(F32).astype(BF16))
    rank = jnp.sum(jnp.where(mine, ahead, 0.0), axis=0, keepdims=True).astype(jnp.int32)
    slot = lax.broadcasted_iota(jnp.int32, (SLOTS, ne), 0) == rank
    h0, l0 = split(vals[0:1])
    h1, l1 = split(vals[1:2])
    a_row = ((i_row % CI) * CJ).astype(F32)
    b_row = (j_row % CJ).astype(F32)

    def rows_of(parts):
        put = [jnp.where(slot, jnp.broadcast_to(p, (SLOTS, ne)), 0.0) for p in parts]
        put.append(jnp.zeros((128 - SLOTS * len(parts), ne), F32))
        return jnp.concatenate(put, axis=0).astype(BF16)

    pay[...] = nt(mine_b, rows_of((h0, h1, a_row))) + nt(mine_b, rows_of((l0, l1, b_row)))


def catch_body(pay, out, hot, hi, lo):
    got = pay[...]
    flip = got.T
    for k in range(SLOTS):
        where = flip[2 * SLOTS + k : 2 * SLOTS + k + 1, :].astype(jnp.int32)
        cell = lax.broadcasted_iota(jnp.int32, (N, 128), 0)
        hot[:, k * 128 : (k + 1) * 128] = (cell == where).astype(F32).astype(BF16)
        both = jnp.concatenate(
            [
                jnp.broadcast_to(got[:, k : k + 1], (128, 128)),
                jnp.broadcast_to(got[:, SLOTS + k : SLOTS + k + 1], (128, 128)),
            ],
            axis=1,
        )
        top, rest = split(both)
        hi[k * 128 : (k + 1) * 128, :] = top.astype(BF16)
        lo[k * 128 : (k + 1) * 128, :] = rest.astype(BF16)
    out[...] = nn(hot[...], hi[...]) + nn(hot[...], lo[...])


def cells_body(ocean, eez, effort, ocol, ecol, zone):
    oc = ocean[...].astype(F32)
    ez = eez[...].astype(F32)
    lane = lax.broadcasted_iota(jnp.int32, (CJ, 128), 1)
    eff = jnp.concatenate([effort[...], jnp.zeros((1, 128 - EEZS), F32)], axis=1)
    for i in range(CI):
        rows = slice(i * CJ, (i + 1) * CJ)
        ocol[rows] = column(oc[i : i + 1, :], CJ, 128)
        hot = (column(ez[i : i + 1, :], CJ, 128).astype(jnp.int32) == lane).astype(F32)
        zone[rows] = hot
        ecol[rows] = jnp.broadcast_to(jnp.sum(hot * eff, axis=1, keepdims=True), (CJ, 128))


def fwd_body(mix, assim, st, ker, mort, sel, wt, ecol, prey, eaten, feed, gain, gs, tmp):
    step = 16

    @pl.loop(0, N // step)
    def _(n):
        rows = pl.ds(n * step, step)
        s = [st[k, rows, :].astype(F32) for k in range(G)]
        part = None
        for k in range(G):
            term = (sel[k : k + 1, :] * wt[...]) * s[k]
            part = term if part is None else part + term
        gs[rows, :] = part[:, :128] + part[:, 128:]
        for g in range(G):
            tot = mix[g, 0] * s[0]
            for k in range(1, G):
                tot = tot + mix[g, k] * s[k]
            prey[g, rows, :] = tot.astype(BF16)

    for g in range(G):
        tmp[g] = nt(prey[g], ker[g])

    @pl.loop(0, N // step)
    def _(n):
        rows = pl.ds(n * step, step)
        for g in range(G):
            enc = tmp[g, rows, :]
            fd = enc / (enc + 1.0)
            feed[g, rows, :] = fd
            eaten[g, rows, :] = (st[g, rows, :].astype(F32) * fd).astype(BF16)

    for g in range(G):
        tmp[g] = nn(eaten[g], ker[g])

    @pl.loop(0, N // step)
    def _(n):
        rows = pl.ds(n * step, step)
        rem = [tmp[g, rows, :] for g in range(G)]
        ef = two(ecol[rows, :])
        for k in range(G):
            loss = mix[0, k] * rem[0]
            for g in range(1, G):
                loss = loss + mix[g, k] * rem[g]
            rate = assim[k] * feed[k, rows, :] - mort[k : k + 1, :] - loss - sel[k : k + 1, :] * ef
            gain[k, rows, :] = 1.0 + H * rate


def adj_body(last, t, *refs):
    (mix, assim, c, la, lb, ta, tb, ocol, ecol, catch, gs, zone, st, prey, eaten, feed, gain) = refs[:17]
    (ker, sel, wt, spr) = refs[17:21]
    refs = refs[21:]
    if last:
        near, kp_in, eff_in, c_out, keep, send = refs[:6]
        refs = refs[6:]
    else:
        c_out, kp, eff, near, ola, olb, ota, otb = refs[:8]
        opad = refs[8]
        refs = refs[9:]
    pad, m_scr, t_scr, grm, genc, y = refs
    par_i, par_j = lax.axis_index("c"), lax.axis_index("zh")
    at_a = jnp.where(par_i == 0, CI + 1, 0)
    at_b = CI + 1 - at_a
    row_a = jnp.where(par_j == 0, CJ + 8, 7)
    row_b = CJ + 15 - row_a

    for g in range(G):
        pad[g, at_a, 8 : 8 + CJ, :] = la[g]
        pad[g, at_b, 8 : 8 + CJ, :] = lb[g]
        for i in range(CI):
            pad[g, i + 1, pl.ds(row_a, 1), :] = ta[g, i : i + 1, :]
            pad[g, i + 1, pl.ds(row_b, 1), :] = tb[g, i : i + 1, :]
    if not last:
        opad[at_a, 8 : 8 + CJ, :] = la[G, :, :128]
        opad[at_b, 8 : 8 + CJ, :] = lb[G, :, :128]
        for i in range(CI):
            opad[i + 1, pl.ds(row_a, 1), :] = ta[G, i : i + 1, :128]
            opad[i + 1, pl.ds(row_b, 1), :] = tb[G, i : i + 1, :128]

    @pl.loop(0, CI)
    def _(i):
        rows = pl.ds(i * CJ, CJ)
        o = ocol[rows, :]
        if not last:
            opad[i + 1, 8 : 8 + CJ, :] = o
        o2 = two(o)
        for g in range(G):
            pad[g, i + 1, 8 : 8 + CJ, :] = c[g, i] * o2

    @pl.loop(0, CI)
    def _(i):
        rows = pl.ds(i * CJ, CJ)
        o = ocol[rows, :]
        if last:
            s4 = near[rows, :]
        else:
            s4 = (
                opad[i + 2, 8 : 8 + CJ, :]
                + opad[i, 8 : 8 + CJ, :]
                + opad[i + 1, 9 : 9 + CJ, :]
                + opad[i + 1, 7 : 7 + CJ, :]
            )
            near[rows, :] = s4
        acc = jnp.zeros((CJ, 128), F32)
        for z in range(2):
            lanes = slice(z * 128, (z + 1) * 128)
            gr = []
            for g in range(G):
                mid = pad[g, i + 1, 8 : 8 + CJ, lanes]
                around = (
                    pad[g, i + 2, 8 : 8 + CJ, lanes]
                    + pad[g, i, 8 : 8 + CJ, lanes]
                    + pad[g, i + 1, 9 : 9 + CJ, lanes]
                    + pad[g, i + 1, 7 : 7 + CJ, lanes]
                )
                m = mid + spr[:, lanes] * (o * around - s4 * mid)
                m_scr[g, rows, lanes] = m
                r = H * m * st[g, rows, lanes].astype(F32)
                acc = acc + sel[g : g + 1, lanes] * r
                gr.append(r)
            for g in range(G):
                tot = mix[g, 0] * gr[0]
                for k in range(1, G):
                    tot = tot + mix[g, k] * gr[k]
                grm[g, rows, lanes] = (-tot).astype(BF16)
        y[rows, :] = (H * o * catch[rows, t * 128 : (t + 1) * 128]) * gs[rows, :] - acc

    for g in range(G):
        t_scr[g] = nt(grm[g], ker[g])

    @pl.loop(0, CI)
    def _(i):
        rows = pl.ds(i * CJ, CJ)
        q = H * ocol[rows, :] * ecol[rows, :] * catch[rows, t * 128 : (t + 1) * 128]
        for g in range(G):
            for z in range(2):
                lanes = slice(z * 128, (z + 1) * 128)
                s = st[g, rows, lanes].astype(F32)
                m = m_scr[g, rows, lanes]
                ge = t_scr[g, rows, lanes]
                fd = feed[g, rows, lanes]
                inv = 1.0 - fd
                gf = assim[g] * (H * m * s) + ge * s
                genc[g, rows, lanes] = (gf * inv * inv).astype(BF16)
                gw = sel[g : g + 1, lanes] * wt[:, lanes]
                c_out[g, i, :, lanes] = m * gain[g, rows, lanes] + ge * fd + q * gw

    for g in range(G):
        t_scr[g] = nn(genc[g], ker[g])

    @pl.loop(0, CI)
    def _(i):
        rows = pl.ds(i * CJ, CJ)
        for z in range(2):
            lanes = slice(z * 128, (z + 1) * 128)
            gp = [t_scr[g, rows, lanes] for g in range(G)]
            for k in range(G):
                tot = mix[0, k] * gp[0]
                for g in range(1, G):
                    tot = tot + mix[g, k] * gp[g]
                c_out[k, i, :, lanes] = c_out[k, i, :, lanes] + tot

    part = jnp.sum(tn(y[...], zone[...], precision=HI), axis=0, keepdims=True)
    if not last:
        eff[...] = jnp.broadcast_to(part, (8, 128))

        def lon_rims(hi, lo):
            for g in range(G):
                hi[g] = c_out[g, CI - 1] * two(ocol[N - CJ : N, :])
                lo[g] = c_out[g, 0] * two(ocol[0:CJ, :])

        def lat_rims(hi, lo):
            for g in range(G):
                for i in range(CI):
                    hi[g, i : i + 1, :] = c_out[g, i, CJ - 1 : CJ, :] * two(
                        ocol[i * CJ + CJ - 1 : i * CJ + CJ, :]
                    )
                    lo[g, i : i + 1, :] = c_out[g, i, 0:1, :] * two(ocol[i * CJ : i * CJ + 1, :])

        pl.when(par_i == 0)(lambda: lon_rims(ola, olb))
        pl.when(par_i == 1)(lambda: lon_rims(olb, ola))
        pl.when(par_j == 0)(lambda: lat_rims(ota, otb))
        pl.when(par_j == 1)(lambda: lat_rims(otb, ota))
        for g in range(G):
            kp[g] = tn(eaten[g], grm[g]) + tn(genc[g], prey[g])
    else:
        both = eff_in[...] + part
        for dst, half in ((send, 1 - par_i), (keep, par_i)):
            dst[2 * Z :, :] = two(both)
            for s in range(2):
                g = 2 * half + s
                dst[s * Z : (s + 1) * Z, :] = kp_in[g] + tn(eaten[g], grm[g]) + tn(genc[g], prey[g])


CH = 17


def merge_body(keep, got, out):
    eff = keep[2 * Z : 2 * Z + 1, :128] + got[2 * Z : 2 * Z + 1, :128]
    for p in range(NCHIP):
        rows = slice(p * 8, p * 8 + 8)
        tot = keep[rows, :] + got[rows, :]
        out[p * CH : p * CH + 8, :] = tot[:, :128]
        out[p * CH + 8 : p * CH + 16, :] = tot[:, 128:]
        out[p * CH + 16 : p * CH + 17, :] = eff


def sum_body(parts, out, eff):
    tot = [None, None, None]
    for p in range(NCHIP):
        new = (
            parts[p * CH : p * CH + 8, :],
            parts[p * CH + 8 : p * CH + 16, :],
            parts[p * CH + 16 : p * CH + 17, :],
        )
        tot = [n if o is None else o + n for o, n in zip(tot, new)]
    both = jnp.concatenate(tot[:2], axis=1)
    eff[...] = tot[2]
    for p in range(NCHIP):
        out[p] = both


def join_body(own, got, out):
    core = lax.axis_index("c")
    for s in range(2):
        out[2 * core + s] = own[s * Z : (s + 1) * Z, :]
        out[2 * (1 - core) + s] = got[s * Z : (s + 1) * Z, :]


def exchange(la, lb, ta, tb):
    return (
        lax.ppermute(la, LON, LON_A),
        lax.ppermute(lb, LON, LON_B),
        lax.ppermute(ta, LAT, LAT_A),
        lax.ppermute(tb, LAT, LAT_B),
    )


def body(
    final_cotangent,
    saved_start,
    saved_middle,
    residuals,
    row_cells,
    row_count,
    ocean_mask,
    cell_eez,
    effort,
    kernel,
    mix,
    assim,
    mortality,
    select,
    weight,
    spread,
):
    devices = 128
    wt, spr = weight.reshape(1, Z), spread.reshape(1, Z)
    rims = [sds((G + 1, CJ, Z))] * 2 + [sds((G + 1, CI, Z))] * 2
    *rim, pay = call(
        prep_body, rims + [sds((devices, 128))], [vm()] * 5, flops=2**27, nbytes=3 * MIB
    )(final_cotangent, ocean_mask, row_cells, row_count.reshape(1, -1), residuals)
    rim = exchange(*rim)
    pay = lax.all_to_all(pay, ALL, 0, 0, tiled=True)

    ocol, ecol, zone = call(cells_body, [sds((N, 128))] * 3, [vm()] * 3, nbytes=MIB)(
        ocean_mask, cell_eez, effort.reshape(1, EEZS)
    )
    fwd = call(
        fwd_body,
        [sds((G, N, Z), BF16)] * 2 + [sds((G, N, Z))] * 2 + [sds((N, 128))],
        [sm(), sm()] + [vm()] * 6,
        [pltpu.VMEM((G, N, Z), F32)],
        flops=2**29,
        nbytes=8 * MIB,
    )
    states, parts = [], []
    for saved in (saved_start, saved_middle):
        st = saved.reshape(G, N, Z)
        states.append(st)
        parts.append(fwd(mix, assim, st, kernel, mortality, select, wt, ecol))
    catch = call(
        catch_body,
        sds((N, 256)),
        [vm()],
        [
            pltpu.VMEM((N, SLOTS * 128), BF16),
            pltpu.VMEM((SLOTS * 128, 256), BF16),
            pltpu.VMEM((SLOTS * 128, 256), BF16),
        ],
        flops=2**29,
        nbytes=MIB,
    )(pay)

    big = [
        pltpu.VMEM((G, CI + 2, CJ + 16, Z), F32),
        pltpu.VMEM((G, N, Z), F32),
        pltpu.VMEM((G, N, Z), F32),
        pltpu.VMEM((G, N, Z), BF16),
        pltpu.VMEM((G, N, Z), BF16),
        pltpu.VMEM((N, 128), F32),
    ]

    def operands(t, cot, rim):
        prey, eaten, feed, gain, gs = parts[t]
        return (mix, assim, cot, *rim, ocol, ecol, catch, gs, zone, states[t], prey, eaten, feed, gain) + (
            kernel,
            select,
            wt,
            spr,
        )

    cot, kp, eff, near, *rim = call(
        functools.partial(adj_body, False, 1),
        [sds((G, CI, CJ, Z)), sds((G, Z, Z)), sds((8, 128)), sds((N, 128))]
        + [sds((G, CJ, Z))] * 2
        + [sds((G, CI, Z))] * 2,
        [sm(), sm()] + [vm()] * 19,
        [pltpu.VMEM((CI + 2, CJ + 16, 128), F32)] + big,
        flops=2**30,
        nbytes=16 * MIB,
    )(*operands(1, final_cotangent, rim))
    rim = exchange(*rim)
    cot, keep, send = call(
        functools.partial(adj_body, True, 0),
        [sds((G, CI, CJ, Z)), sds((2 * Z + 8, Z)), sds((2 * Z + 8, Z))],
        [sm(), sm()] + [vm()] * 22,
        big,
        flops=2**30,
        nbytes=16 * MIB,
    )(*operands(0, cot, rim), near, kp, eff)

    got = lax.ppermute(send, "c", CORE)
    chunks = call(merge_body, sds((NCHIP * CH, 128)), [vm()] * 2, nbytes=2 * MIB)(keep, got)
    chunks = lax.all_to_all(chunks, CHIPS, 0, 0, tiled=True)
    own, eff = call(sum_body, [sds((NCHIP, 8, Z)), sds((1, 128))], [vm()], nbytes=MIB)(chunks)
    own = lax.all_to_all(own, CHIPS, 0, 0, tiled=True).reshape(2 * Z, Z)
    got = lax.ppermute(own, "c", CORE)
    total = call(join_body, sds((G, Z, Z)), [vm()] * 2, nbytes=2 * MIB)(own, got)
    return cot, total, eff[0, :EEZS]


def solution(mesh):
    fine = Mesh(mesh.devices.reshape(2, 4, 2, 4, 2), ("zl", "x", "c", "y", "zh"))
    field = P(None, LON, LAT, None)
    placed = (
        field,
        field,
        field,
        P(None, ALL),
        P(ALL, None),
        P(ALL),
        P(LON, LAT),
        P(LON, LAT),
    ) + (P(),) * 8
    return jax.shard_map(
        body,
        mesh=fine,
        in_specs=placed,
        out_specs=(field, P(), P()),
        check_vma=False,
    )
```

time: 989 us -> 136 us (0.14)
  waiting for transfers between devices: 796 us -> 2.14 us
  Pallas kernels: 0 us -> 54.3 us
  other arithmetic: 38.4 us -> 0 us
  blocking collectives: 69.3 us -> 39.3 us
  local copies, waits for them, and re-layouts: 25.3 us -> 8.19 us
  between operations: 15.2 us -> 0.78 us
  matrix products: 12.5 us -> 0 us
    reduce_scatter x1 -> x0, waiting for transfers between devices: 711 us -> none  [body(): lax.psum_scatter(field_all, ('lon', 'lat'), scatter_dimension=1, tiled=True)]
    psum x1 -> x0, waiting for transfers between devices: 74.3 us -> none  [body(): lax.psum((kernel_part, effort_part), ('lon', 'lat'))]
    psum x1 -> x0, blocking collectives: 69.3 us -> none  [body(): lax.psum((kernel_part, effort_part), ('lon', 'lat'))]
    pallas_call x0 -> x10, Pallas kernels: none -> 54.3 us  [the longest x2 16.2 us: body(): parts.append(fwd(mix, assim, st, kernel, mortality, select, wt, ecol))]
    all_to_all x0 -> x2, blocking collectives: none -> 39.3 us  [the longest x1 22.9 us: body(): chunks = lax.all_to_all(chunks, CHIPS, 0, 0, tiled=True)]
    scatter-add x1 -> x0, other arithmetic: 15.4 us -> none  [body(): field_all = jnp.zeros((2, devices_all * cells_dev), jnp.float32).at[:, po...]
    dot_general x12 -> x0, matrix products: 12.5 us -> none  [the longest x2 3.42 us: local_adjoint(): jnp.einsum('gxyw,gxyz->gwz', eaten, grad_removal, preferred_element_type=...]
    add x5 -> x0, other arithmetic: 11.1 us -> none  [the longest x2 10.4 us: local_adjoint(): grad_state + step_length * ocean * effort_cell * catch_gain * catch_cot]
  transfers between devices with their start and end apart: 14 -> 11, of which waited for: 4 -> 2; matrix products, arithmetic and copies ran while one was open for 4% -> 1% of each run, Pallas kernels for 0% -> 15%
where the time goes in v1:
time: 136 us
  Pallas kernels  54.3 us (40%)
  blocking collectives  39.3 us (29%)
  starting transfers between devices  30.8 us (23%)
  local copies, waits for them, and re-layouts  8.19 us (6%)
  waiting for transfers between devices  2.14 us (2%)
    all_to_all x1, blocking collectives, body(): chunks = lax.all_to_all(chunks, CHIPS, 0, 0, tiled=True)  22.9 us
    all_to_all x1, blocking collectives, body(): own = lax.all_to_all(own, CHIPS, 0, 0, tiled=True).reshape(2 * Z, Z)  16.4 us
    pallas_call x2, Pallas kernels, body(): parts.append(fwd(mix, assim, st, kernel, mortality, select, wt, ecol))  16.2 us
    pallas_call x1, Pallas kernels, body(): call(functools.partial(adj_body, False, 1), [sds((G, CI, CJ, Z)), sds((G,...  12.1 us
    pallas_call x1, Pallas kernels, body(): call(functools.partial(adj_body, True, 0), [sds((G, CI, CJ, Z)), sds((2 *...  11.9 us
    all_to_all x1, starting transfers between devices, body(): pay = lax.all_to_all(pay, ALL, 0, 0, tiled=True)  10.2 us
    ppermute x2, starting transfers between devices, exchange(): lax.ppermute(ta, LAT, LAT_A)  8.82 us
    unnamed x25, local copies, waits for them, and re-layouts  5.06 us
  transfers between devices with their start and end apart: 11, of which 2 were waited for; matrix products, arithmetic and copies ran while one was open for 1% of the time, Pallas kernels for 15%

profile of v1, /device:TPU:1, one launch (start us, length us, event | category | flops | bytes accessed | tf_op | source)
XLA Modules:
  0.0 135.5 jit_solution(5641167955512268246)
XLA Ops:
  0.6 1.4 %copy.21.cells = s32[32,16]{1,0:T(8,128)} copy(s32[32,16]{0,1:T(8,128)} %param.20) | data formatting | bytes 4096 | tf_op args[4]
  2.0 3.2 %shard_map.175 = (f32[5,32,256]{2,1,0:T(8,128)}, f32[5,32,256]{2,1,0:T(8,128)}, f32[5,16,256]{2,1,0:T(8,128)}, f32[5,16,256]{2,1,0:T(8,128)}, f32[128,128]{1,0:T(8,128)}) custom-call(f32[4,16,32,256]{3,2,1,0:T(8,128)} %refs_2_.1, s32[16,32]{1,0:T(8,128)} %ocean.3, s32[32,16]{1,0:T(8,128)} %copy.21.cells, s32[1,32]{1,0:T(1,128)} %bitcast.27, f32[2,32]{1,0:T(2,128)} %resid.1), custom_call_target="tpu_custom_call" | custom-call | flops 134217728 | bytes 3145728 | tf_op jit(solution)/shard_map/pallas_call | solution.py:444
  5.2 1.4 %collective-permute-start = (f32[5,32,256]{2,1,0:T(8,128)}, f32[5,32,256]{2,1,0:T(8,128)S(1)}, u32[]{:S(2)}, u32[]{:S(2)}) collective-permute-start(f32[5,32,256]{2,1,0:T(8,128)} %get-tuple-element.34), channel_id=1, source_target_pairs={{0,8},{8,0},{16,24},{24,16},{32,40},{40,32},{48,56},{56,48},{64,72... | collective-permute-start | bytes 491528 | tf_op jit(solution)/shard_map/ppermute | solution.py:416
  6.6 1.2 collective-permute-start.1
  7.8 10.2 %all-to-all-start = ((f32[128,1,128]{2,1,0:T(1,128)}), f32[128,1,128]{2,1,0:T(1,128)S(1)}, u32[]{:S(2)}, u32[]{:S(2)}) async-start(f32[128,1,128]{2,1,0:T(1,128)} %bitcast.19), calls=%async_computation | async-start | bytes 131072 | tf_op jit(solution)/shard_map/all_to_all | solution.py:448
  18.0 3.4 %collective-permute-start.2 = (f32[5,16,256]{2,1,0:T(8,128)}, f32[5,16,256]{2,1,0:T(8,128)S(1)}, u32[]{:S(2)}, u32[]{:S(2)}) collective-permute-start(f32[5,16,256]{2,1,0:T(8,128)} %get-tuple-element.36), channel_id=1, source_target_pairs={{0,1},{1,0},{2,3},{3,2},{4,5},{5,4},{6,7},{7,6},{8,9},{9,8},{10,11... | collective-permute-start | bytes 245768 | tf_op jit(solution)/shard_map/ppermute | solution.py:418
  22.0 2.1 %shard_map.176 = (f32[512,128]{1,0:T(8,128)}, f32[512,128]{1,0:T(8,128)}, f32[512,128]{1,0:T(8,128)}) custom-call(s32[16,32]{1,0:T(8,128)} %ocean.3, s32[16,32]{1,0:T(8,128)} %eez.1, f32[1,64]{1,0:T(1,128)} %bitcast.28), custom_call_target="tpu_custom_call" | custom-call | bytes 1048576 | tf_op jit(solution)/shard_map/pallas_call | solution.py:450
  24.2 8.1 %shard_map.178 = (bf16[4,512,256]{2,1,0:T(8,128)(2,1)}, bf16[4,512,256]{2,1,0:T(8,128)(2,1)}, f32[4,512,256]{2,1,0:T(8,128)}, f32[4,512,256]{2,1,0:T(8,128)}, f32[512,128]{1,0:T(8,128)}) custom-call(f32[4,4]{1,0:T(4,128)} %refs_0_.3, f32[4]{0:T(128)} %refs_1_.3, bf16[4,512,256]{2,1,0:T(8,128)(2,1)} %bitcast.15, bf16[4,256,256]{2,1,0:T(8,128)(2,1)} %refs_17_.3, ...), custom_call_target="tpu_custom_call" | custom-call | flops 536870912 | bytes 8388608 | tf_op jit(solution)/shard_map/pallas_call | solution.py:465
  32.9 2.5 %shard_map.177.refs_9_ = f32[512,256]{1,0:T(8,128)} custom-call(f32[128,128]{1,0:T(8,128)} %bitcast.20), custom_call_target="tpu_custom_call" | custom-call | flops 536870912 | bytes 1048576 | tf_op jit(solution)/shard_map/pallas_call | solution.py:466
  36.2 12.1 %shard_map.179 = (f32[4,16,32,256]{3,2,1,0:T(8,128)}, f32[4,256,256]{2,1,0:T(8,128)}, f32[8,128]{1,0:T(8,128)}, f32[512,128]{1,0:T(8,128)}, f32[4,32,256]{2,1,0:...) custom-call(f32[4,4]{1,0:T(4,128)} %refs_0_.3, f32[4]{0:T(128)} %refs_1_.3, ...), custom_call_target="tpu_custom_call" | custom-call | flops 1073741824 | bytes 16777216 | tf_op jit(solution)/shard_map/pallas_call | solution.py:497
  49.0 1.2 collective-permute-start.5
  50.2 5.5 %collective-permute-start.6 = (f32[4,16,256]{2,1,0:T(8,128)}, f32[4,16,256]{2,1,0:T(8,128)S(1)}, u32[]{:S(2)}, u32[]{:S(2)}) collective-permute-start(f32[4,16,256]{2,1,0:T(8,128)} %get-tuple-element.50), channel_id=1, source_target_pairs={{0,1},{1,0},{2,3},{3,2},{4,5},{5,4},{6,7},{7,6},{8,9},{9,8},{10,11... | collective-permute-start | bytes 196616 | tf_op jit(solution)/shard_map/ppermute | solution.py:418
  56.3 8.1 %shard_map.180 = (bf16[4,512,256]{2,1,0:T(8,128)(2,1)}, bf16[4,512,256]{2,1,0:T(8,128)(2,1)}, f32[4,512,256]{2,1,0:T(8,128)}, f32[4,512,256]{2,1,0:T(8,128)}, f32[512,128]{1,0:T(8,128)}) custom-call(f32[4,4]{1,0:T(4,128)} %refs_0_.3, f32[4]{0:T(128)} %refs_1_.3, bf16[4,512,256]{2,1,0:T(8,128)(2,1)} %bitcast.17, bf16[4,256,256]{2,1,0:T(8,128)(2,1)} %refs_17_.3, ...), custom_call_target="tpu_custom_call" | custom-call | flops 536870912 | bytes 8388608 | tf_op jit(solution)/shard_map/pallas_call | solution.py:465
  65.2 11.9 %shard_map.181 = (f32[4,16,32,256]{3,2,1,0:T(8,128)}, f32[520,256]{1,0:T(8,128)}, f32[520,256]{1,0:T(8,128)}) custom-call(f32[4,4]{1,0:T(4,128)} %refs_0_.3, f32[4]{0:T(128)} %refs_1_.3, f32[4,16,32,256]{3,2,1,0:T(8,128)} %get-tuple-element.47.refs_2_, f32[4,32,256]{2,1,0:T(8,128)} %copy-done.5, f32[4,32,256]{2,1,0:T(8,128)} %copy-done.6, ...), custom_call_target="tpu_custom_call" | custom-call | flops 1073741824 | bytes 16777216 | tf_op jit(solution)/shard_map/pallas_call | solution.py:508
  77.0 2.9 %collective-permute-start.8 = (f32[520,256]{1,0:T(8,128)}, f32[520,256]{1,0:T(8,128)S(1)}, u32[]{:S(2)}, u32[]{:S(2)}) collective-permute-start(f32[520,256]{1,0:T(8,128)} %get-tuple-element.62), channel_id=1, source_target_pairs={{0,8},{8,0},{1,9},{9,1},{2,10},{10,2},{3,11},{11,3},{4,12},{12,4},... | collective-permute-start | bytes 1597448 | tf_op jit(solution)/shard_map/ppermute | solution.py:517
  79.9 1.8 %collective-permute-done.8.got = f32[520,256]{1,0:T(8,128)S(1)} collective-permute-done((f32[520,256]{1,0:T(8,128)}, f32[520,256]{1,0:T(8,128)S(1)}, u32[]{:S(2)}, u32[]{:S(2)}) %collective-permute-start.8) | collective-permute-done | bytes 532512 | tf_op jit(solution)/shard_map/ppermute | solution.py:517
  82.5 2.1 %shard_map.182 = f32[1088,128]{1,0:T(8,128)} custom-call(f32[520,256]{1,0:T(8,128)} %get-tuple-element.61.keep, f32[520,256]{1,0:T(8,128)} %copy-done.1), custom_call_target="tpu_custom_call" | custom-call | bytes 2097152 | tf_op jit(solution)/shard_map/pallas_call | solution.py:518
  84.6 1.1 all_to_all.20
  85.7 22.9 %all_to_all.27 = f32[64,17,128]{2,1,0:T(8,128)S(1)} all-to-all(f32[64,17,128]{2,1,0:T(8,128)S(1)} %all_to_all.20), channel_id=1, replica_groups=mesh['zl'=2,'x'=4,'c'=2,'y'=4,'zh'=2] {'zl','x','y','zh'}, dimensions={0} | all-to-all | bytes 1114112 | tf_op jit(solution)/shard_map/all_to_all | solution.py:519
  109.5 2.0 %shard_map.183 = (f32[64,8,256]{2,1,0:T(8,128)}, f32[1,128]{1,0:T(1,128)}) custom-call(f32[1088,128]{1,0:T(8,128)} %all_to_all.22.parts), custom_call_target="tpu_custom_call" | custom-call | bytes 1048576 | tf_op jit(solution)/shard_map/pallas_call | solution.py:520
  111.5 16.4 %all_to_all.28 = f32[64,8,256]{2,1,0:T(8,128)S(1)} all-to-all(f32[64,8,256]{2,1,0:T(8,128)} %get-tuple-element.63), channel_id=1, replica_groups=mesh['zl'=2,'x'=4,'c'=2,'y'=4,'zh'=2] {'zl','x','y','zh'}, dimensions={0} | all-to-all | bytes 1048576 | tf_op jit(solution)/shard_map/all_to_all | solution.py:521
  127.9 3.1 %collective-permute-start.9 = (f32[512,256]{1,0:T(8,128)S(1)}, f32[512,256]{1,0:T(8,128)S(1)}, u32[]{:S(2)}, u32[]{:S(2)}) collective-permute-start(f32[512,256]{1,0:T(8,128)S(1)} %bitcast.13), channel_id=1, source_target_pairs={{0,8},{8,0},{1,9},{9,1},{2,10},{10,2},{3,11},{11,3},{4,12},{12,4},... | collective-permute-start | bytes 1572872 | tf_op jit(solution)/shard_map/ppermute | solution.py:522
  130.9 1.2 slice_bitcast_fusion
  133.3 2.2 %shard_map.184 = f32[4,256,256]{2,1,0:T(8,128)} custom-call(f32[512,256]{1,0:T(8,128)} %bitcast.14, f32[512,256]{1,0:T(8,128)} %copy-done.2), custom_call_target="tpu_custom_call" | custom-call | bytes 2097152 | tf_op jit(solution)/shard_map/pallas_call | solution.py:523
  (38 shorter events, 6.9 us)
Async XLA Ops:
  5.2 30.2 %collective-permute-start = (f32[5,32,256]{2,1,0:T(8,128)}, f32[5,32,256]{2,1,0:T(8,128)S(1)}, u32[]{:S(2)}, u32[]{:S(2)}) collective-permute-start(f32[5,32,256]{2,1,0:T(8,128)} %get-tuple-element.34), channel_id=1, source_target_pairs={{0,8},{8,0},{16,24},{24,16},{32,40},{40,32},{48,56},{56,48},{64,72... | collective-permute-start | bytes 491528 | tf_op jit(solution)/shard_map/ppermute | solution.py:416
  6.6 28.9 %collective-permute-start.1 = (f32[5,32,256]{2,1,0:T(8,128)}, f32[5,32,256]{2,1,0:T(8,128)S(1)}, u32[]{:S(2)}, u32[]{:S(2)}) collective-permute-start(f32[5,32,256]{2,1,0:T(8,128)} %get-tuple-element.35), channel_id=1, source_target_pairs={{0,120},{8,16},{16,8},{24,32},{32,24},{40,48},{48,40},{56,64},{64,... | collective-permute-start | bytes 491528 | tf_op jit(solution)/shard_map/ppermute | solution.py:417
  7.8 24.5 %all-to-all-start = ((f32[128,1,128]{2,1,0:T(1,128)}), f32[128,1,128]{2,1,0:T(1,128)S(1)}, u32[]{:S(2)}, u32[]{:S(2)}) async-start(f32[128,1,128]{2,1,0:T(1,128)} %bitcast.19), calls=%async_computation | async-start | bytes 131072 | tf_op jit(solution)/shard_map/all_to_all | solution.py:448
  18.0 17.4 %collective-permute-start.2 = (f32[5,16,256]{2,1,0:T(8,128)}, f32[5,16,256]{2,1,0:T(8,128)S(1)}, u32[]{:S(2)}, u32[]{:S(2)}) collective-permute-start(f32[5,16,256]{2,1,0:T(8,128)} %get-tuple-element.36), channel_id=1, source_target_pairs={{0,1},{1,0},{2,3},{3,2},{4,5},{5,4},{6,7},{7,6},{8,9},{9,8},{10,11... | collective-permute-start | bytes 245768 | tf_op jit(solution)/shard_map/ppermute | solution.py:418
  21.4 14.1 %collective-permute-start.3 = (f32[5,16,256]{2,1,0:T(8,128)}, f32[5,16,256]{2,1,0:T(8,128)S(1)}, u32[]{:S(2)}, u32[]{:S(2)}) collective-permute-start(f32[5,16,256]{2,1,0:T(8,128)} %get-tuple-element.37), channel_id=1, source_target_pairs={{1,2},{2,1},{3,4},{4,3},{5,6},{6,5},{9,10},{10,9},{11,12},{12,11},... | collective-permute-start | bytes 245768 | tf_op jit(solution)/shard_map/ppermute | solution.py:419
  32.2 0.6 copy-start.11
  35.4 0.6 copy-start.7
  35.4 0.7 copy-start.8
  35.4 0.7 copy-start.3
  35.5 0.7 copy-start.4
  48.3 16.1 %collective-permute-start.4 = (f32[4,32,256]{2,1,0:T(8,128)}, f32[4,32,256]{2,1,0:T(8,128)S(1)}, u32[]{:S(2)}, u32[]{:S(2)}) collective-permute-start(f32[4,32,256]{2,1,0:T(8,128)} %get-tuple-element.48), channel_id=1, source_target_pairs={{0,8},{8,0},{16,24},{24,16},{32,40},{40,32},{48,56},{56,48},{64,72... | collective-permute-start | bytes 393224 | tf_op jit(solution)/shard_map/ppermute | solution.py:416
  49.0 15.4 %collective-permute-start.5 = (f32[4,32,256]{2,1,0:T(8,128)}, f32[4,32,256]{2,1,0:T(8,128)S(1)}, u32[]{:S(2)}, u32[]{:S(2)}) collective-permute-start(f32[4,32,256]{2,1,0:T(8,128)} %get-tuple-element.49), channel_id=1, source_target_pairs={{0,120},{8,16},{16,8},{24,32},{32,24},{40,48},{48,40},{56,64},{64,... | collective-permute-start | bytes 393224 | tf_op jit(solution)/shard_map/ppermute | solution.py:417
  50.2 14.2 %collective-permute-start.6 = (f32[4,16,256]{2,1,0:T(8,128)}, f32[4,16,256]{2,1,0:T(8,128)S(1)}, u32[]{:S(2)}, u32[]{:S(2)}) collective-permute-start(f32[4,16,256]{2,1,0:T(8,128)} %get-tuple-element.50), channel_id=1, source_target_pairs={{0,1},{1,0},{2,3},{3,2},{4,5},{5,4},{6,7},{7,6},{8,9},{9,8},{10,11... | collective-permute-start | bytes 196616 | tf_op jit(solution)/shard_map/ppermute | solution.py:418
  55.7 8.8 %collective-permute-start.7 = (f32[4,16,256]{2,1,0:T(8,128)}, f32[4,16,256]{2,1,0:T(8,128)S(1)}, u32[]{:S(2)}, u32[]{:S(2)}) collective-permute-start(f32[4,16,256]{2,1,0:T(8,128)} %get-tuple-element.51), channel_id=1, source_target_pairs={{1,2},{2,1},{3,4},{4,3},{5,6},{6,5},{9,10},{10,9},{11,12},{12,11},... | collective-permute-start | bytes 196616 | tf_op jit(solution)/shard_map/ppermute | solution.py:419
  64.4 0.6 copy-start.9
  64.4 0.6 copy-start.10
  64.5 0.7 copy-start.5
  64.5 0.7 copy-start.6
  77.0 4.7 %collective-permute-start.8 = (f32[520,256]{1,0:T(8,128)}, f32[520,256]{1,0:T(8,128)S(1)}, u32[]{:S(2)}, u32[]{:S(2)}) collective-permute-start(f32[520,256]{1,0:T(8,128)} %get-tuple-element.62), channel_id=1, source_target_pairs={{0,8},{8,0},{1,9},{9,1},{2,10},{10,2},{3,11},{11,3},{4,12},{12,4},... | collective-permute-start | bytes 1597448 | tf_op jit(solution)/shard_map/ppermute | solution.py:517
  81.7 0.8 copy-start.1
  127.9 4.6 %copy-start = (f32[64,8,256]{2,1,0:T(8,128)}, f32[64,8,256]{2,1,0:T(8,128)S(1)}, u32[]{:S(2)}) copy-start(f32[64,8,256]{2,1,0:T(8,128)S(1)} %all_to_all.28) | copy-start | bytes 1572868
  127.9 4.6 %collective-permute-start.9 = (f32[512,256]{1,0:T(8,128)S(1)}, f32[512,256]{1,0:T(8,128)S(1)}, u32[]{:S(2)}, u32[]{:S(2)}) collective-permute-start(f32[512,256]{1,0:T(8,128)S(1)} %bitcast.13), channel_id=1, source_target_pairs={{0,8},{8,0},{1,9},{9,1},{2,10},{10,2},{3,11},{11,3},{4,12},{12,4},... | collective-permute-start | bytes 1572872 | tf_op jit(solution)/shard_map/ppermute | solution.py:522
  132.5 0.8 copy-start.2

commit v2 on v1

v2 whole, which is shorter than its diff:
```python
import functools

import jax
import jax.numpy as jnp
from jax import lax
from jax.experimental import pallas as pl
from jax.experimental.pallas import tpu as pltpu
from jax.sharding import Mesh, PartitionSpec as P

G, Z = 4, 256
CI, CJ = 16, 32
N = CI * CJ
EEZS = 64
H = 0.5
SLOTS = 8
F32, BF16 = jnp.float32, jnp.bfloat16
LON, LAT = ("zl", "x", "c"), ("y", "zh")
ALL = LON + LAT
CHIPS = ("zl", "x", "y", "zh")
NCHIP = 64
MIB = 1024 * 1024
HI = lax.Precision.HIGHEST

LON_A = [(i, i ^ 1) for i in range(16)]
LON_B = [(i, (i + 1) % 16 if i % 2 else (i - 1) % 16) for i in range(16)]
LAT_A = [(i, i ^ 1) for i in range(8)]
LAT_B = [(i, i + 1 if i % 2 else i - 1) for i in range(1, 7)]
CORE = [(0, 1), (1, 0)]


def sds(shape, dtype=F32):
    return jax.ShapeDtypeStruct(shape, dtype)


def vmem(shape, dtype=F32):
    return pltpu.VMEM(shape, dtype)


def vm():
    return pl.BlockSpec(memory_space=pltpu.VMEM)


def sm():
    return pl.BlockSpec(memory_space=pltpu.SMEM)


def call(body, outs, ins, scratch=(), flops=0, nbytes=0, vmem=6, place=True, far=(), out_far=0):
    many = isinstance(outs, list)
    spots = [pl.BlockSpec(memory_space=pl.ANY) if n < out_far else vm() for n in range(len(outs) if many else 1)]
    run = pl.pallas_call(
        body,
        out_shape=outs,
        in_specs=ins,
        out_specs=spots if many else vm(),
        scratch_shapes=list(scratch),
        compiler_params=pltpu.CompilerParams(vmem_limit_bytes=vmem * MIB),
        cost_estimate=pl.CostEstimate(flops=flops, bytes_accessed=nbytes, transcendentals=0),
    )

    def go(*args):
        return run(
            *[
                in_hbm(a) if not place or n in far else near_core(a) if a.size >= 8192 else a
                for n, a in enumerate(args)
            ]
        )

    return go


def near_core(x):
    return pltpu.with_memory_space_constraint(x, pltpu.VMEM)


def in_hbm(x):
    return pltpu.with_memory_space_constraint(x, pltpu.HBM)


def nt(a, b, **kw):
    return lax.dot_general(a, b, (((1,), (1,)), ((), ())), preferred_element_type=F32, **kw)


def nn(a, b, **kw):
    return lax.dot_general(a, b, (((1,), (0,)), ((), ())), preferred_element_type=F32, **kw)


def tn(a, b, **kw):
    return lax.dot_general(a, b, (((0,), (0,)), ((), ())), preferred_element_type=F32, **kw)


def split(x):
    hi = x.astype(BF16).astype(F32)
    return hi, x - hi


def two(x):
    return jnp.concatenate([x, x], axis=1)


def column(row, n, width):
    eye = lax.broadcasted_iota(jnp.int32, (n, n), 0) == lax.broadcasted_iota(jnp.int32, (n, n), 1)
    col = jnp.sum(jnp.where(eye, jnp.broadcast_to(row, (n, n)), 0.0), axis=1, keepdims=True)
    return jnp.broadcast_to(col, (n, width))


def prep_body(c, ocean, cells, count, resid, la, lb, ta, tb, pay, rim_i, rim_j, sem):
    par_i, par_j = lax.axis_index("c"), lax.axis_index("zh")
    copies = [
        pltpu.make_async_copy(c.at[:, CI - 1], rim_i.at[0], sem.at[0]),
        pltpu.make_async_copy(c.at[:, 0], rim_i.at[1], sem.at[1]),
        pltpu.make_async_copy(c.at[:, :, CJ - 8 : CJ, :], rim_j.at[0], sem.at[2]),
        pltpu.make_async_copy(c.at[:, :, 0:8, :], rim_j.at[1], sem.at[3]),
    ]
    for copy in copies:
        copy.start()

    ents, rows = cells.shape
    ne = rows * ents
    devices = pay.shape[0]
    tile_e = lax.broadcasted_iota(jnp.int32, (ents, ne), 1) // rows == lax.broadcasted_iota(
        jnp.int32, (ents, ne), 0
    )
    tile_r = lax.broadcasted_iota(jnp.int32, (rows, ne), 1) % rows == lax.broadcasted_iota(
        jnp.int32, (rows, ne), 0
    )
    tile_rf = tile_r.astype(F32)
    lon_i = (cells[...] // 256).astype(F32)
    lat_i = (cells[...] % 256).astype(F32)

    def flat(x):
        spread_out = nn(x, tile_rf, precision=HI)
        return jnp.sum(jnp.where(tile_e, spread_out, 0.0), axis=0, keepdims=True)

    i_row = flat(lon_i).astype(jnp.int32)
    j_row = flat(lat_i).astype(jnp.int32)
    n_row = nn(count[...].astype(F32), tile_rf, precision=HI)
    r_row = nn(resid[...], tile_rf, precision=HI)
    entry = (lax.broadcasted_iota(jnp.int32, (1, ne), 1) // rows).astype(F32)
    vals = jnp.where(entry < n_row, r_row, 0.0)
    owner = (i_row // CI) * 8 + j_row // CJ
    mine = lax.broadcasted_iota(jnp.int32, (devices, ne), 0) == owner
    mine_b = mine.astype(F32).astype(BF16)
    before = (
        lax.broadcasted_iota(jnp.int32, (ne, ne), 0) < lax.broadcasted_iota(jnp.int32, (ne, ne), 1)
    )
    ahead = nn(mine_b, before.astype(F32).astype(BF16))
    rank = jnp.sum(jnp.where(mine, ahead, 0.0), axis=0, keepdims=True).astype(jnp.int32)
    slot = lax.broadcasted_iota(jnp.int32, (SLOTS, ne), 0) == rank
    h0, l0 = split(vals[0:1])
    h1, l1 = split(vals[1:2])
    a_row = ((i_row % CI) * CJ).astype(F32)
    b_row = (j_row % CJ).astype(F32)

    def rows_of(parts):
        put = [jnp.where(slot, jnp.broadcast_to(p, (SLOTS, ne)), 0.0) for p in parts]
        put.append(jnp.zeros((128 - SLOTS * len(parts), ne), F32))
        return jnp.concatenate(put, axis=0).astype(BF16)

    pay[...] = nt(mine_b, rows_of((h0, h1, a_row))) + nt(mine_b, rows_of((l0, l1, b_row)))

    oc = ocean[...].astype(F32)
    edge_i = (column(oc[CI - 1 : CI, :], CJ, Z), column(oc[0:1, :], CJ, Z))
    edge_j = (
        jnp.broadcast_to(oc[:, CJ - 1 : CJ], (CI, Z)),
        jnp.broadcast_to(oc[:, 0:1], (CI, Z)),
    )
    for copy in copies:
        copy.wait()

    def rims(odd, a, b, value):
        for n, (even_to, odd_to) in enumerate(((a, b), (b, a))):
            for g in range(G + 1):
                v = value(n, g)

                @pl.when(odd == 0)
                def _():
                    even_to[g] = v

                @pl.when(odd == 1)
                def _():
                    odd_to[g] = v

    rims(par_i, la, lb, lambda n, g: edge_i[n] if g == G else rim_i[n, g] * edge_i[n])
    rims(
        par_j,
        ta,
        tb,
        lambda n, g: edge_j[n] if g == G else rim_j[n, g, :, 7 if n == 0 else 0, :] * edge_j[n],
    )


def cells_body(ocean, eez, effort, pay, ker, ocol, ecol, zone, out, flipped, hot, hi, lo):
    for g in range(G):
        flipped[g] = ker[g].T
    oc = ocean[...].astype(F32)
    ez = eez[...].astype(F32)
    lane = lax.broadcasted_iota(jnp.int32, (CJ, 128), 1)
    eff = jnp.concatenate([effort[...], jnp.zeros((1, 128 - EEZS), F32)], axis=1)
    for i in range(CI):
        rows = slice(i * CJ, (i + 1) * CJ)
        ocol[rows] = column(oc[i : i + 1, :], CJ, 128)
        here = (column(ez[i : i + 1, :], CJ, 128).astype(jnp.int32) == lane).astype(F32)
        zone[rows] = here
        ecol[rows] = jnp.broadcast_to(jnp.sum(here * eff, axis=1, keepdims=True), (CJ, 128))

    got = pay[...]
    flip = got.T
    for k in range(SLOTS):
        where = flip[2 * SLOTS + k : 2 * SLOTS + k + 1, :].astype(jnp.int32)
        cell = lax.broadcasted_iota(jnp.int32, (N, 128), 0)
        hot[:, k * 128 : (k + 1) * 128] = (cell == where).astype(F32).astype(BF16)
        both = jnp.concatenate(
            [
                jnp.broadcast_to(got[:, k : k + 1], (128, 128)),
                jnp.broadcast_to(got[:, SLOTS + k : SLOTS + k + 1], (128, 128)),
            ],
            axis=1,
        )
        top, rest = split(both)
        hi[k * 128 : (k + 1) * 128, :] = top.astype(BF16)
        lo[k * 128 : (k + 1) * 128, :] = rest.astype(BF16)
    out[...] = nn(hot[...], hi[...]) + nn(hot[...], lo[...])


R = 128
CHUNKS = N // R


def recip(d):
    r = pltpu.reciprocal(d, approx=True)
    return r * (2.0 - d * r)


def mixed(rows_of, mix, k, turned=False):
    tot = None
    for g in range(G):
        term = (mix[g, k] if turned else mix[k, g]) * rows_of[g]
        tot = term if tot is None else tot + term
    return tot


def gain_of(k, mix, assim, mort, sel, ef, feed, rem):
    tot = (1.0 - H * mort[k : k + 1, :]) - (H * sel[k : k + 1, :]) * ef + (H * assim[k]) * feed
    for g in range(G):
        tot = tot + (-H * mix[g, k]) * rem[g]
    return tot


def fwd_body(full, *refs):
    if full:
        mix, assim, saved, ker, turn, mort, sel, wt, ecol, st, prey, eaten, feed, gs, gain, rem, sem = refs
    else:
        mix, assim, saved, ker, turn, mort, sel, wt, ecol, st, prey, eaten, feed, gs, sem = refs
    copies = []
    for n in range(CHUNKS):
        rows = slice(n * R, (n + 1) * R)
        copies.append(pltpu.make_async_copy(saved.at[:, rows, :], st.at[:, rows, :], sem.at[n]))
        copies[-1].start()
    for n in range(CHUNKS):
        rows = slice(n * R, (n + 1) * R)
        copies[n].wait()
        s = [st[k, rows, :].astype(F32) for k in range(G)]
        part = None
        for k in range(G):
            term = (sel[k : k + 1, :] * wt[...]) * s[k]
            part = term if part is None else part + term
        gs[rows, :] = part[:, :128] + part[:, 128:]
        for g in range(G):
            prey[g, rows, :] = mixed(s, mix, g).astype(BF16)
        for g in range(G):
            enc = nn(prey[g, rows, :], turn[g])
            fd = enc * recip(enc + 1.0)
            feed[g, rows, :] = fd
            eaten[g, rows, :] = (st[g, rows, :].astype(F32) * fd).astype(BF16)
        if full:
            for g in range(G):
                rem[g, rows, :] = nn(eaten[g, rows, :], ker[g])
            parts = [rem[g, rows, :] for g in range(G)]
            ef = two(ecol[rows, :])
            for k in range(G):
                gain[k, rows, :] = gain_of(k, mix, assim, mort, sel, ef, feed[k, rows, :], parts)


def fill(pad, opad, c, la, lb, ta, tb, ocol):
    par_i, par_j = lax.axis_index("c"), lax.axis_index("zh")
    at_a = jnp.where(par_i == 0, CI + 1, 0)
    at_b = CI + 1 - at_a
    row_a = jnp.where(par_j == 0, CJ + 8, 7)
    row_b = CJ + 15 - row_a
    for g in range(G):
        pad[g, at_a, 8 : 8 + CJ, :] = la[g]
        pad[g, at_b, 8 : 8 + CJ, :] = lb[g]
        for i in range(CI):
            pad[g, i + 1, pl.ds(row_a, 1), :] = ta[g, i : i + 1, :]
            pad[g, i + 1, pl.ds(row_b, 1), :] = tb[g, i : i + 1, :]
    if opad is not None:
        opad[at_a, 8 : 8 + CJ, :] = la[G, :, :128]
        opad[at_b, 8 : 8 + CJ, :] = lb[G, :, :128]
        for i in range(CI):
            opad[i + 1, pl.ds(row_a, 1), :] = ta[G, i : i + 1, :128]
            opad[i + 1, pl.ds(row_b, 1), :] = tb[G, i : i + 1, :128]
    for i in range(CI):
        o = ocol[i * CJ : (i + 1) * CJ, :]
        if opad is not None:
            opad[i + 1, 8 : 8 + CJ, :] = o
        for g in range(G):
            pad[g, i + 1, 8 : 8 + CJ, :] = c[g, i] * two(o)


def around(pad, i, lanes):
    return (pad[i + 2, 8 : 8 + CJ, lanes] + pad[i, 8 : 8 + CJ, lanes]) + (
        pad[i + 1, 9 : 9 + CJ, lanes] + pad[i + 1, 7 : 7 + CJ, lanes]
    )


def spread_row(i, t, pad, s4, mix, ocol, catch, gs, st, sel, spr, m_out, grm, y):
    rows = slice(i * CJ, (i + 1) * CJ)
    o = ocol[rows, :]
    acc = None
    for z in range(2):
        lanes = slice(z * 128, (z + 1) * 128)
        ms = []
        for g in range(G):
            mid = pad[g, i + 1, 8 : 8 + CJ, lanes]
            m = mid + spr[:, lanes] * (o * around(pad.at[g], i, lanes) - s4 * mid)
            m_out[g, rows, lanes] = m
            ms.append(m * st[g, rows, lanes].astype(F32))
            term = sel[g : g + 1, lanes] * ms[-1]
            acc = term if acc is None else acc + term
        for g in range(G):
            tot = None
            for k in range(G):
                term = (-H * mix[g, k]) * ms[k]
                tot = term if tot is None else tot + term
            grm[g, rows, lanes] = tot.astype(BF16)
    y[rows, :] = H * ((o * catch[rows, t * 128 : (t + 1) * 128]) * gs[rows, :] - acc)


def enc_grad(g, assim, m, s, ge, fd):
    inv = 1.0 - fd
    return (((H * assim[g]) * (m * s) + ge * s) * (inv * inv)).astype(BF16)


def adj_body(*refs):
    mix, assim, c, la, lb, ta, tb, ocol, ecol, catch, gs, zone, st, feed, gain, ker, turn, sel, wt, spr = refs[:20]
    c_out, grm, genc, eff, near, ola, olb, ota, otb, opad, pad, m_scr, t_scr, y = refs[20:]
    par_i, par_j = lax.axis_index("c"), lax.axis_index("zh")
    fill(pad, opad, c, la, lb, ta, tb, ocol)
    for n in range(CHUNKS):
        rows = slice(n * R, (n + 1) * R)
        for i in range(n * R // CJ, (n + 1) * R // CJ):
            s4 = around(opad, i, slice(None))
            near[i * CJ : (i + 1) * CJ, :] = s4
            spread_row(i, 1, pad, s4, mix, ocol, catch, gs, st, sel, spr, m_scr, grm, y)
        q = two(H * ocol[rows, :] * ecol[rows, :] * catch[rows, 128:])
        for g in range(G):
            ge = nn(grm[g, rows, :], turn[g])
            m, fd = m_scr[g, rows, :], feed[g, rows, :]
            genc[g, rows, :] = enc_grad(g, assim, m, st[g, rows, :].astype(F32), ge, fd)
            m_scr[g, rows, :] = m * gain[g, rows, :] + ge * fd + q * (sel[g : g + 1, :] * wt[...])
        for g in range(G):
            t_scr[g, rows, :] = nn(genc[g, rows, :], ker[g])
        for i in range(n * R // CJ, (n + 1) * R // CJ):
            here = slice(i * CJ, (i + 1) * CJ)
            gp = [t_scr[g, here, :] for g in range(G)]
            for k in range(G):
                c_out[k, i] = m_scr[k, here, :] + mixed(gp, mix, k, True)
    part = jnp.sum(tn(y[...], zone[...], precision=HI), axis=0, keepdims=True)
    eff[...] = jnp.broadcast_to(part, (8, 128))

    def lon_rims(hi, lo):
        for g in range(G):
            hi[g] = c_out[g, CI - 1] * two(ocol[N - CJ : N, :])
            lo[g] = c_out[g, 0] * two(ocol[0:CJ, :])

    def lat_rims(hi, lo):
        for g in range(G):
            for i in range(CI):
                at = i * CJ
                hi[g, i : i + 1, :] = c_out[g, i, CJ - 1 : CJ, :] * two(ocol[at + CJ - 1 : at + CJ, :])
                lo[g, i : i + 1, :] = c_out[g, i, 0:1, :] * two(ocol[at : at + 1, :])

    pl.when(par_i == 0)(lambda: lon_rims(ola, olb))
    pl.when(par_i == 1)(lambda: lon_rims(olb, ola))
    pl.when(par_j == 0)(lambda: lat_rims(ota, otb))
    pl.when(par_j == 1)(lambda: lat_rims(otb, ota))


def part_body(eaten, grm, genc, prey, kp):
    for g in range(G):
        kp[g] = tn(eaten[g], grm[g]) + tn(genc[g], prey[g])


def last_body(*refs):
    mix, assim, c, la, lb, ta, tb, ocol, ecol, catch, gs, zone, st, prey, eaten, feed, turn, sel, spr, near, kp, eff = refs[:22]
    m_hbm, ge_hbm, q_hbm, e_hbm, keep, send, pad, m_scr, ge_scr, grm, genc, y, q_scr, sem = refs[22:]
    core = lax.axis_index("c")
    fill(pad, None, c, la, lb, ta, tb, ocol)
    q_scr[...] = H * ocol[...] * ecol[...] * catch[:, :128]
    copies = [
        pltpu.make_async_copy(q_scr, q_hbm, sem.at[0]),
        pltpu.make_async_copy(ecol, e_hbm, sem.at[1]),
    ]
    for copy in copies:
        copy.start()
    for n in range(CHUNKS):
        rows = slice(n * R, (n + 1) * R)
        for i in range(n * R // CJ, (n + 1) * R // CJ):
            s4 = near[i * CJ : (i + 1) * CJ, :]
            spread_row(i, 0, pad, s4, mix, ocol, catch, gs, st, sel, spr, m_scr, grm, y)
        for g in range(G):
            ge = nn(grm[g, rows, :], turn[g])
            ge_scr[g, rows, :] = ge
            genc[g, rows, :] = enc_grad(
                g, assim, m_scr[g, rows, :], st[g, rows, :].astype(F32), ge, feed[g, rows, :]
            )
        for k, (src, dst) in enumerate(((m_scr, m_hbm), (ge_scr, ge_hbm))):
            copies.append(
                pltpu.make_async_copy(src.at[:, rows, :], dst.at[:, rows, :], sem.at[2 + 2 * n + k])
            )
            copies[-1].start()
    part = jnp.sum(tn(y[...], zone[...], precision=HI), axis=0, keepdims=True)
    both = two(eff[...] + part)
    for dst, half in ((send, 1 - core), (keep, core)):
        dst[2 * Z :, :] = both
        for s in range(2):
            g = 2 * half + s
            dst[s * Z : (s + 1) * Z, :] = kp[g] + tn(eaten[g], grm[g]) + tn(genc[g], prey[g])
    for copy in copies:
        copy.wait()


def rest_body(mix, assim, saved, m_in, ge_in, q_in, ecol, ker, mort, sel, wt, out, feed, rem, turn):
    @pl.when(pl.program_id(0) == 0)
    def _():
        for g in range(G):
            turn[g] = ker[g].T

    s = [saved[k].astype(F32) for k in range(G)]
    for g in range(G):
        enc = nn(mixed(s, mix, g).astype(BF16), turn[g])
        fd = enc * recip(enc + 1.0)
        feed[g] = fd
        rem[g] = nn((s[g] * fd).astype(BF16), ker[g])
    parts = [rem[g] for g in range(G)]
    ef, q = two(ecol[...]), two(q_in[...])
    for k in range(G):
        fd = feed[k]
        gain = gain_of(k, mix, assim, mort, sel, ef, fd, parts)
        out[k] = m_in[k] * gain + ge_in[k] * fd + q * (sel[k : k + 1, :] * wt[...])
    for g in range(G):
        rem[g] = nn(enc_grad(g, assim, m_in[g], saved[g].astype(F32), ge_in[g], feed[g]), ker[g])
    parts = [rem[g] for g in range(G)]
    for k in range(G):
        out[k] = out[k] + mixed(parts, mix, k, True)


CH = 17


def merge_body(keep, got, out):
    eff = keep[2 * Z : 2 * Z + 1, :128] + got[2 * Z : 2 * Z + 1, :128]
    for p in range(NCHIP):
        rows = slice(p * 8, p * 8 + 8)
        tot = keep[rows, :] + got[rows, :]
        out[p * CH : p * CH + 8, :] = tot[:, :128]
        out[p * CH + 8 : p * CH + 16, :] = tot[:, 128:]
        out[p * CH + 16 : p * CH + 17, :] = eff


def sum_body(parts, out, eff):
    tot = [None, None, None]
    for p in range(NCHIP):
        new = (
            parts[p * CH : p * CH + 8, :],
            parts[p * CH + 8 : p * CH + 16, :],
            parts[p * CH + 16 : p * CH + 17, :],
        )
        tot = [n if o is None else o + n for o, n in zip(tot, new)]
    both = jnp.concatenate(tot[:2], axis=1)
    eff[...] = tot[2]
    for p in range(NCHIP):
        out[p] = both


def join_body(own, got, out):
    core = lax.axis_index("c")
    for s in range(2):
        out[2 * core + s] = own[s * Z : (s + 1) * Z, :]
        out[2 * (1 - core) + s] = got[s * Z : (s + 1) * Z, :]


def exchange(la, lb, ta, tb):
    return (
        lax.ppermute(la, LON, LON_A),
        lax.ppermute(lb, LON, LON_B),
        lax.ppermute(ta, LAT, LAT_A),
        lax.ppermute(tb, LAT, LAT_B),
    )


def body(
    final_cotangent,
    saved_start,
    saved_middle,
    residuals,
    row_cells,
    row_count,
    ocean_mask,
    cell_eez,
    effort,
    kernel,
    mix,
    assim,
    mortality,
    select,
    weight,
    spread,
):
    devices = 128
    wt, spr = weight.reshape(1, Z), spread.reshape(1, Z)
    any_ = pl.BlockSpec(memory_space=pl.ANY)
    field = (G, N, Z)
    rims = [vmem((G + 1, CJ, Z))] * 2 + [vmem((G + 1, CI, Z))] * 2
    *rim, pay = call(
        prep_body,
        rims + [vmem((devices, 128))],
        [any_] + [vm()] * 4,
        [
            pltpu.VMEM((2, G, CJ, Z), F32),
            pltpu.VMEM((2, G, CI, 8, Z), F32),
            pltpu.SemaphoreType.DMA((4,)),
        ],
        flops=2**27,
        nbytes=3 * MIB,
        place=False,
    )(final_cotangent, ocean_mask, row_cells.T, row_count.reshape(1, -1), residuals)
    rim = exchange(*rim)
    pay = lax.all_to_all(pay, ALL, 0, 0, tiled=True)

    ocol, ecol, zone, catch, turn = call(
        cells_body,
        [vmem((N, 128))] * 3 + [vmem((N, 256)), vmem((G, Z, Z), BF16)],
        [vm()] * 5,
        [
            pltpu.VMEM((N, SLOTS * 128), BF16),
            pltpu.VMEM((SLOTS * 128, 256), BF16),
            pltpu.VMEM((SLOTS * 128, 256), BF16),
        ],
        flops=2**29,
        nbytes=MIB,
    )(ocean_mask, cell_eez, effort.reshape(1, EEZS), pay, kernel)

    def forward(saved, full):
        return call(
            functools.partial(fwd_body, full),
            [vmem(field, BF16)] * 3 + [vmem(field), vmem((N, 128))] + [vmem(field)] * full,
            [sm(), sm(), any_] + [vm()] * 6,
            [pltpu.VMEM(field, F32)] * full + [pltpu.SemaphoreType.DMA((CHUNKS,))],
            flops=2**29,
            nbytes=8 * MIB,
            vmem=8,
            far=(2,),
        )(mix, assim, saved.reshape(field), kernel, turn, mortality, select, wt, ecol)

    st, prey, eaten, feed, gs, gain = forward(saved_middle, True)
    pads = pltpu.VMEM((G, CI + 2, CJ + 16, Z), F32)
    cot, grm, genc, eff, near, *rim = call(
        adj_body,
        [vmem((G, CI, CJ, Z))]
        + [vmem(field, BF16)] * 2
        + [vmem((8, 128)), vmem((N, 128))]
        + [vmem((G, CJ, Z))] * 2
        + [vmem((G, CI, Z))] * 2,
        [sm(), sm()] + [vm()] * 18,
        [pltpu.VMEM((CI + 2, CJ + 16, 128), F32), pads]
        + [pltpu.VMEM(field, F32)] * 2
        + [pltpu.VMEM((N, 128), F32)],
        flops=2**30,
        nbytes=16 * MIB,
        vmem=16,
    )(
        *(mix, assim, final_cotangent, *rim, ocol, ecol, catch, gs, zone, st, feed, gain),
        *(kernel, turn, select, wt, spr),
    )
    rim = exchange(*rim)
    kp = call(part_body, vmem((G, Z, Z)), [vm()] * 4, flops=2**29, nbytes=5 * MIB)(
        eaten, grm, genc, prey
    )
    st, prey, eaten, feed, gs = forward(saved_start, False)
    m, ge, q, ef, keep, send = call(
        last_body,
        [pltpu.HBM(field, F32)] * 2 + [pltpu.HBM((N, 128), F32)] * 2 + [vmem((2 * Z + 8, Z))] * 2,
        [sm(), sm()] + [vm()] * 20,
        [pads]
        + [pltpu.VMEM(field, F32)] * 2
        + [pltpu.VMEM(field, BF16)] * 2
        + [pltpu.VMEM((N, 128), F32)] * 2
        + [pltpu.SemaphoreType.DMA((2 + 2 * CHUNKS,))],
        flops=2**30,
        nbytes=16 * MIB,
        vmem=16,
        out_far=4,
    )(
        *(mix, assim, cot, *rim, ocol, ecol, catch, gs, zone, st, prey, eaten, feed),
        *(turn, select, spr, near, kp, eff),
    )
    block = pl.BlockSpec((G, R, Z), lambda n: (0, n, 0))
    cells = pl.BlockSpec((R, 128), lambda n: (n, 0))
    whole = pl.BlockSpec((G, Z), lambda n: (0, 0))
    cot = pl.pallas_call(
        rest_body,
        grid=(CHUNKS,),
        out_shape=sds(field),
        in_specs=[sm(), sm(), block, block, block, cells, cells]
        + [pl.BlockSpec((G, Z, Z), lambda n: (0, 0, 0)), whole, whole]
        + [pl.BlockSpec((1, Z), lambda n: (0, 0))],
        out_specs=block,
        scratch_shapes=[pltpu.VMEM((G, R, Z), F32)] * 2 + [pltpu.VMEM((G, Z, Z), BF16)],
        compiler_params=pltpu.CompilerParams(vmem_limit_bytes=16 * MIB),
        cost_estimate=pl.CostEstimate(flops=2**30, bytes_accessed=12 * MIB, transcendentals=0),
    )(mix, assim, *map(in_hbm, (saved_start.reshape(field), m, ge, q, ef, kernel)), mortality, select, wt)
    cot = cot.reshape(G, CI, CJ, Z)

    got = lax.ppermute(send, "c", CORE)
    chunks = call(merge_body, vmem((NCHIP * CH, 128)), [vm()] * 2, nbytes=2 * MIB)(keep, got)
    chunks = lax.all_to_all(chunks.reshape(NCHIP, 1, CH * 128), CHIPS, 0, 0, tiled=True)
    chunks = chunks.reshape(NCHIP * CH, 128)
    own, eff = call(sum_body, [vmem((NCHIP, 8, Z)), vmem((1, 128))], [vm()], nbytes=MIB)(chunks)
    own, cot = lax.optimization_barrier((own, cot))
    own = lax.all_to_all(own, CHIPS, 0, 0, tiled=True).reshape(2 * Z, Z)
    got = lax.ppermute(own, "c", CORE)
    total = call(join_body, sds((G, Z, Z)), [vm()] * 2, nbytes=2 * MIB)(own, got)
    return cot, total, eff[0, :EEZS]


def solution(mesh):
    fine = Mesh(mesh.devices.reshape(2, 4, 2, 4, 2), ("zl", "x", "c", "y", "zh"))
    field = P(None, LON, LAT, None)
    placed = (
        field,
        field,
        field,
        P(None, ALL),
        P(ALL, None),
        P(ALL),
        P(LON, LAT),
        P(LON, LAT),
    ) + (P(),) * 8
    return jax.shard_map(
        body,
        mesh=fine,
        in_specs=placed,
        out_specs=(field, P(), P()),
        check_vma=False,
    )
```

time: 136 us -> 98.5 us (0.72)
  blocking collectives: 39.3 us -> 15.8 us
  Pallas kernels: 54.3 us -> 32.2 us
  waiting for transfers between devices: 2.14 us -> 12.2 us
  local copies, waits for them, and re-layouts: 8.19 us -> 0.56 us
  starting transfers between devices: 30.8 us -> 36.3 us
    all_to_all x1 -> x0, blocking collectives: 22.9 us -> none  [body(): chunks = lax.all_to_all(chunks, CHIPS, 0, 0, tiled=True)]
    pallas_call x10 -> x11, Pallas kernels: 54.3 us -> 32.2 us  [the longest x10 25.2 us: go(): run(*[in_hbm(a) if not place or n in far else near_core(a) if a.size >= 8...]
    all_to_all x0 -> x1, starting transfers between devices: none -> 9.68 us  [body(): lax.all_to_all(chunks.reshape(NCHIP, 1, CH * 128), CHIPS, 0, 0, tiled=True)]
    all_to_all x0 -> x1, waiting for transfers between devices: none -> 5.74 us  [body(): lax.all_to_all(chunks.reshape(NCHIP, 1, CH * 128), CHIPS, 0, 0, tiled=True)]
    unnamed x25 -> x22, local copies, waits for them, and re-layouts: 5.06 us -> 0.05 us
    all_to_all x1, waiting for transfers between devices: 0.01 us -> 3.89 us  [body(): pay = lax.all_to_all(pay, ALL, 0, 0, tiled=True)]
    ppermute x2, starting transfers between devices: 8.82 us -> 6.29 us  [exchange(): lax.ppermute(ta, LAT, LAT_A)]
    all_to_all x2 -> x0, local copies, waits for them, and re-layouts: 1.95 us -> none  [body(): chunks = lax.all_to_all(chunks, CHIPS, 0, 0, tiled=True)]
  transfers between devices with their start and end apart: 11 -> 12, of which waited for: 2 -> 4; matrix products, arithmetic and copies ran while one was open for 1% -> 1% of each run, Pallas kernels for 15% -> 17%
where the time goes in v2:
time: 98.5 us; the launch traced here: 98 us
  starting transfers between devices  36.3 us (37%)
  Pallas kernels  32.2 us (33%)
  blocking collectives  15.8 us (16%)
  waiting for transfers between devices  12.2 us (12%)
    pallas_call x10, Pallas kernels, go(): run(*[in_hbm(a) if not place or n in far else near_core(a) if a.size >= 8...  25.2 us
    all_to_all x1, blocking collectives, body(): own = lax.all_to_all(own, CHIPS, 0, 0, tiled=True).reshape(2 * Z, Z)  15.8 us
    all_to_all x1, starting transfers between devices, body(): pay = lax.all_to_all(pay, ALL, 0, 0, tiled=True)  11.5 us
    all_to_all x1, starting transfers between devices, body(): lax.all_to_all(chunks.reshape(NCHIP, 1, CH * 128), CHIPS, 0, 0, tiled=True)  9.68 us
    pallas_call x1, Pallas kernels, body(): pl.pallas_call(rest_body, grid=(CHUNKS,), out_shape=sds(field), in_specs=...  7.04 us
    ppermute x2, starting transfers between devices, exchange(): lax.ppermute(ta, LAT, LAT_A)  6.29 us
    all_to_all x1, waiting for transfers between devices, body(): lax.all_to_all(chunks.reshape(NCHIP, 1, CH * 128), CHIPS, 0, 0, tiled=True)  5.74 us
    all_to_all x1, waiting for transfers between devices, body(): pay = lax.all_to_all(pay, ALL, 0, 0, tiled=True)  3.89 us
  transfers between devices with their start and end apart: 12, of which 4 were waited for; matrix products, arithmetic and copies ran while one was open for 1% of the time, Pallas kernels for 17%

profile of v2, /device:TPU:1, one launch (start us, length us, event | category | flops | bytes accessed | tf_op | source)
XLA Modules:
  0.0 98.0 jit_solution(18298553093034282260)
XLA Ops:
  0.7 3.0 %shard_map.175 = (f32[5,32,256]{2,1,0:T(8,128)S(1)}, f32[5,32,256]{2,1,0:T(8,128)S(1)}, f32[5,16,256]{2,1,0:T(8,128)S(1)}, f32[5,16,256]{2,1,0:T(8,128)S(1)}, f32[128,128]{1,0:T(8,128)}) custom-call(f32[4,16,32,256]{3,2,1,0:T(8,128)} %refs_2_.1, s32[16,32]{1,0:T(8,128)} %ocean.3, s32[16,32]{1,0:T(8,128)} %bitcast.32, s32[1,32]{1,0:T(1,128)} %bitcast.33, ...), custom_call_target="tpu_custom_call" | custom-call | flops 134217728 | bytes 3145728 | tf_op jit(solution)/shard_map/pallas_call | solution.py:61
  3.7 11.5 %all-to-all-start = ((f32[128,1,128]{2,1,0:T(1,128)}), f32[128,1,128]{2,1,0:T(1,128)S(1)}, u32[]{:S(2)}, u32[]{:S(2)}) async-start(f32[128,1,128]{2,1,0:T(1,128)} %bitcast.4), calls=%async_computation | async-start | bytes 131072 | tf_op jit(solution)/shard_map/all_to_all | solution.py:539
  15.2 1.1 %collective-permute-start = (f32[5,32,256]{2,1,0:T(8,128)S(1)}, f32[5,32,256]{2,1,0:T(8,128)S(1)}, u32[]{:S(2)}, u32[]{:S(2)}) collective-permute-start(f32[5,32,256]{2,1,0:T(8,128)S(1)} %get-tuple-element.43), channel_id=1, source_target_pairs={{0,8},{8,0},{16,24},{24,16},{32,40},{40,32},{48,56},{56,48},{64,72... | collective-permute-start | bytes 491528 | tf_op jit(solution)/shard_map/ppermute | solution.py:495
  17.1 3.1 %collective-permute-start.2 = (f32[5,16,256]{2,1,0:T(8,128)S(1)}, f32[5,16,256]{2,1,0:T(8,128)S(1)}, u32[]{:S(2)}, u32[]{:S(2)}) collective-permute-start(f32[5,16,256]{2,1,0:T(8,128)S(1)} %get-tuple-element.45), channel_id=1, source_target_pairs={{0,1},{1,0},{2,3},{3,2},{4,5},{5,4},{6,7},{7,6},{8,9},{9,8},{10,11... | collective-permute-start | bytes 245768 | tf_op jit(solution)/shard_map/ppermute | solution.py:497
  20.8 3.9 %all-to-all-done = f32[128,1,128]{2,1,0:T(1,128)S(1)} async-done(((f32[128,1,128]{2,1,0:T(1,128)}), f32[128,1,128]{2,1,0:T(1,128)S(1)}, u32[]{:S(2)}, u32[]{:S(2)}) %all-to-all-start) | async-done | bytes 65568 | tf_op jit(solution)/shard_map/all_to_all | solution.py:539
  24.7 1.6 %shard_map.176 = (f32[512,128]{1,0:T(8,128)S(1)}, f32[512,128]{1,0:T(8,128)S(1)}, f32[512,128]{1,0:T(8,128)S(1)}, f32[512,256]{1,0:T(8,128)S(1)}, bf16[4,256,256]{2,1,0:T(8,128)(2,1)S(1)}) custom-call(s32[16,32]{1,0:T(8,128)S(1)} %copy-done.7, s32[16,32]{1,0:T(8,128)S(1)} %copy-done.9, f32[1,64]{1,0:T(1,128)S(1)} %bitcast.27, f32[128,128]{1,0:T(8,128)S(1)} %bitcast.20, ...), custom_call_target="tpu_custom_call" | custom-call | flops 536870912 | bytes 1048576 | tf_op jit(solution)/shard_map/pallas_call | solution.py:61
  26.4 4.1 %shard_map.177 = (bf16[4,512,256]{2,1,0:T(8,128)(2,1)S(1)}, bf16[4,512,256]{2,1,0:T(8,128)(2,1)S(1)}, bf16[4,512,256]{2,1,0:T(8,128)(2,1)S(1)}, f32[4,512,256]{2...) custom-call(f32[4,4]{1,0:T(4,128)S(1)} %copy-done.3, f32[4]{0:T(128)S(1)} %copy-done.6, ...), custom_call_target="tpu_custom_call" | custom-call | flops 536870912 | bytes 8388608 | tf_op jit(solution)/shard_map/pallas_call | solution.py:61
  30.6 5.1 %shard_map.178 = (f32[4,16,32,256]{3,2,1,0:T(8,128)S(1)}, bf16[4,512,256]{2,1,0:T(8,128)(2,1)S(1)}, bf16[4,512,256]{2,1,0:T(8,128)(2,1)S(1)}, f32[8,128]{1,0:T(8...) custom-call(f32[4,4]{1,0:T(4,128)S(1)} %copy-done.3, ...), custom_call_target="tpu_custom_call" | custom-call | flops 1073741824 | bytes 16777216 | tf_op jit(solution)/shard_map/pallas_call | solution.py:61
  35.7 1.1 %collective-permute-start.4 = (f32[4,32,256]{2,1,0:T(8,128)S(1)}, f32[4,32,256]{2,1,0:T(8,128)S(1)}, u32[]{:S(2)}, u32[]{:S(2)}) collective-permute-start(f32[4,32,256]{2,1,0:T(8,128)S(1)} %get-tuple-element.58), channel_id=1, source_target_pairs={{0,8},{8,0},{16,24},{24,16},{32,40},{40,32},{48,56},{56,48},{64,72... | collective-permute-start | bytes 393224 | tf_op jit(solution)/shard_map/ppermute | solution.py:495
  36.9 3.2 %collective-permute-start.6 = (f32[4,16,256]{2,1,0:T(8,128)S(1)}, f32[4,16,256]{2,1,0:T(8,128)S(1)}, u32[]{:S(2)}, u32[]{:S(2)}) collective-permute-start(f32[4,16,256]{2,1,0:T(8,128)S(1)} %get-tuple-element.60), channel_id=1, source_target_pairs={{0,1},{1,0},{2,3},{3,2},{4,5},{5,4},{6,7},{7,6},{8,9},{9,8},{10,11... | collective-permute-start | bytes 196616 | tf_op jit(solution)/shard_map/ppermute | solution.py:497
  40.1 0.8 collective-permute-start.7
  41.0 3.1 %shard_map.179 = (bf16[4,512,256]{2,1,0:T(8,128)(2,1)S(1)}, bf16[4,512,256]{2,1,0:T(8,128)(2,1)S(1)}, bf16[4,512,256]{2,1,0:T(8,128)(2,1)S(1)}, f32[4,512,256]{2,1,0:T(8,128)S(1)}, f32[512,128]{1,0:T(8,128)S(1)}) custom-call(f32[4,4]{1,0:T(4,128)S(1)} %copy-done.3, f32[4]{0:T(128)S(1)} %copy-done.6, bf16[4,512,256]{2,1,0:T(8,128)(2,1)} %bitcast.28, ...), custom_call_target="tpu_custom_call" | custom-call | flops 536870912 | bytes 8388608 | tf_op jit(solution)/shard_map/pallas_call | solution.py:61
  44.1 0.8 shard_map.180.refs_20_
  44.9 5.5 %shard_map.181 = (f32[4,512,256]{2,1,0:T(8,128)}, f32[4,512,256]{2,1,0:T(8,128)}, f32[512,128]{1,0:T(8,128)}, f32[512,128]{1,0:T(8,128)}, f32[520,256]{1,0:T(8,128)S(1)}, /*index=5*/f32[520,256]{1,0:T(8,128)S(1)}) custom-call(f32[4,4]{1,0:T(4,128)S(1)} %copy-done.3, f32[4]{0:T(128)S(1)} %copy-done.6, f32[4,16,32,256]{3,2,1,0:T(8,128)S(1)} %get-tuple-element.57.refs_2_, ...), custom_call_target="tpu_custom_call" | custom-call | flops 1073741824 | bytes 16777216 | tf_op jit(solution)/shard_map/pallas_call | solution.py:61
  50.4 1.3 %collective-permute-start.8 = (f32[520,256]{1,0:T(8,128)S(1)}, f32[520,256]{1,0:T(8,128)S(1)}, u32[]{:S(2)}, u32[]{:S(2)}) collective-permute-start(f32[520,256]{1,0:T(8,128)S(1)} %get-tuple-element.74), channel_id=1, source_target_pairs={{0,8},{8,0},{1,9},{9,1},{2,10},{10,2},{3,11},{11,3},{4,12},{12,4},... | collective-permute-start | bytes 1597448 | tf_op jit(solution)/shard_map/ppermute | solution.py:625
  51.7 1.5 %collective-permute-done.8.got = f32[520,256]{1,0:T(8,128)S(1)} collective-permute-done((f32[520,256]{1,0:T(8,128)S(1)}, f32[520,256]{1,0:T(8,128)S(1)}, u32[]{:S(2)}, u32[]{:S(2)}) %collective-permute-start.8) | collective-permute-done | bytes 532512 | tf_op jit(solution)/shard_map/ppermute | solution.py:625
  53.2 0.9 shard_map.182
  54.1 9.7 %all-to-all-start.1 = ((f32[64,1,2176]{2,1,0:T(1,128)}), f32[64,1,2176]{2,1,0:T(1,128)S(1)}, u32[]{:S(2)}, u32[]{:S(2)}) async-start(f32[64,1,2176]{2,1,0:T(1,128)} %bitcast.10), calls=%async_computation.1 | async-start | bytes 1114112 | tf_op jit(solution)/shard_map/all_to_all | solution.py:627
  63.8 7.0 %shard_map.184 = f32[4,512,256]{2,1,0:T(8,128)} custom-call(f32[4,4]{1,0:T(4,128)S(1)} %copy-done.3, f32[4]{0:T(128)S(1)} %copy-done.6, bf16[4,512,256]{2,1,0:T(8,128)(2,1)} %bitcast.29, f32[4,512,256]{2,1,0:T(8,128)} %get-tuple-element.76.m_in, f32[4,512,256]{2,1,0:T(8,128)} %get-tuple-element.77.ge_in, f32[512,128]{1,0:T(8,128)} %get-tuple-element.78.q_in, ...), custom_call_target="tpu_custom_call" | custom-call | flops 1073741824 | bytes 12582912 | tf_op jit(solution)/shard_map/pallas_call | solution.py:611
  70.8 5.7 %all-to-all-done.1 = f32[64,1,2176]{2,1,0:T(1,128)S(1)} async-done(((f32[64,1,2176]{2,1,0:T(1,128)}), f32[64,1,2176]{2,1,0:T(1,128)S(1)}, u32[]{:S(2)}, u32[]{:S(2)}) %all-to-all-start.1) | async-done | bytes 557088 | tf_op jit(solution)/shard_map/all_to_all | solution.py:627
  76.7 15.8 %all_to_all.21 = f32[64,8,256]{2,1,0:T(8,128)S(1)} all-to-all(f32[64,8,256]{2,1,0:T(8,128)S(1)} %get-tuple-element.81), channel_id=1, replica_groups=mesh['zl'=2,'x'=4,'c'=2,'y'=4,'zh'=2] {'zl','x','y','zh'}, dimensions={0} | all-to-all | bytes 1048576 | tf_op jit(solution)/shard_map/all_to_all | solution.py:631
  92.4 3.0 %collective-permute-start.9 = (f32[512,256]{1,0:T(8,128)S(1)}, f32[512,256]{1,0:T(8,128)S(1)}, u32[]{:S(2)}, u32[]{:S(2)}) collective-permute-start(f32[512,256]{1,0:T(8,128)S(1)} %bitcast.18), channel_id=1, source_target_pairs={{0,8},{8,0},{1,9},{9,1},{2,10},{10,2},{3,11},{11,3},{4,12},{12,4},... | collective-permute-start | bytes 1572872 | tf_op jit(solution)/shard_map/ppermute | solution.py:632
  96.0 1.0 %collective-permute-done.9.got = f32[512,256]{1,0:T(8,128)S(1)} collective-permute-done((f32[512,256]{1,0:T(8,128)S(1)}, f32[512,256]{1,0:T(8,128)S(1)}, u32[]{:S(2)}, u32[]{:S(2)}) %collective-permute-start.9) | collective-permute-done | bytes 524320 | tf_op jit(solution)/shard_map/ppermute | solution.py:632
  97.0 1.1 %shard_map.185 = f32[4,256,256]{2,1,0:T(8,128)} custom-call(f32[512,256]{1,0:T(8,128)S(1)} %bitcast.19, f32[512,256]{1,0:T(8,128)S(1)} %collective-permute-done.9.got), custom_call_target="tpu_custom_call" | custom-call | bytes 2097152 | tf_op jit(solution)/shard_map/pallas_call | solution.py:61
  (35 shorter events, 2.1 us)
Async XLA Ops:
  0.6 24.1 %copy-start.7 = (s32[16,32]{1,0:T(8,128)S(1)}, s32[16,32]{1,0:T(8,128)}, u32[]{:S(2)}) copy-start(s32[16,32]{1,0:T(8,128)} %ocean.3) | copy-start | bytes 6148
  0.6 24.1 %copy-start.10 = (f32[64]{0:T(128)S(1)}, f32[64]{0:T(128)}, u32[]{:S(2)}) copy-start(f32[64]{0:T(128)} %param.24) | copy-start | bytes 772
  0.7 24.1 %copy-start.9 = (s32[16,32]{1,0:T(8,128)S(1)}, s32[16,32]{1,0:T(8,128)}, u32[]{:S(2)}) copy-start(s32[16,32]{1,0:T(8,128)} %eez.1) | copy-start | bytes 6148
  0.7 24.1 %copy-start = (bf16[4,256,256]{2,1,0:T(8,128)(2,1)S(1)}, bf16[4,256,256]{2,1,0:T(8,128)(2,1)}, u32[]{:S(2)}) copy-start(bf16[4,256,256]{2,1,0:T(8,128)(2,1)} %ker.3) | copy-start | bytes 1572868
  0.7 25.7 %copy-start.2 = (f32[4,256]{1,0:T(4,128)S(1)}, f32[4,256]{1,0:T(4,128)}, u32[]{:S(2)}) copy-start(f32[4,256]{1,0:T(4,128)} %sel.1) | copy-start | bytes 12292
  0.7 25.7 %copy-start.3 = (f32[4,4]{1,0:T(4,128)S(1)}, f32[4,4]{1,0:T(4,128)}, u32[]{:S(2)}) copy-start(f32[4,4]{1,0:T(4,128)} %mix.1) | copy-start | bytes 196
  0.7 25.7 %copy-start.4 = (f32[4,256]{1,0:T(4,128)S(1)}, f32[4,256]{1,0:T(4,128)}, u32[]{:S(2)}) copy-start(f32[4,256]{1,0:T(4,128)} %mort.1) | copy-start | bytes 12292
  0.7 25.7 %copy-start.5 = (f32[256]{0:T(256)S(1)}, f32[256]{0:T(256)}, u32[]{:S(2)}) copy-start(f32[256]{0:T(256)} %param.30) | copy-start | bytes 3076
  0.7 25.7 %copy-start.6 = (f32[4]{0:T(128)S(1)}, f32[4]{0:T(128)}, u32[]{:S(2)}) copy-start(f32[4]{0:T(128)} %assim.1) | copy-start | bytes 52
  3.7 21.0 %all-to-all-start = ((f32[128,1,128]{2,1,0:T(1,128)}), f32[128,1,128]{2,1,0:T(1,128)S(1)}, u32[]{:S(2)}, u32[]{:S(2)}) async-start(f32[128,1,128]{2,1,0:T(1,128)} %bitcast.4), calls=%async_computation | async-start | bytes 131072 | tf_op jit(solution)/shard_map/all_to_all | solution.py:539
  15.2 15.4 %collective-permute-start = (f32[5,32,256]{2,1,0:T(8,128)S(1)}, f32[5,32,256]{2,1,0:T(8,128)S(1)}, u32[]{:S(2)}, u32[]{:S(2)}) collective-permute-start(f32[5,32,256]{2,1,0:T(8,128)S(1)} %get-tuple-element.43), channel_id=1, source_target_pairs={{0,8},{8,0},{16,24},{24,16},{32,40},{40,32},{48,56},{56,48},{64,72... | collective-permute-start | bytes 491528 | tf_op jit(solution)/shard_map/ppermute | solution.py:495
  16.3 14.2 %collective-permute-start.1 = (f32[5,32,256]{2,1,0:T(8,128)S(1)}, f32[5,32,256]{2,1,0:T(8,128)S(1)}, u32[]{:S(2)}, u32[]{:S(2)}) collective-permute-start(f32[5,32,256]{2,1,0:T(8,128)S(1)} %get-tuple-element.44), channel_id=1, source_target_pairs={{0,120},{8,16},{16,8},{24,32},{32,24},{40,48},{48,40},{56,64},{64,... | collective-permute-start | bytes 491528 | tf_op jit(solution)/shard_map/ppermute | solution.py:496
  17.1 13.5 %collective-permute-start.2 = (f32[5,16,256]{2,1,0:T(8,128)S(1)}, f32[5,16,256]{2,1,0:T(8,128)S(1)}, u32[]{:S(2)}, u32[]{:S(2)}) collective-permute-start(f32[5,16,256]{2,1,0:T(8,128)S(1)} %get-tuple-element.45), channel_id=1, source_target_pairs={{0,1},{1,0},{2,3},{3,2},{4,5},{5,4},{6,7},{7,6},{8,9},{9,8},{10,11... | collective-permute-start | bytes 245768 | tf_op jit(solution)/shard_map/ppermute | solution.py:497
  20.2 10.4 %collective-permute-start.3 = (f32[5,16,256]{2,1,0:T(8,128)S(1)}, f32[5,16,256]{2,1,0:T(8,128)S(1)}, u32[]{:S(2)}, u32[]{:S(2)}) collective-permute-start(f32[5,16,256]{2,1,0:T(8,128)S(1)} %get-tuple-element.46), channel_id=1, source_target_pairs={{1,2},{2,1},{3,4},{4,3},{5,6},{6,5},{9,10},{10,9},{11,12},{12,11},... | collective-permute-start | bytes 245768 | tf_op jit(solution)/shard_map/ppermute | solution.py:498
  24.7 5.8 %copy-start.1 = (f32[4,16,32,256]{3,2,1,0:T(8,128)S(1)}, f32[4,16,32,256]{3,2,1,0:T(8,128)}, u32[]{:S(2)}) copy-start(f32[4,16,32,256]{3,2,1,0:T(8,128)} %refs_2_.1) | copy-start | bytes 6291460
  24.7 5.8 %copy-start.8 = (f32[256]{0:T(256)S(1)}, f32[256]{0:T(256)}, u32[]{:S(2)}) copy-start(f32[256]{0:T(256)} %param.31) | copy-start | bytes 3076
  35.7 9.2 %collective-permute-start.4 = (f32[4,32,256]{2,1,0:T(8,128)S(1)}, f32[4,32,256]{2,1,0:T(8,128)S(1)}, u32[]{:S(2)}, u32[]{:S(2)}) collective-permute-start(f32[4,32,256]{2,1,0:T(8,128)S(1)} %get-tuple-element.58), channel_id=1, source_target_pairs={{0,8},{8,0},{16,24},{24,16},{32,40},{40,32},{48,56},{56,48},{64,72... | collective-permute-start | bytes 393224 | tf_op jit(solution)/shard_map/ppermute | solution.py:495
  36.8 8.0 %collective-permute-start.5 = (f32[4,32,256]{2,1,0:T(8,128)S(1)}, f32[4,32,256]{2,1,0:T(8,128)S(1)}, u32[]{:S(2)}, u32[]{:S(2)}) collective-permute-start(f32[4,32,256]{2,1,0:T(8,128)S(1)} %get-tuple-element.59), channel_id=1, source_target_pairs={{0,120},{8,16},{16,8},{24,32},{32,24},{40,48},{48,40},{56,64},{64,... | collective-permute-start | bytes 393224 | tf_op jit(solution)/shard_map/ppermute | solution.py:496
  36.9 7.9 %collective-permute-start.6 = (f32[4,16,256]{2,1,0:T(8,128)S(1)}, f32[4,16,256]{2,1,0:T(8,128)S(1)}, u32[]{:S(2)}, u32[]{:S(2)}) collective-permute-start(f32[4,16,256]{2,1,0:T(8,128)S(1)} %get-tuple-element.60), channel_id=1, source_target_pairs={{0,1},{1,0},{2,3},{3,2},{4,5},{5,4},{6,7},{7,6},{8,9},{9,8},{10,11... | collective-permute-start | bytes 196616 | tf_op jit(solution)/shard_map/ppermute | solution.py:497
  40.1 4.7 %collective-permute-start.7 = (f32[4,16,256]{2,1,0:T(8,128)S(1)}, f32[4,16,256]{2,1,0:T(8,128)S(1)}, u32[]{:S(2)}, u32[]{:S(2)}) collective-permute-start(f32[4,16,256]{2,1,0:T(8,128)S(1)} %get-tuple-element.61), channel_id=1, source_target_pairs={{1,2},{2,1},{3,4},{4,3},{5,6},{6,5},{9,10},{10,9},{11,12},{12,11},... | collective-permute-start | bytes 196616 | tf_op jit(solution)/shard_map/ppermute | solution.py:498
  50.4 2.9 %collective-permute-start.8 = (f32[520,256]{1,0:T(8,128)S(1)}, f32[520,256]{1,0:T(8,128)S(1)}, u32[]{:S(2)}, u32[]{:S(2)}) collective-permute-start(f32[520,256]{1,0:T(8,128)S(1)} %get-tuple-element.74), channel_id=1, source_target_pairs={{0,8},{8,0},{1,9},{9,1},{2,10},{10,2},{3,11},{11,3},{4,12},{12,4},... | collective-permute-start | bytes 1597448 | tf_op jit(solution)/shard_map/ppermute | solution.py:625
  54.1 22.5 %all-to-all-start.1 = ((f32[64,1,2176]{2,1,0:T(1,128)}), f32[64,1,2176]{2,1,0:T(1,128)S(1)}, u32[]{:S(2)}, u32[]{:S(2)}) async-start(f32[64,1,2176]{2,1,0:T(1,128)} %bitcast.10), calls=%async_computation.1 | async-start | bytes 1114112 | tf_op jit(solution)/shard_map/all_to_all | solution.py:627
  92.4 4.5 %collective-permute-start.9 = (f32[512,256]{1,0:T(8,128)S(1)}, f32[512,256]{1,0:T(8,128)S(1)}, u32[]{:S(2)}, u32[]{:S(2)}) collective-permute-start(f32[512,256]{1,0:T(8,128)S(1)} %bitcast.18), channel_id=1, source_target_pairs={{0,8},{8,0},{1,9},{9,1},{2,10},{10,2},{3,11},{11,3},{4,12},{12,4},... | collective-permute-start | bytes 1572872 | tf_op jit(solution)/shard_map/ppermute | solution.py:632

commit v3 on v2

--- a/solution.py
+++ b/solution.py
@@ -113,10 +113,9 @@
     ]
     for copy in copies:
         copy.start()
-
     ents, rows = cells.shape
     ne = rows * ents
-    devices = pay.shape[0]
+    devices = 2 * NCHIP
     tile_e = lax.broadcasted_iota(jnp.int32, (ents, ne), 1) // rows == lax.broadcasted_iota(
         jnp.int32, (ents, ne), 0
     )
@@ -126,18 +125,25 @@
     tile_rf = tile_r.astype(F32)
     lon_i = (cells[...] // 256).astype(F32)
     lat_i = (cells[...] % 256).astype(F32)
+    r_hi, r_rest = split(resid[...])
+    r_mid, r_lo = split(r_rest)
+    few = jnp.concatenate([count[...].astype(F32), r_hi, r_mid, r_lo, jnp.zeros((1, rows), F32)], axis=0)
+    wide = nn(
+        jnp.concatenate([lon_i, lat_i, few], axis=0).astype(BF16), tile_rf.astype(BF16)
+    )
 
     def flat(x):
-        spread_out = nn(x, tile_rf, precision=HI)
-        return jnp.sum(jnp.where(tile_e, spread_out, 0.0), axis=0, keepdims=True)
-
-    i_row = flat(lon_i).astype(jnp.int32)
-    j_row = flat(lat_i).astype(jnp.int32)
-    n_row = nn(count[...].astype(F32), tile_rf, precision=HI)
-    r_row = nn(resid[...], tile_rf, precision=HI)
+        return jnp.sum(jnp.where(tile_e, x, 0.0), axis=0, keepdims=True)
+
+    i_row = flat(wide[:ents]).astype(jnp.int32)
+    j_row = flat(wide[ents : 2 * ents]).astype(jnp.int32)
+    few = wide[2 * ents :]
+    n_row = few[0:1]
+    r_row = few[1:3] + few[3:5] + few[5:7]
     entry = (lax.broadcasted_iota(jnp.int32, (1, ne), 1) // rows).astype(F32)
     vals = jnp.where(entry < n_row, r_row, 0.0)
-    owner = (i_row // CI) * 8 + j_row // CJ
+    lon = i_row // CI
+    owner = (lon % 2) * NCHIP + (lon // 2) * 8 + j_row // CJ
     mine = lax.broadcasted_iota(jnp.int32, (devices, ne), 0) == owner
     mine_b = mine.astype(F32).astype(BF16)
     before = (
@@ -156,7 +162,8 @@
         put.append(jnp.zeros((128 - SLOTS * len(parts), ne), F32))
         return jnp.concatenate(put, axis=0).astype(BF16)
 
-    pay[...] = nt(mine_b, rows_of((h0, h1, a_row))) + nt(mine_b, rows_of((l0, l1, b_row)))
+    sorted_ = nt(mine_b, rows_of((h0, h1, a_row))) + nt(mine_b, rows_of((l0, l1, b_row)))
+    pay[...] = jnp.concatenate([sorted_[:NCHIP, :64], sorted_[NCHIP:, :64]], axis=1)
 
     oc = ocean[...].astype(F32)
     edge_i = (column(oc[CI - 1 : CI, :], CJ, Z), column(oc[0:1, :], CJ, Z))
@@ -189,9 +196,7 @@
     )
 
 
-def cells_body(ocean, eez, effort, pay, ker, ocol, ecol, zone, out, flipped, hot, hi, lo):
-    for g in range(G):
-        flipped[g] = ker[g].T
+def tables(ocean, eez, effort, ocol, ecol, zone):
     oc = ocean[...].astype(F32)
     ez = eez[...].astype(F32)
     lane = lax.broadcasted_iota(jnp.int32, (CJ, 128), 1)
@@ -200,26 +205,37 @@
         rows = slice(i * CJ, (i + 1) * CJ)
         ocol[rows] = column(oc[i : i + 1, :], CJ, 128)
         here = (column(ez[i : i + 1, :], CJ, 128).astype(jnp.int32) == lane).astype(F32)
-        zone[rows] = here
+        zone[rows] = here.astype(BF16)
         ecol[rows] = jnp.broadcast_to(jnp.sum(here * eff, axis=1, keepdims=True), (CJ, 128))
 
-    got = pay[...]
-    flip = got.T
+
+def gather_catch(own, other, hot, hi, lo):
+    core = lax.axis_index("c")
+    both = jnp.concatenate([own[...], other[...]], axis=0)
+    flip = both.T
+    flip = jnp.where(core == 0, flip[:64], flip[64:])
+    got = jnp.where(core == 0, both[:, :64], both[:, 64:])
     for k in range(SLOTS):
         where = flip[2 * SLOTS + k : 2 * SLOTS + k + 1, :].astype(jnp.int32)
         cell = lax.broadcasted_iota(jnp.int32, (N, 128), 0)
         hot[:, k * 128 : (k + 1) * 128] = (cell == where).astype(F32).astype(BF16)
-        both = jnp.concatenate(
+        pair = jnp.concatenate(
             [
                 jnp.broadcast_to(got[:, k : k + 1], (128, 128)),
                 jnp.broadcast_to(got[:, SLOTS + k : SLOTS + k + 1], (128, 128)),
             ],
             axis=1,
         )
-        top, rest = split(both)
+        top, rest = split(pair)
         hi[k * 128 : (k + 1) * 128, :] = top.astype(BF16)
         lo[k * 128 : (k + 1) * 128, :] = rest.astype(BF16)
-    out[...] = nn(hot[...], hi[...]) + nn(hot[...], lo[...])
+    return nn(hot[...], hi[...]) + nn(hot[...], lo[...])
+
+
+def by_zone(y, zone):
+    top, rest = split(y[...])
+    parts = jnp.concatenate([top, rest], axis=1).astype(BF16)
+    return jnp.sum(tn(parts, zone[...]), axis=0, keepdims=True)
 
 
 R = 128
@@ -246,39 +262,51 @@
     return tot
 
 
-def fwd_body(full, *refs):
-    if full:
-        mix, assim, saved, ker, turn, mort, sel, wt, ecol, st, prey, eaten, feed, gs, gain, rem, sem = refs
-    else:
-        mix, assim, saved, ker, turn, mort, sel, wt, ecol, st, prey, eaten, feed, gs, sem = refs
+def forward_rows(rows, mix, st, turn, sel, wt, prey, eaten, feed, gs):
+    s = [st[k, rows, :].astype(F32) for k in range(G)]
+    part = None
+    for k in range(G):
+        term = (sel[k : k + 1, :] * wt[...]) * s[k]
+        part = term if part is None else part + term
+    gs[rows, :] = part[:, :128] + part[:, 128:]
+    for g in range(G):
+        prey[g, rows, :] = mixed(s, mix, g).astype(BF16)
+    for g in range(G):
+        enc = nn(prey[g, rows, :], turn[g])
+        fd = enc * recip(enc + 1.0)
+        feed[g, rows, :] = fd
+        eaten[g, rows, :] = (st[g, rows, :].astype(F32) * fd).astype(BF16)
+
+
+def first_body(*refs):
+    mix, assim, saved, c_far, ker, mort, sel, wt, ocean, eez, effort = refs[:11]
+    ocol, ecol, zone, turn, st, prey, eaten, feed, gs, gain, c, rem, sem = refs[11:]
     copies = []
     for n in range(CHUNKS):
         rows = slice(n * R, (n + 1) * R)
         copies.append(pltpu.make_async_copy(saved.at[:, rows, :], st.at[:, rows, :], sem.at[n]))
         copies[-1].start()
+    copies.append(pltpu.make_async_copy(c_far, c, sem.at[CHUNKS]))
+    copies[-1].start()
+    for g in range(G):
+        turn[g] = ker[g].T
+    tables(ocean, eez, effort, ocol, ecol, zone)
     for n in range(CHUNKS):
         rows = slice(n * R, (n + 1) * R)
         copies[n].wait()
-        s = [st[k, rows, :].astype(F32) for k in range(G)]
-        part = None
+        forward_rows(rows, mix, st, turn, sel, wt, prey, eaten, feed, gs)
+        for g in range(G):
+            rem[g, rows, :] = nn(eaten[g, rows, :], ker[g])
+        parts = [rem[g, rows, :] for g in range(G)]
+        ef = two(ecol[rows, :])
         for k in range(G):
-            term = (sel[k : k + 1, :] * wt[...]) * s[k]
-            part = term if part is None else part + term
-        gs[rows, :] = part[:, :128] + part[:, 128:]
-        for g in range(G):
-            prey[g, rows, :] = mixed(s, mix, g).astype(BF16)
-        for g in range(G):
-            enc = nn(prey[g, rows, :], turn[g])
-            fd = enc * recip(enc + 1.0)
-            feed[g, rows, :] = fd
-            eaten[g, rows, :] = (st[g, rows, :].astype(F32) * fd).astype(BF16)
-        if full:
-            for g in range(G):
-                rem[g, rows, :] = nn(eaten[g, rows, :], ker[g])
-            parts = [rem[g, rows, :] for g in range(G)]
-            ef = two(ecol[rows, :])
-            for k in range(G):
-                gain[k, rows, :] = gain_of(k, mix, assim, mort, sel, ef, feed[k, rows, :], parts)
+            gain[k, rows, :] = gain_of(k, mix, assim, mort, sel, ef, feed[k, rows, :], parts)
+    copies[CHUNKS].wait()
+
+
+def second_body(mix, st, turn, sel, wt, prey, eaten, feed, gs):
+    for n in range(CHUNKS):
+        forward_rows(slice(n * R, (n + 1) * R), mix, st, turn, sel, wt, prey, eaten, feed, gs)
 
 
 def fill(pad, opad, c, la, lb, ta, tb, ocol):
@@ -313,7 +341,7 @@
     )
 
 
-def spread_row(i, t, pad, s4, mix, ocol, catch, gs, st, sel, spr, m_out, grm, y):
+def spread_row(i, pad, s4, mix, ocol, catch, gs, st, sel, spr, m_out, grm, y):
     rows = slice(i * CJ, (i + 1) * CJ)
     o = ocol[rows, :]
     acc = None
@@ -333,7 +361,7 @@
                 term = (-H * mix[g, k]) * ms[k]
                 tot = term if tot is None else tot + term
             grm[g, rows, lanes] = tot.astype(BF16)
-    y[rows, :] = H * ((o * catch[rows, t * 128 : (t + 1) * 128]) * gs[rows, :] - acc)
+    y[rows, :] = H * ((o * catch[rows, :]) * gs[rows, :] - acc)
 
 
 def enc_grad(g, assim, m, s, ge, fd):
@@ -342,17 +370,20 @@
 
 
 def adj_body(*refs):
-    mix, assim, c, la, lb, ta, tb, ocol, ecol, catch, gs, zone, st, feed, gain, ker, turn, sel, wt, spr = refs[:20]
-    c_out, grm, genc, eff, near, ola, olb, ota, otb, opad, pad, m_scr, t_scr, y = refs[20:]
+    mix, assim, c, la, lb, ta, tb, ocol, ecol, own, other, gs, zone, st, feed, gain, ker, turn, sel, wt, spr = refs[:21]
+    c_out, grm, genc, eff, near, later, ola, olb, ota, otb, opad, pad, m_scr, t_scr, y, catch, hot, hi, lo = refs[21:]
     par_i, par_j = lax.axis_index("c"), lax.axis_index("zh")
     fill(pad, opad, c, la, lb, ta, tb, ocol)
+    caught = gather_catch(own, other, hot, hi, lo)
+    later[...] = caught[:, :128]
+    catch[...] = caught[:, 128:]
     for n in range(CHUNKS):
         rows = slice(n * R, (n + 1) * R)
         for i in range(n * R // CJ, (n + 1) * R // CJ):
             s4 = around(opad, i, slice(None))
             near[i * CJ : (i + 1) * CJ, :] = s4
-            spread_row(i, 1, pad, s4, mix, ocol, catch, gs, st, sel, spr, m_scr, grm, y)
-        q = two(H * ocol[rows, :] * ecol[rows, :] * catch[rows, 128:])
+            spread_row(i, pad, s4, mix, ocol, catch, gs, st, sel, spr, m_scr, grm, y)
+        q = two(H * ocol[rows, :] * ecol[rows, :] * catch[rows, :])
         for g in range(G):
             ge = nn(grm[g, rows, :], turn[g])
             m, fd = m_scr[g, rows, :], feed[g, rows, :]
@@ -365,8 +396,7 @@
             gp = [t_scr[g, here, :] for g in range(G)]
             for k in range(G):
                 c_out[k, i] = m_scr[k, here, :] + mixed(gp, mix, k, True)
-    part = jnp.sum(tn(y[...], zone[...], precision=HI), axis=0, keepdims=True)
-    eff[...] = jnp.broadcast_to(part, (8, 128))
+    eff[...] = jnp.broadcast_to(by_zone(y, zone), (8, 128))
 
     def lon_rims(hi, lo):
         for g in range(G):
@@ -391,12 +421,22 @@
         kp[g] = tn(eaten[g], grm[g]) + tn(genc[g], prey[g])
 
 
+def kernel_half(dst, half, kp, eaten, grm, genc, prey):
+    for s in range(2):
+        g = 2 * half + s
+        dst[s * Z : (s + 1) * Z, :] = kp[g] + tn(eaten[g], grm[g]) + tn(genc[g], prey[g])
+
+
+def keep_body(kp, eaten, grm, genc, prey, keep):
+    kernel_half(keep, lax.axis_index("c"), kp, eaten, grm, genc, prey)
+
+
 def last_body(*refs):
     mix, assim, c, la, lb, ta, tb, ocol, ecol, catch, gs, zone, st, prey, eaten, feed, turn, sel, spr, near, kp, eff = refs[:22]
-    m_hbm, ge_hbm, q_hbm, e_hbm, keep, send, pad, m_scr, ge_scr, grm, genc, y, q_scr, sem = refs[22:]
+    m_hbm, ge_hbm, q_hbm, e_hbm, send, grm, genc, pad, m_scr, ge_scr, y, q_scr, sem = refs[22:]
     core = lax.axis_index("c")
     fill(pad, None, c, la, lb, ta, tb, ocol)
-    q_scr[...] = H * ocol[...] * ecol[...] * catch[:, :128]
+    q_scr[...] = H * ocol[...] * ecol[...] * catch[...]
     copies = [
         pltpu.make_async_copy(q_scr, q_hbm, sem.at[0]),
         pltpu.make_async_copy(ecol, e_hbm, sem.at[1]),
@@ -407,7 +447,7 @@
         rows = slice(n * R, (n + 1) * R)
         for i in range(n * R // CJ, (n + 1) * R // CJ):
             s4 = near[i * CJ : (i + 1) * CJ, :]
-            spread_row(i, 0, pad, s4, mix, ocol, catch, gs, st, sel, spr, m_scr, grm, y)
+            spread_row(i, pad, s4, mix, ocol, catch, gs, st, sel, spr, m_scr, grm, y)
         for g in range(G):
             ge = nn(grm[g, rows, :], turn[g])
             ge_scr[g, rows, :] = ge
@@ -419,13 +459,8 @@
                 pltpu.make_async_copy(src.at[:, rows, :], dst.at[:, rows, :], sem.at[2 + 2 * n + k])
             )
             copies[-1].start()
-    part = jnp.sum(tn(y[...], zone[...], precision=HI), axis=0, keepdims=True)
-    both = two(eff[...] + part)
-    for dst, half in ((send, 1 - core), (keep, core)):
-        dst[2 * Z :, :] = both
-        for s in range(2):
-            g = 2 * half + s
-            dst[s * Z : (s + 1) * Z, :] = kp[g] + tn(eaten[g], grm[g]) + tn(genc[g], prey[g])
+    send[2 * Z :, :] = two(eff[...] + by_zone(y, zone))
+    kernel_half(send, 1 - core, kp, eaten, grm, genc, prey)
     for copy in copies:
         copy.wait()
 
@@ -458,8 +493,8 @@
 CH = 17
 
 
-def merge_body(keep, got, out):
-    eff = keep[2 * Z : 2 * Z + 1, :128] + got[2 * Z : 2 * Z + 1, :128]
+def merge_body(keep, send, got, out):
+    eff = send[2 * Z : 2 * Z + 1, :128] + got[2 * Z : 2 * Z + 1, :128]
     for p in range(NCHIP):
         rows = slice(p * 8, p * 8 + 8)
         tot = keep[rows, :] + got[rows, :]
@@ -483,11 +518,19 @@
         out[p] = both
 
 
-def join_body(own, got, out):
+def join_body(own, got, out, sem):
     core = lax.axis_index("c")
-    for s in range(2):
-        out[2 * core + s] = own[s * Z : (s + 1) * Z, :]
-        out[2 * (1 - core) + s] = got[s * Z : (s + 1) * Z, :]
+    copies = []
+    for n, (half, src) in enumerate(((core, own), (1 - core, got))):
+        for s in range(2):
+            copies.append(
+                pltpu.make_async_copy(
+                    src.at[s * Z : (s + 1) * Z, :], out.at[2 * half + s], sem.at[2 * n + s]
+                )
+            )
+            copies[-1].start()
+    for copy in copies:
+        copy.wait()
 
 
 def exchange(la, lb, ta, tb):
@@ -517,14 +560,13 @@
     weight,
     spread,
 ):
-    devices = 128
     wt, spr = weight.reshape(1, Z), spread.reshape(1, Z)
     any_ = pl.BlockSpec(memory_space=pl.ANY)
     field = (G, N, Z)
     rims = [vmem((G + 1, CJ, Z))] * 2 + [vmem((G + 1, CI, Z))] * 2
     *rim, pay = call(
         prep_body,
-        rims + [vmem((devices, 128))],
+        rims + [vmem((NCHIP, 128))],
         [any_] + [vm()] * 4,
         [
             pltpu.VMEM((2, G, CJ, Z), F32),
@@ -536,65 +578,65 @@
         place=False,
     )(final_cotangent, ocean_mask, row_cells.T, row_count.reshape(1, -1), residuals)
     rim = exchange(*rim)
-    pay = lax.all_to_all(pay, ALL, 0, 0, tiled=True)
-
-    ocol, ecol, zone, catch, turn = call(
-        cells_body,
-        [vmem((N, 128))] * 3 + [vmem((N, 256)), vmem((G, Z, Z), BF16)],
-        [vm()] * 5,
-        [
-            pltpu.VMEM((N, SLOTS * 128), BF16),
-            pltpu.VMEM((SLOTS * 128, 256), BF16),
-            pltpu.VMEM((SLOTS * 128, 256), BF16),
-        ],
+    own = lax.all_to_all(pay, CHIPS, 0, 0, tiled=True)
+    own, middle = lax.optimization_barrier((own, saved_middle))
+    other = lax.ppermute(own, "c", CORE)
+
+    ocol, ecol, zone, turn, st, prey, eaten, feed, gs, gain, cot = call(
+        first_body,
+        [vmem((N, 128))] * 2
+        + [vmem((N, 128), BF16), vmem((G, Z, Z), BF16)]
+        + [vmem(field, BF16)] * 3
+        + [vmem(field), vmem((N, 128)), vmem(field), vmem((G, CI, CJ, Z))],
+        [sm(), sm(), any_, any_] + [vm()] * 7,
+        [pltpu.VMEM(field, F32), pltpu.SemaphoreType.DMA((CHUNKS + 1,))],
         flops=2**29,
-        nbytes=MIB,
-    )(ocean_mask, cell_eez, effort.reshape(1, EEZS), pay, kernel)
-
-    def forward(saved, full):
-        return call(
-            functools.partial(fwd_body, full),
-            [vmem(field, BF16)] * 3 + [vmem(field), vmem((N, 128))] + [vmem(field)] * full,
-            [sm(), sm(), any_] + [vm()] * 6,
-            [pltpu.VMEM(field, F32)] * full + [pltpu.SemaphoreType.DMA((CHUNKS,))],
-            flops=2**29,
-            nbytes=8 * MIB,
-            vmem=8,
-            far=(2,),
-        )(mix, assim, saved.reshape(field), kernel, turn, mortality, select, wt, ecol)
-
-    st, prey, eaten, feed, gs, gain = forward(saved_middle, True)
+        nbytes=8 * MIB,
+        vmem=8,
+        far=(2, 3),
+    )(
+        *(mix, assim, middle.reshape(field), final_cotangent, kernel, mortality, select, wt),
+        *(ocean_mask, cell_eez, effort.reshape(1, EEZS)),
+    )
     pads = pltpu.VMEM((G, CI + 2, CJ + 16, Z), F32)
-    cot, grm, genc, eff, near, *rim = call(
+    cot, grm, genc, eff, near, catch, *rim = call(
         adj_body,
         [vmem((G, CI, CJ, Z))]
         + [vmem(field, BF16)] * 2
-        + [vmem((8, 128)), vmem((N, 128))]
+        + [vmem((8, 128)), vmem((N, 128)), vmem((N, 128))]
         + [vmem((G, CJ, Z))] * 2
         + [vmem((G, CI, Z))] * 2,
-        [sm(), sm()] + [vm()] * 18,
+        [sm(), sm()] + [vm()] * 19,
         [pltpu.VMEM((CI + 2, CJ + 16, 128), F32), pads]
         + [pltpu.VMEM(field, F32)] * 2
-        + [pltpu.VMEM((N, 128), F32)],
+        + [pltpu.VMEM((N, 128), F32)] * 2
+        + [pltpu.VMEM((N, SLOTS * 128), BF16)]
+        + [pltpu.VMEM((SLOTS * 128, 256), BF16)] * 2,
         flops=2**30,
         nbytes=16 * MIB,
         vmem=16,
     )(
-        *(mix, assim, final_cotangent, *rim, ocol, ecol, catch, gs, zone, st, feed, gain),
+        *(mix, assim, cot, *rim, ocol, ecol, own, other, gs, zone, st, feed, gain),
         *(kernel, turn, select, wt, spr),
     )
     rim = exchange(*rim)
     kp = call(part_body, vmem((G, Z, Z)), [vm()] * 4, flops=2**29, nbytes=5 * MIB)(
         eaten, grm, genc, prey
     )
-    st, prey, eaten, feed, gs = forward(saved_start, False)
-    m, ge, q, ef, keep, send = call(
+    st = saved_start.reshape(field)
+    prey, eaten, feed, gs = call(
+        second_body,
+        [vmem(field, BF16)] * 2 + [vmem(field), vmem((N, 128))],
+        [sm()] + [vm()] * 4,
+        flops=2**28,
+        nbytes=4 * MIB,
+    )(mix, st, turn, select, wt)
+    m, ge, q, ef, send, grm, genc = call(
         last_body,
-        [pltpu.HBM(field, F32)] * 2 + [pltpu.HBM((N, 128), F32)] * 2 + [vmem((2 * Z + 8, Z))] * 2,
+        [pltpu.HBM(field, F32)] * 2 + [pltpu.HBM((N, 128), F32)] * 2 + [vmem((2 * Z + 8, Z))] + [vmem(field, BF16)] * 2,
         [sm(), sm()] + [vm()] * 20,
         [pads]
         + [pltpu.VMEM(field, F32)] * 2
-        + [pltpu.VMEM(field, BF16)] * 2
         + [pltpu.VMEM((N, 128), F32)] * 2
         + [pltpu.SemaphoreType.DMA((2 + 2 * CHUNKS,))],
         flops=2**30,
@@ -623,14 +665,24 @@
     cot = cot.reshape(G, CI, CJ, Z)
 
     got = lax.ppermute(send, "c", CORE)
-    chunks = call(merge_body, vmem((NCHIP * CH, 128)), [vm()] * 2, nbytes=2 * MIB)(keep, got)
+    keep = call(keep_body, vmem((2 * Z, Z)), [vm()] * 5, flops=2**28, nbytes=4 * MIB)(
+        kp, eaten, grm, genc, prey
+    )
+    chunks = call(merge_body, vmem((NCHIP * CH, 128)), [vm()] * 3, nbytes=2 * MIB)(keep, send, got)
     chunks = lax.all_to_all(chunks.reshape(NCHIP, 1, CH * 128), CHIPS, 0, 0, tiled=True)
     chunks = chunks.reshape(NCHIP * CH, 128)
     own, eff = call(sum_body, [vmem((NCHIP, 8, Z)), vmem((1, 128))], [vm()], nbytes=MIB)(chunks)
     own, cot = lax.optimization_barrier((own, cot))
     own = lax.all_to_all(own, CHIPS, 0, 0, tiled=True).reshape(2 * Z, Z)
     got = lax.ppermute(own, "c", CORE)
-    total = call(join_body, sds((G, Z, Z)), [vm()] * 2, nbytes=2 * MIB)(own, got)
+    total = call(
+        join_body,
+        [pltpu.HBM((G, Z, Z), F32)],
+        [vm()] * 2,
+        [pltpu.SemaphoreType.DMA((4,))],
+        nbytes=2 * MIB,
+        out_far=1,
+    )(own, got)[0]
     return cot, total, eff[0, :EEZS]
 
 

time: 98.5 us -> 98.3 us (level)
  Pallas kernels: 32.2 us -> 31 us
    ppermute x2, starting transfers between devices: 6.29 us -> 3.47 us  [exchange(): lax.ppermute(ta, LAT, LAT_A)]
    ppermute x0 -> x1, starting transfers between devices: none -> 1.85 us  [body(): other = lax.ppermute(own, 'c', CORE)]
    ppermute x1, starting transfers between devices: 1.31 us -> 2.7 us  [body(): got = lax.ppermute(send, 'c', CORE)]
    pallas_call x10, Pallas kernels: 25.2 us -> 23.9 us  [go(): run(*[in_hbm(a) if not place or n in far else near_core(a) if a.size >= 8...]
    ppermute x2, starting transfers between devices: 0.8 us -> 1.99 us  [exchange(): lax.ppermute(lb, LON, LON_B)]
    all_to_all x1, waiting for transfers between devices: 3.89 us -> 5.08 us  [body(): own = lax.all_to_all(pay, CHIPS, 0, 0, tiled=True)]
  transfers between devices with their start and end apart: 12 -> 13, of which waited for: 4 -> 5; matrix products, arithmetic and copies ran while one was open for 1% -> 1% of each run, Pallas kernels for 17% -> 15%
where the time goes in v3:
time: 98.3 us; the launch traced here: 97.9 us
  starting transfers between devices  36.8 us (37%)
  Pallas kernels  31 us (32%)
  blocking collectives  15.5 us (16%)
  waiting for transfers between devices  13 us (13%)
  between operations  1.09 us (1%)
    pallas_call x10, Pallas kernels, go(): run(*[in_hbm(a) if not place or n in far else near_core(a) if a.size >= 8...  23.9 us
    all_to_all x1, blocking collectives, body(): own = lax.all_to_all(own, CHIPS, 0, 0, tiled=True).reshape(2 * Z, Z)  15.5 us
    all_to_all x1, starting transfers between devices, body(): own = lax.all_to_all(pay, CHIPS, 0, 0, tiled=True)  10.8 us
    all_to_all x1, starting transfers between devices, body(): lax.all_to_all(chunks.reshape(NCHIP, 1, CH * 128), CHIPS, 0, 0, tiled=True)  9.58 us
    pallas_call x1, Pallas kernels, body(): pl.pallas_call(rest_body, grid=(CHUNKS,), out_shape=sds(field), in_specs=...  7.03 us
    all_to_all x1, waiting for transfers between devices, body(): lax.all_to_all(chunks.reshape(NCHIP, 1, CH * 128), CHIPS, 0, 0, tiled=True)  5.43 us
    all_to_all x1, waiting for transfers between devices, body(): own = lax.all_to_all(pay, CHIPS, 0, 0, tiled=True)  5.08 us
    ppermute x2, starting transfers between devices, exchange(): lax.ppermute(ta, LAT, LAT_A)  3.47 us
  transfers between devices with their start and end apart: 13, of which 5 were waited for; matrix products, arithmetic and copies ran while one was open for 1% of the time, Pallas kernels for 15%

profile of v3, /device:TPU:1, one launch (start us, length us, event | category | flops | bytes accessed | tf_op | source)
XLA Modules:
  0.0 97.9 jit_solution(18057835717287722333)
XLA Ops:
  0.7 3.0 %shard_map.175 = (f32[5,32,256]{2,1,0:T(8,128)S(1)}, f32[5,32,256]{2,1,0:T(8,128)S(1)}, f32[5,16,256]{2,1,0:T(8,128)S(1)}, f32[5,16,256]{2,1,0:T(8,128)S(1)}, f32[64,128]{1,0:T(8,128)}) custom-call(f32[4,16,32,256]{3,2,1,0:T(8,128)} %refs_3_.1, s32[16,32]{1,0:T(8,128)} %refs_8_.1, s32[16,32]{1,0:T(8,128)} %bitcast.34, s32[1,32]{1,0:T(1,128)} %bitcast.35, ...), custom_call_target="tpu_custom_call" | custom-call | flops 134217728 | bytes 3145728 | tf_op jit(solution)/shard_map/pallas_call | solution.py:61
  3.7 1.5 %collective-permute-start = (f32[5,32,256]{2,1,0:T(8,128)S(1)}, f32[5,32,256]{2,1,0:T(8,128)S(1)}, u32[]{:S(2)}, u32[]{:S(2)}) collective-permute-start(f32[5,32,256]{2,1,0:T(8,128)S(1)} %get-tuple-element.50), channel_id=1, source_target_pairs={{0,8},{8,0},{16,24},{24,16},{32,40},{40,32},{48,56},{56,48},{64,72... | collective-permute-start | bytes 491528 | tf_op jit(solution)/shard_map/ppermute | solution.py:538
  5.2 1.3 %collective-permute-start.1 = (f32[5,32,256]{2,1,0:T(8,128)S(1)}, f32[5,32,256]{2,1,0:T(8,128)S(1)}, u32[]{:S(2)}, u32[]{:S(2)}) collective-permute-start(f32[5,32,256]{2,1,0:T(8,128)S(1)} %get-tuple-element.51), channel_id=1, source_target_pairs={{0,120},{8,16},{16,8},{24,32},{32,24},{40,48},{48,40},{56,64},{64,... | collective-permute-start | bytes 491528 | tf_op jit(solution)/shard_map/ppermute | solution.py:539
  6.5 10.8 %all-to-all-start = ((f32[64,1,128]{2,1,0:T(1,128)}), f32[64,1,128]{2,1,0:T(1,128)S(1)}, u32[]{:S(2)}, u32[]{:S(2)}) async-start(f32[64,1,128]{2,1,0:T(1,128)} %bitcast.3), calls=%async_computation | async-start | bytes 65536 | tf_op jit(solution)/shard_map/all_to_all | solution.py:581
  17.3 2.6 %collective-permute-start.2 = (f32[5,16,256]{2,1,0:T(8,128)S(1)}, f32[5,16,256]{2,1,0:T(8,128)S(1)}, u32[]{:S(2)}, u32[]{:S(2)}) collective-permute-start(f32[5,16,256]{2,1,0:T(8,128)S(1)} %get-tuple-element.52), channel_id=1, source_target_pairs={{0,1},{1,0},{2,3},{3,2},{4,5},{5,4},{6,7},{7,6},{8,9},{9,8},{10,11... | collective-permute-start | bytes 245768 | tf_op jit(solution)/shard_map/ppermute | solution.py:540
  20.6 5.1 %all-to-all-done = f32[64,1,128]{2,1,0:T(1,128)S(1)} async-done(((f32[64,1,128]{2,1,0:T(1,128)}), f32[64,1,128]{2,1,0:T(1,128)S(1)}, u32[]{:S(2)}, u32[]{:S(2)}) %all-to-all-start) | async-done | bytes 32800 | tf_op jit(solution)/shard_map/all_to_all | solution.py:581
  25.6 1.8 %collective-permute-start.4 = (f32[64,128]{1,0:T(8,128)S(1)}, f32[64,128]{1,0:T(8,128)S(1)}, u32[]{:S(2)}, u32[]{:S(2)}) collective-permute-start(f32[64,128]{1,0:T(8,128)S(1)} %bitcast.23), channel_id=1, source_target_pairs={{0,8},{8,0},{1,9},{9,1},{2,10},{10,2},{3,11},{11,3},{4,12},{12,4},... | collective-permute-start | bytes 98312 | tf_op jit(solution)/shard_map/ppermute | solution.py:583
  27.6 4.4 %shard_map.176 = (f32[512,128]{1,0:T(8,128)S(1)}, f32[512,128]{1,0:T(8,128)S(1)}, bf16[512,128]{1,0:T(8,128)(2,1)S(1)}, bf16[4,256,256]{2,1,0:T(8,128)(2,1)S(1)}...) custom-call(f32[4,4]{1,0:T(4,128)S(1)} %copy-done.3, ...), custom_call_target="tpu_custom_call" | custom-call | flops 536870912 | bytes 8388608 | tf_op jit(solution)/shard_map/pallas_call | solution.py:61
  32.0 6.0 %shard_map.177 = (f32[4,16,32,256]{3,2,1,0:T(8,128)S(1)}, bf16[4,512,256]{2,1,0:T(8,128)(2,1)S(1)}, bf16[4,512,256]{2,1,0:T(8,128)(2,1)S(1)}, f32[8,128]{1,0:T(8...) custom-call(f32[4,4]{1,0:T(4,128)S(1)} %copy-done.3, ...), custom_call_target="tpu_custom_call" | custom-call | flops 1073741824 | bytes 16777216 | tf_op jit(solution)/shard_map/pallas_call | solution.py:61
  38.8 0.9 collective-permute-start.7
  39.7 0.8 collective-permute-start.8
  40.6 2.1 %shard_map.179 = (bf16[4,512,256]{2,1,0:T(8,128)(2,1)S(1)}, bf16[4,512,256]{2,1,0:T(8,128)(2,1)S(1)}, f32[4,512,256]{2,1,0:T(8,128)S(1)}, f32[512,128]{1,0:T(8,128)S(1)}) custom-call(f32[4,4]{1,0:T(4,128)S(1)} %copy-done.3, bf16[4,512,256]{2,1,0:T(8,128)(2,1)S(1)} %bitcast.18, bf16[4,256,256]{2,1,0:T(8,128)(2,1)S(1)} %get-tuple-element.62.refs_17_.turn.refs_16_, ...), custom_call_target="tpu_custom_call" | custom-call | flops 268435456 | bytes 4194304 | tf_op jit(solution)/shard_map/pallas_call | solution.py:61
  42.6 0.8 shard_map.178.refs_20_.kp
  43.8 5.3 %shard_map.180 = (f32[4,512,256]{2,1,0:T(8,128)}, f32[4,512,256]{2,1,0:T(8,128)}, f32[512,128]{1,0:T(8,128)}, f32[512,128]{1,0:T(8,128)}, f32[520,256]{1,0:T(8,1...) custom-call(f32[4,4]{1,0:T(4,128)S(1)} %copy-done.3, f32[4]{0:T(128)S(1)} %copy-done.8, ...), custom_call_target="tpu_custom_call" | custom-call | flops 1073741824 | bytes 16777216 | tf_op jit(solution)/shard_map/pallas_call | solution.py:61
  49.1 2.7 %collective-permute-start.9 = (f32[520,256]{1,0:T(8,128)S(1)}, f32[520,256]{1,0:T(8,128)S(1)}, u32[]{:S(2)}, u32[]{:S(2)}) collective-permute-start(f32[520,256]{1,0:T(8,128)S(1)} %get-tuple-element.80.send), channel_id=1, source_target_pairs={{0,8},{8,0},{1,9},{9,1},{2,10},{10,2},{3,11},{11,3},{4,12},{12,4},... | collective-permute-start | bytes 1597448 | tf_op jit(solution)/shard_map/ppermute | solution.py:667
  52.3 1.1 %collective-permute-done.9.got = f32[520,256]{1,0:T(8,128)S(1)} collective-permute-done((f32[520,256]{1,0:T(8,128)S(1)}, f32[520,256]{1,0:T(8,128)S(1)}, u32[]{:S(2)}, u32[]{:S(2)}) %collective-permute-start.9) | collective-permute-done | bytes 532512 | tf_op jit(solution)/shard_map/ppermute | solution.py:667
  53.3 0.9 shard_map.182
  54.2 9.6 %all-to-all-start.1 = ((f32[64,1,2176]{2,1,0:T(1,128)}), f32[64,1,2176]{2,1,0:T(1,128)S(1)}, u32[]{:S(2)}, u32[]{:S(2)}) async-start(f32[64,1,2176]{2,1,0:T(1,128)} %bitcast.10), calls=%async_computation.1 | async-start | bytes 1114112 | tf_op jit(solution)/shard_map/all_to_all | solution.py:672
  63.8 7.0 %shard_map.184 = f32[4,512,256]{2,1,0:T(8,128)} custom-call(f32[4,4]{1,0:T(4,128)S(1)} %copy-done.3, f32[4]{0:T(128)S(1)} %copy-done.8, bf16[4,512,256]{2,1,0:T(8,128)(2,1)} %bitcast.17, f32[4,512,256]{2,1,0:T(8,128)} %get-tuple-element.82.m_in, f32[4,512,256]{2,1,0:T(8,128)} %get-tuple-element.83.ge_in, f32[512,128]{1,0:T(8,128)} %get-tuple-element.84.q_in, ...), custom_call_target="tpu_custom_call" | custom-call | flops 1073741824 | bytes 12582912 | tf_op jit(solution)/shard_map/pallas_call | solution.py:653
  70.8 5.4 %all-to-all-done.1 = f32[64,1,2176]{2,1,0:T(1,128)S(1)} async-done(((f32[64,1,2176]{2,1,0:T(1,128)}), f32[64,1,2176]{2,1,0:T(1,128)S(1)}, u32[]{:S(2)}, u32[]{:S(2)}) %all-to-all-start.1) | async-done | bytes 557088 | tf_op jit(solution)/shard_map/all_to_all | solution.py:672
  76.4 15.5 %all_to_all.22 = f32[64,8,256]{2,1,0:T(8,128)S(1)} all-to-all(f32[64,8,256]{2,1,0:T(8,128)S(1)} %get-tuple-element.87), channel_id=1, replica_groups=mesh['zl'=2,'x'=4,'c'=2,'y'=4,'zh'=2] {'zl','x','y','zh'}, dimensions={0} | all-to-all | bytes 1048576 | tf_op jit(solution)/shard_map/all_to_all | solution.py:676
  91.8 3.4 %collective-permute-start.10 = (f32[512,256]{1,0:T(8,128)S(1)}, f32[512,256]{1,0:T(8,128)S(1)}, u32[]{:S(2)}, u32[]{:S(2)}) collective-permute-start(f32[512,256]{1,0:T(8,128)S(1)} %bitcast.21), channel_id=1, source_target_pairs={{0,8},{8,0},{1,9},{9,1},{2,10},{10,2},{3,11},{11,3},{4,12},{12,4},... | collective-permute-start | bytes 1572872 | tf_op jit(solution)/shard_map/ppermute | solution.py:677
  95.7 1.0 %collective-permute-done.10.got = f32[512,256]{1,0:T(8,128)S(1)} collective-permute-done((f32[512,256]{1,0:T(8,128)S(1)}, f32[512,256]{1,0:T(8,128)S(1)}, u32[]{:S(2)}, u32[]{:S(2)}) %collective-permute-start.10) | collective-permute-done | bytes 524320 | tf_op jit(solution)/shard_map/ppermute | solution.py:677
  96.7 1.0 %shard_map.185 = f32[4,256,256]{2,1,0:T(8,128)} custom-call(f32[512,256]{1,0:T(8,128)S(1)} %bitcast.22, f32[512,256]{1,0:T(8,128)S(1)} %collective-permute-done.10.got), custom_call_target="tpu_custom_call" | custom-call | bytes 2097152 | tf_op jit(solution)/shard_map/pallas_call | solution.py:61
  (37 shorter events, 3.0 us)
Async XLA Ops:
  0.6 26.9 %copy-start.4 = (s32[16,32]{1,0:T(8,128)S(1)}, s32[16,32]{1,0:T(8,128)}, u32[]{:S(2)}) copy-start(s32[16,32]{1,0:T(8,128)} %refs_8_.1) | copy-start | bytes 6148
  0.6 26.9 %copy-start.5 = (f32[256]{0:T(256)S(1)}, f32[256]{0:T(256)}, u32[]{:S(2)}) copy-start(f32[256]{0:T(256)} %param.30) | copy-start | bytes 3076
  0.7 26.8 %copy-start.10 = (f32[64]{0:T(128)S(1)}, f32[64]{0:T(128)}, u32[]{:S(2)}) copy-start(f32[64]{0:T(128)} %param.24) | copy-start | bytes 772
  0.7 26.8 %copy-start.7 = (s32[16,32]{1,0:T(8,128)S(1)}, s32[16,32]{1,0:T(8,128)}, u32[]{:S(2)}) copy-start(s32[16,32]{1,0:T(8,128)} %refs_9_.1) | copy-start | bytes 6148
  0.7 26.8 %copy-start.1 = (bf16[4,256,256]{2,1,0:T(8,128)(2,1)S(1)}, bf16[4,256,256]{2,1,0:T(8,128)(2,1)}, u32[]{:S(2)}) copy-start(bf16[4,256,256]{2,1,0:T(8,128)(2,1)} %ker.1) | copy-start | bytes 1572868
  0.7 26.8 %copy-start.3 = (f32[4,4]{1,0:T(4,128)S(1)}, f32[4,4]{1,0:T(4,128)}, u32[]{:S(2)}) copy-start(f32[4,4]{1,0:T(4,128)} %mix.3) | copy-start | bytes 196
  0.7 26.8 %copy-start.8 = (f32[4]{0:T(128)S(1)}, f32[4]{0:T(128)}, u32[]{:S(2)}) copy-start(f32[4]{0:T(128)} %assim.1) | copy-start | bytes 52
  0.7 26.8 %copy-start.6 = (f32[4,256]{1,0:T(4,128)S(1)}, f32[4,256]{1,0:T(4,128)}, u32[]{:S(2)}) copy-start(f32[4,256]{1,0:T(4,128)} %mort.1) | copy-start | bytes 12292
  0.7 26.8 %copy-start.2 = (f32[4,256]{1,0:T(4,128)S(1)}, f32[4,256]{1,0:T(4,128)}, u32[]{:S(2)}) copy-start(f32[4,256]{1,0:T(4,128)} %sel.3) | copy-start | bytes 12292
  3.7 28.3 %copy-start.9 = (f32[256]{0:T(256)S(1)}, f32[256]{0:T(256)}, u32[]{:S(2)}) copy-start(f32[256]{0:T(256)} %param.31) | copy-start | bytes 3076
  3.7 28.2 %collective-permute-start = (f32[5,32,256]{2,1,0:T(8,128)S(1)}, f32[5,32,256]{2,1,0:T(8,128)S(1)}, u32[]{:S(2)}, u32[]{:S(2)}) collective-permute-start(f32[5,32,256]{2,1,0:T(8,128)S(1)} %get-tuple-element.50), channel_id=1, source_target_pairs={{0,8},{8,0},{16,24},{24,16},{32,40},{40,32},{48,56},{56,48},{64,72... | collective-permute-start | bytes 491528 | tf_op jit(solution)/shard_map/ppermute | solution.py:538
  5.2 26.7 %collective-permute-start.1 = (f32[5,32,256]{2,1,0:T(8,128)S(1)}, f32[5,32,256]{2,1,0:T(8,128)S(1)}, u32[]{:S(2)}, u32[]{:S(2)}) collective-permute-start(f32[5,32,256]{2,1,0:T(8,128)S(1)} %get-tuple-element.51), channel_id=1, source_target_pairs={{0,120},{8,16},{16,8},{24,32},{32,24},{40,48},{48,40},{56,64},{64,... | collective-permute-start | bytes 491528 | tf_op jit(solution)/shard_map/ppermute | solution.py:539
  6.5 19.2 %all-to-all-start = ((f32[64,1,128]{2,1,0:T(1,128)}), f32[64,1,128]{2,1,0:T(1,128)S(1)}, u32[]{:S(2)}, u32[]{:S(2)}) async-start(f32[64,1,128]{2,1,0:T(1,128)} %bitcast.3), calls=%async_computation | async-start | bytes 65536 | tf_op jit(solution)/shard_map/all_to_all | solution.py:581
  17.3 14.6 %collective-permute-start.2 = (f32[5,16,256]{2,1,0:T(8,128)S(1)}, f32[5,16,256]{2,1,0:T(8,128)S(1)}, u32[]{:S(2)}, u32[]{:S(2)}) collective-permute-start(f32[5,16,256]{2,1,0:T(8,128)S(1)} %get-tuple-element.52), channel_id=1, source_target_pairs={{0,1},{1,0},{2,3},{3,2},{4,5},{5,4},{6,7},{7,6},{8,9},{9,8},{10,11... | collective-permute-start | bytes 245768 | tf_op jit(solution)/shard_map/ppermute | solution.py:540
  19.9 12.0 %collective-permute-start.3 = (f32[5,16,256]{2,1,0:T(8,128)S(1)}, f32[5,16,256]{2,1,0:T(8,128)S(1)}, u32[]{:S(2)}, u32[]{:S(2)}) collective-permute-start(f32[5,16,256]{2,1,0:T(8,128)S(1)} %get-tuple-element.53), channel_id=1, source_target_pairs={{1,2},{2,1},{3,4},{4,3},{5,6},{6,5},{9,10},{10,9},{11,12},{12,11},... | collective-permute-start | bytes 245768 | tf_op jit(solution)/shard_map/ppermute | solution.py:541
  25.6 6.3 %collective-permute-start.4 = (f32[64,128]{1,0:T(8,128)S(1)}, f32[64,128]{1,0:T(8,128)S(1)}, u32[]{:S(2)}, u32[]{:S(2)}) collective-permute-start(f32[64,128]{1,0:T(8,128)S(1)} %bitcast.23), channel_id=1, source_target_pairs={{0,8},{8,0},{1,9},{9,1},{2,10},{10,2},{3,11},{11,3},{4,12},{12,4},... | collective-permute-start | bytes 98312 | tf_op jit(solution)/shard_map/ppermute | solution.py:583
  32.0 8.6 %copy-start = (bf16[4,16,32,256]{3,2,1,0:T(8,128)(2,1)S(1)}, bf16[4,16,32,256]{3,2,1,0:T(8,128)(2,1)}, u32[]{:S(2)}) copy-start(bf16[4,16,32,256]{3,2,1,0:T(8,128)(2,1)} %param.17) | copy-start | bytes 3145732
  38.0 5.7 %collective-permute-start.5 = (f32[4,32,256]{2,1,0:T(8,128)S(1)}, f32[4,32,256]{2,1,0:T(8,128)S(1)}, u32[]{:S(2)}, u32[]{:S(2)}) collective-permute-start(f32[4,32,256]{2,1,0:T(8,128)S(1)} %get-tuple-element.68), channel_id=1, source_target_pairs={{0,8},{8,0},{16,24},{24,16},{32,40},{40,32},{48,56},{56,48},{64,72... | collective-permute-start | bytes 393224 | tf_op jit(solution)/shard_map/ppermute | solution.py:538
  38.1 5.6 %collective-permute-start.6 = (f32[4,32,256]{2,1,0:T(8,128)S(1)}, f32[4,32,256]{2,1,0:T(8,128)S(1)}, u32[]{:S(2)}, u32[]{:S(2)}) collective-permute-start(f32[4,32,256]{2,1,0:T(8,128)S(1)} %get-tuple-element.69), channel_id=1, source_target_pairs={{0,120},{8,16},{16,8},{24,32},{32,24},{40,48},{48,40},{56,64},{64,... | collective-permute-start | bytes 393224 | tf_op jit(solution)/shard_map/ppermute | solution.py:539
  38.8 4.9 %collective-permute-start.7 = (f32[4,16,256]{2,1,0:T(8,128)S(1)}, f32[4,16,256]{2,1,0:T(8,128)S(1)}, u32[]{:S(2)}, u32[]{:S(2)}) collective-permute-start(f32[4,16,256]{2,1,0:T(8,128)S(1)} %get-tuple-element.70), channel_id=1, source_target_pairs={{0,1},{1,0},{2,3},{3,2},{4,5},{5,4},{6,7},{7,6},{8,9},{9,8},{10,11... | collective-permute-start | bytes 196616 | tf_op jit(solution)/shard_map/ppermute | solution.py:540
  39.7 4.0 %collective-permute-start.8 = (f32[4,16,256]{2,1,0:T(8,128)S(1)}, f32[4,16,256]{2,1,0:T(8,128)S(1)}, u32[]{:S(2)}, u32[]{:S(2)}) collective-permute-start(f32[4,16,256]{2,1,0:T(8,128)S(1)} %get-tuple-element.71), channel_id=1, source_target_pairs={{1,2},{2,1},{3,4},{4,3},{5,6},{6,5},{9,10},{10,9},{11,12},{12,11},... | collective-permute-start | bytes 196616 | tf_op jit(solution)/shard_map/ppermute | solution.py:541
  49.1 4.2 %collective-permute-start.9 = (f32[520,256]{1,0:T(8,128)S(1)}, f32[520,256]{1,0:T(8,128)S(1)}, u32[]{:S(2)}, u32[]{:S(2)}) collective-permute-start(f32[520,256]{1,0:T(8,128)S(1)} %get-tuple-element.80.send), channel_id=1, source_target_pairs={{0,8},{8,0},{1,9},{9,1},{2,10},{10,2},{3,11},{11,3},{4,12},{12,4},... | collective-permute-start | bytes 1597448 | tf_op jit(solution)/shard_map/ppermute | solution.py:667
  54.2 22.1 %all-to-all-start.1 = ((f32[64,1,2176]{2,1,0:T(1,128)}), f32[64,1,2176]{2,1,0:T(1,128)S(1)}, u32[]{:S(2)}, u32[]{:S(2)}) async-start(f32[64,1,2176]{2,1,0:T(1,128)} %bitcast.10), calls=%async_computation.1 | async-start | bytes 1114112 | tf_op jit(solution)/shard_map/all_to_all | solution.py:672
  91.8 4.9 %collective-permute-start.10 = (f32[512,256]{1,0:T(8,128)S(1)}, f32[512,256]{1,0:T(8,128)S(1)}, u32[]{:S(2)}, u32[]{:S(2)}) collective-permute-start(f32[512,256]{1,0:T(8,128)S(1)} %bitcast.21), channel_id=1, source_target_pairs={{0,8},{8,0},{1,9},{9,1},{2,10},{10,2},{3,11},{11,3},{4,12},{12,4},... | collective-permute-start | bytes 1572872 | tf_op jit(solution)/shard_map/ppermute | solution.py:677

commit v4 on v3

--- a/solution.py
+++ b/solution.py
@@ -342,7 +342,7 @@
 
 
 def spread_row(i, pad, s4, mix, ocol, catch, gs, st, sel, spr, m_out, grm, y):
-    rows = slice(i * CJ, (i + 1) * CJ)
+    rows = pl.ds(i * CJ, CJ)
     o = ocol[rows, :]
     acc = None
     for z in range(2):
@@ -370,7 +370,7 @@
 
 
 def adj_body(*refs):
-    mix, assim, c, la, lb, ta, tb, ocol, ecol, own, other, gs, zone, st, feed, gain, ker, turn, sel, wt, spr = refs[:21]
+    mix, assim, c, tb, ta, lb, la, ocol, ecol, own, other, gs, zone, st, feed, gain, ker, turn, sel, wt, spr = refs[:21]
     c_out, grm, genc, eff, near, later, ola, olb, ota, otb, opad, pad, m_scr, t_scr, y, catch, hot, hi, lo = refs[21:]
     par_i, par_j = lax.axis_index("c"), lax.axis_index("zh")
     fill(pad, opad, c, la, lb, ta, tb, ocol)
@@ -432,7 +432,7 @@
 
 
 def last_body(*refs):
-    mix, assim, c, la, lb, ta, tb, ocol, ecol, catch, gs, zone, st, prey, eaten, feed, turn, sel, spr, near, kp, eff = refs[:22]
+    mix, assim, c, tb, ta, lb, la, ocol, ecol, catch, gs, zone, st, prey, eaten, feed, turn, sel, spr, near, kp, eff = refs[:22]
     m_hbm, ge_hbm, q_hbm, e_hbm, send, grm, genc, pad, m_scr, ge_scr, y, q_scr, sem = refs[22:]
     core = lax.axis_index("c")
     fill(pad, None, c, la, lb, ta, tb, ocol)
@@ -443,22 +443,32 @@
     ]
     for copy in copies:
         copy.start()
-    for n in range(CHUNKS):
-        rows = slice(n * R, (n + 1) * R)
-        for i in range(n * R // CJ, (n + 1) * R // CJ):
-            s4 = near[i * CJ : (i + 1) * CJ, :]
-            spread_row(i, pad, s4, mix, ocol, catch, gs, st, sel, spr, m_scr, grm, y)
-        for g in range(G):
-            ge = nn(grm[g, rows, :], turn[g])
-            ge_scr[g, rows, :] = ge
+
+    @pl.loop(0, CI)
+    def _(i):
+        s4 = near[pl.ds(i * CJ, CJ), :]
+        spread_row(i, pad, s4, mix, ocol, catch, gs, st, sel, spr, m_scr, grm, y)
+
+    copies.append(pltpu.make_async_copy(m_scr, m_hbm, sem.at[2]))
+    copies[-1].start()
+    for g in range(G):
+        ge_scr[g] = nn(grm[g], turn[g])
+    copies.append(pltpu.make_async_copy(ge_scr, ge_hbm, sem.at[3]))
+    copies[-1].start()
+
+    @pl.loop(0, CI)
+    def _(i):
+        rows = pl.ds(i * CJ, CJ)
+        for g in range(G):
             genc[g, rows, :] = enc_grad(
-                g, assim, m_scr[g, rows, :], st[g, rows, :].astype(F32), ge, feed[g, rows, :]
+                g,
+                assim,
+                m_scr[g, rows, :],
+                st[g, rows, :].astype(F32),
+                ge_scr[g, rows, :],
+                feed[g, rows, :],
             )
-        for k, (src, dst) in enumerate(((m_scr, m_hbm), (ge_scr, ge_hbm))):
-            copies.append(
-                pltpu.make_async_copy(src.at[:, rows, :], dst.at[:, rows, :], sem.at[2 + 2 * n + k])
-            )
-            copies[-1].start()
+
     send[2 * Z :, :] = two(eff[...] + by_zone(y, zone))
     kernel_half(send, 1 - core, kp, eaten, grm, genc, prey)
     for copy in copies:
@@ -534,12 +544,11 @@
 
 
 def exchange(la, lb, ta, tb):
-    return (
-        lax.ppermute(la, LON, LON_A),
-        lax.ppermute(lb, LON, LON_B),
-        lax.ppermute(ta, LAT, LAT_A),
-        lax.ppermute(tb, LAT, LAT_B),
-    )
+    tb = lax.ppermute(tb, LAT, LAT_B)
+    ta = lax.ppermute(ta, LAT, LAT_A)
+    lb = lax.ppermute(lb, LON, LON_B)
+    la = lax.ppermute(la, LON, LON_A)
+    return la, lb, ta, tb
 
 
 def body(
@@ -590,8 +599,8 @@
         + [vmem(field), vmem((N, 128)), vmem(field), vmem((G, CI, CJ, Z))],
         [sm(), sm(), any_, any_] + [vm()] * 7,
         [pltpu.VMEM(field, F32), pltpu.SemaphoreType.DMA((CHUNKS + 1,))],
-        flops=2**29,
-        nbytes=8 * MIB,
+        flops=2**32,
+        nbytes=16 * MIB,
         vmem=8,
         far=(2, 3),
     )(
@@ -616,7 +625,7 @@
         nbytes=16 * MIB,
         vmem=16,
     )(
-        *(mix, assim, cot, *rim, ocol, ecol, own, other, gs, zone, st, feed, gain),
+        *(mix, assim, cot, *reversed(rim), ocol, ecol, own, other, gs, zone, st, feed, gain),
         *(kernel, turn, select, wt, spr),
     )
     rim = exchange(*rim)
@@ -628,8 +637,8 @@
         second_body,
         [vmem(field, BF16)] * 2 + [vmem(field), vmem((N, 128))],
         [sm()] + [vm()] * 4,
-        flops=2**28,
-        nbytes=4 * MIB,
+        flops=2**32,
+        nbytes=16 * MIB,
     )(mix, st, turn, select, wt)
     m, ge, q, ef, send, grm, genc = call(
         last_body,
@@ -638,13 +647,13 @@
         [pads]
         + [pltpu.VMEM(field, F32)] * 2
         + [pltpu.VMEM((N, 128), F32)] * 2
-        + [pltpu.SemaphoreType.DMA((2 + 2 * CHUNKS,))],
+        + [pltpu.SemaphoreType.DMA((4,))],
         flops=2**30,
         nbytes=16 * MIB,
         vmem=16,
         out_far=4,
     )(
-        *(mix, assim, cot, *rim, ocol, ecol, catch, gs, zone, st, prey, eaten, feed),
+        *(mix, assim, cot, *reversed(rim), ocol, ecol, catch, gs, zone, st, prey, eaten, feed),
         *(turn, select, spr, near, kp, eff),
     )
     block = pl.BlockSpec((G, R, Z), lambda n: (0, n, 0))

time: 98.3 us -> 98.3 us (level)
  starting transfers between devices: 36.8 us -> 42.9 us
  waiting for transfers between devices: 13 us -> 7.53 us
    ppermute x8, starting transfers between devices: 8.54 us -> 17.3 us  [the longest x2 10.6 us: exchange(): ta = lax.ppermute(ta, LAT, LAT_A)]
    all_to_all x1, waiting for transfers between devices: 5.08 us -> 0.01 us  [body(): own = lax.all_to_all(pay, CHIPS, 0, 0, tiled=True)]
    ppermute x1, starting transfers between devices: 2.7 us -> 0.64 us  [body(): got = lax.ppermute(send, 'c', CORE)]
    all_to_all x1, starting transfers between devices: 10.8 us -> 11.9 us  [body(): own = lax.all_to_all(pay, CHIPS, 0, 0, tiled=True)]
    ppermute x1, starting transfers between devices: 1.85 us -> 0.72 us  [body(): other = lax.ppermute(own, 'c', CORE)]
  transfers between devices with their start and end apart: 13 -> 13, of which waited for: 5 -> 3; matrix products, arithmetic and copies ran while one was open for 1% -> 1% of each run, Pallas kernels for 15% -> 15%
where the time goes in v4:
time: 98.3 us; the launch traced here: 97.9 us
  starting transfers between devices  42.9 us (44%)
  Pallas kernels  30.4 us (31%)
  blocking collectives  15.5 us (16%)
  waiting for transfers between devices  7.53 us (8%)
  between operations  1.1 us (1%)
    pallas_call x10, Pallas kernels, go(): run(*[in_hbm(a) if not place or n in far else near_core(a) if a.size >= 8...  23.4 us
    all_to_all x1, blocking collectives, body(): own = lax.all_to_all(own, CHIPS, 0, 0, tiled=True).reshape(2 * Z, Z)  15.5 us
    all_to_all x1, starting transfers between devices, body(): own = lax.all_to_all(pay, CHIPS, 0, 0, tiled=True)  11.9 us
    ppermute x2, starting transfers between devices, exchange(): ta = lax.ppermute(ta, LAT, LAT_A)  10.6 us
    all_to_all x1, starting transfers between devices, body(): lax.all_to_all(chunks.reshape(NCHIP, 1, CH * 128), CHIPS, 0, 0, tiled=True)  8.88 us
    pallas_call x1, Pallas kernels, body(): pl.pallas_call(rest_body, grid=(CHUNKS,), out_shape=sds(field), in_specs=...  7.03 us
    all_to_all x1, waiting for transfers between devices, body(): lax.all_to_all(chunks.reshape(NCHIP, 1, CH * 128), CHIPS, 0, 0, tiled=True)  5.43 us
    ppermute x1, starting transfers between devices, body(): got = lax.ppermute(own, 'c', CORE)  3.36 us
  transfers between devices with their start and end apart: 13, of which 3 were waited for; matrix products, arithmetic and copies ran while one was open for 1% of the time, Pallas kernels for 15%

profile of v4, /device:TPU:1, one launch (start us, length us, event | category | flops | bytes accessed | tf_op | source)
XLA Modules:
  0.0 97.9 jit_solution(14015940216793252060)
XLA Ops:
  0.7 3.0 %shard_map.175 = (f32[5,32,256]{2,1,0:T(8,128)S(1)}, f32[5,32,256]{2,1,0:T(8,128)S(1)}, f32[5,16,256]{2,1,0:T(8,128)S(1)}, f32[5,16,256]{2,1,0:T(8,128)S(1)}, f32[64,128]{1,0:T(8,128)}) custom-call(f32[4,16,32,256]{3,2,1,0:T(8,128)} %refs_3_.1, s32[16,32]{1,0:T(8,128)} %refs_8_.1, s32[16,32]{1,0:T(8,128)} %bitcast.33, s32[1,32]{1,0:T(1,128)} %bitcast.34, ...), custom_call_target="tpu_custom_call" | custom-call | flops 134217728 | bytes 3145728 | tf_op jit(solution)/shard_map/pallas_call | solution.py:61
  3.7 11.9 %all-to-all-start = ((f32[64,1,128]{2,1,0:T(1,128)}), f32[64,1,128]{2,1,0:T(1,128)S(1)}, u32[]{:S(2)}, u32[]{:S(2)}) async-start(f32[64,1,128]{2,1,0:T(1,128)} %bitcast.3), calls=%async_computation | async-start | bytes 65536 | tf_op jit(solution)/shard_map/all_to_all | solution.py:590
  15.7 2.2 %collective-permute-start.2 = (f32[5,32,256]{2,1,0:T(8,128)S(1)}, f32[5,32,256]{2,1,0:T(8,128)S(1)}, u32[]{:S(2)}, u32[]{:S(2)}) collective-permute-start(f32[5,32,256]{2,1,0:T(8,128)S(1)} %get-tuple-element.52), channel_id=1, source_target_pairs={{0,120},{8,16},{16,8},{24,32},{32,24},{40,48},{48,40},{56,64},{64,... | collective-permute-start | bytes 491528 | tf_op jit(solution)/shard_map/ppermute | solution.py:549
  17.9 1.6 %collective-permute-start.3 = (f32[5,32,256]{2,1,0:T(8,128)S(1)}, f32[5,32,256]{2,1,0:T(8,128)S(1)}, u32[]{:S(2)}, u32[]{:S(2)}) collective-permute-start(f32[5,32,256]{2,1,0:T(8,128)S(1)} %get-tuple-element.53), channel_id=1, source_target_pairs={{0,8},{8,0},{16,24},{24,16},{32,40},{40,32},{48,56},{56,48},{64,72... | collective-permute-start | bytes 491528 | tf_op jit(solution)/shard_map/ppermute | solution.py:550
  19.5 0.7 collective-permute-start
  20.2 5.2 %collective-permute-start.1 = (f32[5,16,256]{2,1,0:T(8,128)S(1)}, f32[5,16,256]{2,1,0:T(8,128)S(1)}, u32[]{:S(2)}, u32[]{:S(2)}) collective-permute-start(f32[5,16,256]{2,1,0:T(8,128)S(1)} %get-tuple-element.51), channel_id=1, source_target_pairs={{0,1},{1,0},{2,3},{3,2},{4,5},{5,4},{6,7},{7,6},{8,9},{9,8},{10,11... | collective-permute-start | bytes 245768 | tf_op jit(solution)/shard_map/ppermute | solution.py:548
  25.4 0.7 collective-permute-start.4
  26.2 4.3 %shard_map.176 = (f32[512,128]{1,0:T(8,128)S(1)}, f32[512,128]{1,0:T(8,128)S(1)}, bf16[512,128]{1,0:T(8,128)(2,1)S(1)}, bf16[4,256,256]{2,1,0:T(8,128)(2,1)S(1)}...) custom-call(f32[4,4]{1,0:T(4,128)S(1)} %copy-done.3, ...), custom_call_target="tpu_custom_call" | custom-call | flops 4294967296 | bytes 16777216 | tf_op jit(solution)/shard_map/pallas_call | solution.py:61
  30.6 6.0 %shard_map.177 = (f32[4,16,32,256]{3,2,1,0:T(8,128)S(1)}, bf16[4,512,256]{2,1,0:T(8,128)(2,1)S(1)}, bf16[4,512,256]{2,1,0:T(8,128)(2,1)S(1)}, f32[8,128]{1,0:T(8...) custom-call(f32[4,4]{1,0:T(4,128)S(1)} %copy-done.3, ...), custom_call_target="tpu_custom_call" | custom-call | flops 1073741824 | bytes 16777216 | tf_op jit(solution)/shard_map/pallas_call | solution.py:61
  36.9 1.3 %collective-permute-start.8 = (f32[4,32,256]{2,1,0:T(8,128)S(1)}, f32[4,32,256]{2,1,0:T(8,128)S(1)}, u32[]{:S(2)}, u32[]{:S(2)}) collective-permute-start(f32[4,32,256]{2,1,0:T(8,128)S(1)} %get-tuple-element.71), channel_id=1, source_target_pairs={{0,8},{8,0},{16,24},{24,16},{32,40},{40,32},{48,56},{56,48},{64,72... | collective-permute-start | bytes 393224 | tf_op jit(solution)/shard_map/ppermute | solution.py:550
  38.2 0.7 collective-permute-start.5
  38.9 5.4 %collective-permute-start.6 = (f32[4,16,256]{2,1,0:T(8,128)S(1)}, f32[4,16,256]{2,1,0:T(8,128)S(1)}, u32[]{:S(2)}, u32[]{:S(2)}) collective-permute-start(f32[4,16,256]{2,1,0:T(8,128)S(1)} %get-tuple-element.69), channel_id=1, source_target_pairs={{0,1},{1,0},{2,3},{3,2},{4,5},{5,4},{6,7},{7,6},{8,9},{9,8},{10,11... | collective-permute-start | bytes 196616 | tf_op jit(solution)/shard_map/ppermute | solution.py:548
  44.2 2.1 %shard_map.179 = (bf16[4,512,256]{2,1,0:T(8,128)(2,1)S(1)}, bf16[4,512,256]{2,1,0:T(8,128)(2,1)S(1)}, f32[4,512,256]{2,1,0:T(8,128)S(1)}, f32[512,128]{1,0:T(8,128)S(1)}) custom-call(f32[4,4]{1,0:T(4,128)S(1)} %copy-done.3, bf16[4,512,256]{2,1,0:T(8,128)(2,1)S(1)} %bitcast.18, bf16[4,256,256]{2,1,0:T(8,128)(2,1)S(1)} %get-tuple-element.62.refs_17_.turn.refs_16_, ...), custom_call_target="tpu_custom_call" | custom-call | flops 4294967296 | bytes 16777216 | tf_op jit(solution)/shard_map/pallas_call | solution.py:61
  46.3 0.8 shard_map.178.refs_20_.kp
  47.1 4.8 %shard_map.180 = (f32[4,512,256]{2,1,0:T(8,128)}, f32[4,512,256]{2,1,0:T(8,128)}, f32[512,128]{1,0:T(8,128)}, f32[512,128]{1,0:T(8,128)}, f32[520,256]{1,0:T(8,1...) custom-call(f32[4,4]{1,0:T(4,128)S(1)} %copy-done.3, f32[4]{0:T(128)S(1)} %copy-done.5, ...), custom_call_target="tpu_custom_call" | custom-call | flops 1073741824 | bytes 16777216 | tf_op jit(solution)/shard_map/pallas_call | solution.py:61
  53.0 1.1 %collective-permute-done.9.got = f32[520,256]{1,0:T(8,128)S(1)} collective-permute-done((f32[520,256]{1,0:T(8,128)S(1)}, f32[520,256]{1,0:T(8,128)S(1)}, u32[]{:S(2)}, u32[]{:S(2)}) %collective-permute-start.9) | collective-permute-done | bytes 532512 | tf_op jit(solution)/shard_map/ppermute | solution.py:676
  54.1 0.9 shard_map.182
  55.0 8.9 %all-to-all-start.1 = ((f32[64,1,2176]{2,1,0:T(1,128)}), f32[64,1,2176]{2,1,0:T(1,128)S(1)}, u32[]{:S(2)}, u32[]{:S(2)}) async-start(f32[64,1,2176]{2,1,0:T(1,128)} %bitcast.10), calls=%async_computation.1 | async-start | bytes 1114112 | tf_op jit(solution)/shard_map/all_to_all | solution.py:681
  63.8 7.0 %shard_map.184 = f32[4,512,256]{2,1,0:T(8,128)} custom-call(f32[4,4]{1,0:T(4,128)S(1)} %copy-done.3, f32[4]{0:T(128)S(1)} %copy-done.5, bf16[4,512,256]{2,1,0:T(8,128)(2,1)} %bitcast.17, f32[4,512,256]{2,1,0:T(8,128)} %get-tuple-element.82.m_in, f32[4,512,256]{2,1,0:T(8,128)} %get-tuple-element.83.ge_in, f32[512,128]{1,0:T(8,128)} %get-tuple-element.84.q_in, ...), custom_call_target="tpu_custom_call" | custom-call | flops 1073741824 | bytes 12582912 | tf_op jit(solution)/shard_map/pallas_call | solution.py:662
  70.9 5.4 %all-to-all-done.1 = f32[64,1,2176]{2,1,0:T(1,128)S(1)} async-done(((f32[64,1,2176]{2,1,0:T(1,128)}), f32[64,1,2176]{2,1,0:T(1,128)S(1)}, u32[]{:S(2)}, u32[]{:S(2)}) %all-to-all-start.1) | async-done | bytes 557088 | tf_op jit(solution)/shard_map/all_to_all | solution.py:681
  76.4 15.5 %all_to_all.22 = f32[64,8,256]{2,1,0:T(8,128)S(1)} all-to-all(f32[64,8,256]{2,1,0:T(8,128)S(1)} %get-tuple-element.87), channel_id=1, replica_groups=mesh['zl'=2,'x'=4,'c'=2,'y'=4,'zh'=2] {'zl','x','y','zh'}, dimensions={0} | all-to-all | bytes 1048576 | tf_op jit(solution)/shard_map/all_to_all | solution.py:685
  91.9 3.4 %collective-permute-start.10 = (f32[512,256]{1,0:T(8,128)S(1)}, f32[512,256]{1,0:T(8,128)S(1)}, u32[]{:S(2)}, u32[]{:S(2)}) collective-permute-start(f32[512,256]{1,0:T(8,128)S(1)} %bitcast.21), channel_id=1, source_target_pairs={{0,8},{8,0},{1,9},{9,1},{2,10},{10,2},{3,11},{11,3},{4,12},{12,4},... | collective-permute-start | bytes 1572872 | tf_op jit(solution)/shard_map/ppermute | solution.py:686
  95.8 1.0 %collective-permute-done.10.got = f32[512,256]{1,0:T(8,128)S(1)} collective-permute-done((f32[512,256]{1,0:T(8,128)S(1)}, f32[512,256]{1,0:T(8,128)S(1)}, u32[]{:S(2)}, u32[]{:S(2)}) %collective-permute-start.10) | collective-permute-done | bytes 524320 | tf_op jit(solution)/shard_map/ppermute | solution.py:686
  96.8 1.0 %shard_map.185 = f32[4,256,256]{2,1,0:T(8,128)} custom-call(f32[512,256]{1,0:T(8,128)S(1)} %bitcast.22, f32[512,256]{1,0:T(8,128)S(1)} %collective-permute-done.10.got), custom_call_target="tpu_custom_call" | custom-call | bytes 2097152 | tf_op jit(solution)/shard_map/pallas_call | solution.py:61
  (37 shorter events, 2.1 us)
Async XLA Ops:
  0.6 25.5 %copy-start.4 = (s32[16,32]{1,0:T(8,128)S(1)}, s32[16,32]{1,0:T(8,128)}, u32[]{:S(2)}) copy-start(s32[16,32]{1,0:T(8,128)} %refs_8_.1) | copy-start | bytes 6148
  0.6 25.5 %copy-start.8 = (f32[256]{0:T(256)S(1)}, f32[256]{0:T(256)}, u32[]{:S(2)}) copy-start(f32[256]{0:T(256)} %param.30) | copy-start | bytes 3076
  0.7 25.5 %copy-start.10 = (f32[64]{0:T(128)S(1)}, f32[64]{0:T(128)}, u32[]{:S(2)}) copy-start(f32[64]{0:T(128)} %param.24) | copy-start | bytes 772
  0.7 25.4 %copy-start.9 = (s32[16,32]{1,0:T(8,128)S(1)}, s32[16,32]{1,0:T(8,128)}, u32[]{:S(2)}) copy-start(s32[16,32]{1,0:T(8,128)} %refs_9_.1) | copy-start | bytes 6148
  0.7 25.4 %copy-start.1 = (bf16[4,256,256]{2,1,0:T(8,128)(2,1)S(1)}, bf16[4,256,256]{2,1,0:T(8,128)(2,1)}, u32[]{:S(2)}) copy-start(bf16[4,256,256]{2,1,0:T(8,128)(2,1)} %ker.1) | copy-start | bytes 1572868
  0.7 25.4 %copy-start.3 = (f32[4,4]{1,0:T(4,128)S(1)}, f32[4,4]{1,0:T(4,128)}, u32[]{:S(2)}) copy-start(f32[4,4]{1,0:T(4,128)} %mix.3) | copy-start | bytes 196
  0.7 25.4 %copy-start.5 = (f32[4]{0:T(128)S(1)}, f32[4]{0:T(128)}, u32[]{:S(2)}) copy-start(f32[4]{0:T(128)} %assim.1) | copy-start | bytes 52
  0.7 25.4 %copy-start.6 = (f32[4,256]{1,0:T(4,128)S(1)}, f32[4,256]{1,0:T(4,128)}, u32[]{:S(2)}) copy-start(f32[4,256]{1,0:T(4,128)} %mort.1) | copy-start | bytes 12292
  0.7 25.4 %copy-start.2 = (f32[4,256]{1,0:T(4,128)S(1)}, f32[4,256]{1,0:T(4,128)}, u32[]{:S(2)}) copy-start(f32[4,256]{1,0:T(4,128)} %sel.3) | copy-start | bytes 12292
  3.7 21.7 %all-to-all-start = ((f32[64,1,128]{2,1,0:T(1,128)}), f32[64,1,128]{2,1,0:T(1,128)S(1)}, u32[]{:S(2)}, u32[]{:S(2)}) async-start(f32[64,1,128]{2,1,0:T(1,128)} %bitcast.3), calls=%async_computation | async-start | bytes 65536 | tf_op jit(solution)/shard_map/all_to_all | solution.py:590
  15.7 14.9 %collective-permute-start.2 = (f32[5,32,256]{2,1,0:T(8,128)S(1)}, f32[5,32,256]{2,1,0:T(8,128)S(1)}, u32[]{:S(2)}, u32[]{:S(2)}) collective-permute-start(f32[5,32,256]{2,1,0:T(8,128)S(1)} %get-tuple-element.52), channel_id=1, source_target_pairs={{0,120},{8,16},{16,8},{24,32},{32,24},{40,48},{48,40},{56,64},{64,... | collective-permute-start | bytes 491528 | tf_op jit(solution)/shard_map/ppermute | solution.py:549
  17.9 12.7 %collective-permute-start.3 = (f32[5,32,256]{2,1,0:T(8,128)S(1)}, f32[5,32,256]{2,1,0:T(8,128)S(1)}, u32[]{:S(2)}, u32[]{:S(2)}) collective-permute-start(f32[5,32,256]{2,1,0:T(8,128)S(1)} %get-tuple-element.53), channel_id=1, source_target_pairs={{0,8},{8,0},{16,24},{24,16},{32,40},{40,32},{48,56},{56,48},{64,72... | collective-permute-start | bytes 491528 | tf_op jit(solution)/shard_map/ppermute | solution.py:550
  19.5 11.0 %collective-permute-start = (f32[5,16,256]{2,1,0:T(8,128)S(1)}, f32[5,16,256]{2,1,0:T(8,128)S(1)}, u32[]{:S(2)}, u32[]{:S(2)}) collective-permute-start(f32[5,16,256]{2,1,0:T(8,128)S(1)} %get-tuple-element.50), channel_id=1, source_target_pairs={{1,2},{2,1},{3,4},{4,3},{5,6},{6,5},{9,10},{10,9},{11,12},{12,11},... | collective-permute-start | bytes 245768 | tf_op jit(solution)/shard_map/ppermute | solution.py:547
  20.2 10.4 %collective-permute-start.1 = (f32[5,16,256]{2,1,0:T(8,128)S(1)}, f32[5,16,256]{2,1,0:T(8,128)S(1)}, u32[]{:S(2)}, u32[]{:S(2)}) collective-permute-start(f32[5,16,256]{2,1,0:T(8,128)S(1)} %get-tuple-element.51), channel_id=1, source_target_pairs={{0,1},{1,0},{2,3},{3,2},{4,5},{5,4},{6,7},{7,6},{8,9},{9,8},{10,11... | collective-permute-start | bytes 245768 | tf_op jit(solution)/shard_map/ppermute | solution.py:548
  25.4 5.2 %collective-permute-start.4 = (f32[64,128]{1,0:T(8,128)S(1)}, f32[64,128]{1,0:T(8,128)S(1)}, u32[]{:S(2)}, u32[]{:S(2)}) collective-permute-start(f32[64,128]{1,0:T(8,128)S(1)} %bitcast.23), channel_id=1, source_target_pairs={{0,8},{8,0},{1,9},{9,1},{2,10},{10,2},{3,11},{11,3},{4,12},{12,4},... | collective-permute-start | bytes 98312 | tf_op jit(solution)/shard_map/ppermute | solution.py:592
  26.2 4.4 %copy-start.7 = (f32[256]{0:T(256)S(1)}, f32[256]{0:T(256)}, u32[]{:S(2)}) copy-start(f32[256]{0:T(256)} %param.31) | copy-start | bytes 3076
  30.6 13.6 %copy-start = (bf16[4,16,32,256]{3,2,1,0:T(8,128)(2,1)S(1)}, bf16[4,16,32,256]{3,2,1,0:T(8,128)(2,1)}, u32[]{:S(2)}) copy-start(bf16[4,16,32,256]{3,2,1,0:T(8,128)(2,1)} %param.17) | copy-start | bytes 3145732
  36.6 10.5 %collective-permute-start.7 = (f32[4,32,256]{2,1,0:T(8,128)S(1)}, f32[4,32,256]{2,1,0:T(8,128)S(1)}, u32[]{:S(2)}, u32[]{:S(2)}) collective-permute-start(f32[4,32,256]{2,1,0:T(8,128)S(1)} %get-tuple-element.70), channel_id=1, source_target_pairs={{0,120},{8,16},{16,8},{24,32},{32,24},{40,48},{48,40},{56,64},{64,... | collective-permute-start | bytes 393224 | tf_op jit(solution)/shard_map/ppermute | solution.py:549
  36.9 10.2 %collective-permute-start.8 = (f32[4,32,256]{2,1,0:T(8,128)S(1)}, f32[4,32,256]{2,1,0:T(8,128)S(1)}, u32[]{:S(2)}, u32[]{:S(2)}) collective-permute-start(f32[4,32,256]{2,1,0:T(8,128)S(1)} %get-tuple-element.71), channel_id=1, source_target_pairs={{0,8},{8,0},{16,24},{24,16},{32,40},{40,32},{48,56},{56,48},{64,72... | collective-permute-start | bytes 393224 | tf_op jit(solution)/shard_map/ppermute | solution.py:550
  38.2 8.9 %collective-permute-start.5 = (f32[4,16,256]{2,1,0:T(8,128)S(1)}, f32[4,16,256]{2,1,0:T(8,128)S(1)}, u32[]{:S(2)}, u32[]{:S(2)}) collective-permute-start(f32[4,16,256]{2,1,0:T(8,128)S(1)} %get-tuple-element.68), channel_id=1, source_target_pairs={{1,2},{2,1},{3,4},{4,3},{5,6},{6,5},{9,10},{10,9},{11,12},{12,11},... | collective-permute-start | bytes 196616 | tf_op jit(solution)/shard_map/ppermute | solution.py:547
  38.9 8.2 %collective-permute-start.6 = (f32[4,16,256]{2,1,0:T(8,128)S(1)}, f32[4,16,256]{2,1,0:T(8,128)S(1)}, u32[]{:S(2)}, u32[]{:S(2)}) collective-permute-start(f32[4,16,256]{2,1,0:T(8,128)S(1)} %get-tuple-element.69), channel_id=1, source_target_pairs={{0,1},{1,0},{2,3},{3,2},{4,5},{5,4},{6,7},{7,6},{8,9},{9,8},{10,11... | collective-permute-start | bytes 196616 | tf_op jit(solution)/shard_map/ppermute | solution.py:548
  51.9 2.2 %collective-permute-start.9 = (f32[520,256]{1,0:T(8,128)S(1)}, f32[520,256]{1,0:T(8,128)S(1)}, u32[]{:S(2)}, u32[]{:S(2)}) collective-permute-start(f32[520,256]{1,0:T(8,128)S(1)} %get-tuple-element.80.send), channel_id=1, source_target_pairs={{0,8},{8,0},{1,9},{9,1},{2,10},{10,2},{3,11},{11,3},{4,12},{12,4},... | collective-permute-start | bytes 1597448 | tf_op jit(solution)/shard_map/ppermute | solution.py:676
  55.0 21.4 %all-to-all-start.1 = ((f32[64,1,2176]{2,1,0:T(1,128)}), f32[64,1,2176]{2,1,0:T(1,128)S(1)}, u32[]{:S(2)}, u32[]{:S(2)}) async-start(f32[64,1,2176]{2,1,0:T(1,128)} %bitcast.10), calls=%async_computation.1 | async-start | bytes 1114112 | tf_op jit(solution)/shard_map/all_to_all | solution.py:681
  91.9 4.9 %collective-permute-start.10 = (f32[512,256]{1,0:T(8,128)S(1)}, f32[512,256]{1,0:T(8,128)S(1)}, u32[]{:S(2)}, u32[]{:S(2)}) collective-permute-start(f32[512,256]{1,0:T(8,128)S(1)} %bitcast.21), channel_id=1, source_target_pairs={{0,8},{8,0},{1,9},{9,1},{2,10},{10,2},{3,11},{11,3},{4,12},{12,4},... | collective-permute-start | bytes 1572872 | tf_op jit(solution)/shard_map/ppermute | solution.py:686

commit v5 on v4

--- a/solution.py
+++ b/solution.py
@@ -44,7 +44,7 @@
     return pl.BlockSpec(memory_space=pltpu.SMEM)
 
 
-def call(body, outs, ins, scratch=(), flops=0, nbytes=0, vmem=6, place=True, far=(), out_far=0):
+def call(body, outs, ins, scratch=(), flops=0, nbytes=0, vmem=6, place=True, far=(), out_far=0, aliases={}):
     many = isinstance(outs, list)
     spots = [pl.BlockSpec(memory_space=pl.ANY) if n < out_far else vm() for n in range(len(outs) if many else 1)]
     run = pl.pallas_call(
@@ -53,6 +53,7 @@
         in_specs=ins,
         out_specs=spots if many else vm(),
         scratch_shapes=list(scratch),
+        input_output_aliases=aliases,
         compiler_params=pltpu.CompilerParams(vmem_limit_bytes=vmem * MIB),
         cost_estimate=pl.CostEstimate(flops=flops, bytes_accessed=nbytes, transcendentals=0),
     )
@@ -142,8 +143,7 @@
     r_row = few[1:3] + few[3:5] + few[5:7]
     entry = (lax.broadcasted_iota(jnp.int32, (1, ne), 1) // rows).astype(F32)
     vals = jnp.where(entry < n_row, r_row, 0.0)
-    lon = i_row // CI
-    owner = (lon % 2) * NCHIP + (lon // 2) * 8 + j_row // CJ
+    owner = (i_row // CI) * 8 + j_row // CJ
     mine = lax.broadcasted_iota(jnp.int32, (devices, ne), 0) == owner
     mine_b = mine.astype(F32).astype(BF16)
     before = (
@@ -162,8 +162,7 @@
         put.append(jnp.zeros((128 - SLOTS * len(parts), ne), F32))
         return jnp.concatenate(put, axis=0).astype(BF16)
 
-    sorted_ = nt(mine_b, rows_of((h0, h1, a_row))) + nt(mine_b, rows_of((l0, l1, b_row)))
-    pay[...] = jnp.concatenate([sorted_[:NCHIP, :64], sorted_[NCHIP:, :64]], axis=1)
+    pay[...] = nt(mine_b, rows_of((h0, h1, a_row))) + nt(mine_b, rows_of((l0, l1, b_row)))
 
     oc = ocean[...].astype(F32)
     edge_i = (column(oc[CI - 1 : CI, :], CJ, Z), column(oc[0:1, :], CJ, Z))
@@ -209,12 +208,9 @@
         ecol[rows] = jnp.broadcast_to(jnp.sum(here * eff, axis=1, keepdims=True), (CJ, 128))
 
 
-def gather_catch(own, other, hot, hi, lo):
-    core = lax.axis_index("c")
-    both = jnp.concatenate([own[...], other[...]], axis=0)
-    flip = both.T
-    flip = jnp.where(core == 0, flip[:64], flip[64:])
-    got = jnp.where(core == 0, both[:, :64], both[:, 64:])
+def gather_catch(pay, hot, hi, lo):
+    got = pay[...]
+    flip = got.T
     for k in range(SLOTS):
         where = flip[2 * SLOTS + k : 2 * SLOTS + k + 1, :].astype(jnp.int32)
         cell = lax.broadcasted_iota(jnp.int32, (N, 128), 0)
@@ -370,11 +366,11 @@
 
 
 def adj_body(*refs):
-    mix, assim, c, tb, ta, lb, la, ocol, ecol, own, other, gs, zone, st, feed, gain, ker, turn, sel, wt, spr = refs[:21]
-    c_out, grm, genc, eff, near, later, ola, olb, ota, otb, opad, pad, m_scr, t_scr, y, catch, hot, hi, lo = refs[21:]
+    mix, assim, c, tb, ta, lb, la, ocol, ecol, pay, gs, zone, st, feed, gain, ker, turn, sel, wt, spr = refs[:20]
+    c_out, grm, genc, eff, near, later, ola, olb, ota, otb, opad, pad, m_scr, t_scr, y, catch, hot, hi, lo = refs[20:]
     par_i, par_j = lax.axis_index("c"), lax.axis_index("zh")
     fill(pad, opad, c, la, lb, ta, tb, ocol)
-    caught = gather_catch(own, other, hot, hi, lo)
+    caught = gather_catch(pay, hot, hi, lo)
     later[...] = caught[:, :128]
     catch[...] = caught[:, 128:]
     for n in range(CHUNKS):
@@ -528,19 +524,23 @@
         out[p] = both
 
 
-def join_body(own, got, out, sem):
-    core = lax.axis_index("c")
+def place_half(half, src, out, sem):
     copies = []
-    for n, (half, src) in enumerate(((core, own), (1 - core, got))):
-        for s in range(2):
-            copies.append(
-                pltpu.make_async_copy(
-                    src.at[s * Z : (s + 1) * Z, :], out.at[2 * half + s], sem.at[2 * n + s]
-                )
-            )
-            copies[-1].start()
+    for s in range(2):
+        copies.append(
+            pltpu.make_async_copy(src.at[s * Z : (s + 1) * Z, :], out.at[2 * half + s], sem.at[s])
+        )
+        copies[-1].start()
     for copy in copies:
         copy.wait()
+
+
+def own_body(own, out, sem):
+    place_half(lax.axis_index("c"), own, out, sem)
+
+
+def other_body(got, _, out, sem):
+    place_half(1 - lax.axis_index("c"), got, out, sem)
 
 
 def exchange(la, lb, ta, tb):
@@ -575,7 +575,7 @@
     rims = [vmem((G + 1, CJ, Z))] * 2 + [vmem((G + 1, CI, Z))] * 2
     *rim, pay = call(
         prep_body,
-        rims + [vmem((NCHIP, 128))],
+        rims + [vmem((2 * NCHIP, 128))],
         [any_] + [vm()] * 4,
         [
             pltpu.VMEM((2, G, CJ, Z), F32),
@@ -587,9 +587,8 @@
         place=False,
     )(final_cotangent, ocean_mask, row_cells.T, row_count.reshape(1, -1), residuals)
     rim = exchange(*rim)
-    own = lax.all_to_all(pay, CHIPS, 0, 0, tiled=True)
-    own, middle = lax.optimization_barrier((own, saved_middle))
-    other = lax.ppermute(own, "c", CORE)
+    pay = lax.all_to_all(pay, ALL, 0, 0, tiled=True)
+    pay, middle = lax.optimization_barrier((pay, saved_middle))
 
     ocol, ecol, zone, turn, st, prey, eaten, feed, gs, gain, cot = call(
         first_body,
@@ -615,7 +614,7 @@
         + [vmem((8, 128)), vmem((N, 128)), vmem((N, 128))]
         + [vmem((G, CJ, Z))] * 2
         + [vmem((G, CI, Z))] * 2,
-        [sm(), sm()] + [vm()] * 19,
+        [sm(), sm()] + [vm()] * 18,
         [pltpu.VMEM((CI + 2, CJ + 16, 128), F32), pads]
         + [pltpu.VMEM(field, F32)] * 2
         + [pltpu.VMEM((N, 128), F32)] * 2
@@ -625,7 +624,7 @@
         nbytes=16 * MIB,
         vmem=16,
     )(
-        *(mix, assim, cot, *reversed(rim), ocol, ecol, own, other, gs, zone, st, feed, gain),
+        *(mix, assim, cot, *reversed(rim), ocol, ecol, pay, gs, zone, st, feed, gain),
         *(kernel, turn, select, wt, spr),
     )
     rim = exchange(*rim)
@@ -684,14 +683,12 @@
     own, cot = lax.optimization_barrier((own, cot))
     own = lax.all_to_all(own, CHIPS, 0, 0, tiled=True).reshape(2 * Z, Z)
     got = lax.ppermute(own, "c", CORE)
+    whole = [pltpu.HBM((G, Z, Z), F32)]
+    sems = [pltpu.SemaphoreType.DMA((2,))]
+    total = call(own_body, whole, [vm()], sems, nbytes=MIB, out_far=1)(own)[0]
     total = call(
-        join_body,
-        [pltpu.HBM((G, Z, Z), F32)],
-        [vm()] * 2,
-        [pltpu.SemaphoreType.DMA((4,))],
-        nbytes=2 * MIB,
-        out_far=1,
-    )(own, got)[0]
+        other_body, whole, [vm(), any_], sems, nbytes=MIB, out_far=1, far=(1,), aliases={1: 0}
+    )(got, total)[0]
     return cot, total, eff[0, :EEZS]
 
 

time: 98.3 us -> 98.5 us (level)
    all_to_all x1, starting transfers between devices: 8.88 us -> 10.3 us  [body(): lax.all_to_all(chunks.reshape(NCHIP, 1, CH * 128), CHIPS, 0, 0, tiled=True)]
    pallas_call x10 -> x11, Pallas kernels: 23.4 us -> 23.9 us  [go(): run(*[in_hbm(a) if not place or n in far else near_core(a) if a.size >= 8...]
  transfers between devices with their start and end apart: 13 -> 12, of which waited for: 3 -> 3; matrix products, arithmetic and copies ran while one was open for 1% -> 1% of each run, Pallas kernels for 15% -> 16%
where the time goes in v5:
time: 98.5 us; the launch traced here: 98.1 us
  starting transfers between devices  43.3 us (44%)
  Pallas kernels  30.9 us (31%)
  blocking collectives  15.5 us (16%)
  waiting for transfers between devices  6.72 us (7%)
  between operations  1.11 us (1%)
    pallas_call x11, Pallas kernels, go(): run(*[in_hbm(a) if not place or n in far else near_core(a) if a.size >= 8...  23.9 us
    all_to_all x1, blocking collectives, body(): own = lax.all_to_all(own, CHIPS, 0, 0, tiled=True).reshape(2 * Z, Z)  15.5 us
    all_to_all x1, starting transfers between devices, body(): pay = lax.all_to_all(pay, ALL, 0, 0, tiled=True)  11.5 us
    ppermute x2, starting transfers between devices, exchange(): ta = lax.ppermute(ta, LAT, LAT_A)  11 us
    all_to_all x1, starting transfers between devices, body(): lax.all_to_all(chunks.reshape(NCHIP, 1, CH * 128), CHIPS, 0, 0, tiled=True)  10.3 us
    pallas_call x1, Pallas kernels, body(): pl.pallas_call(rest_body, grid=(CHUNKS,), out_shape=sds(field), in_specs=...  7.03 us
    all_to_all x1, waiting for transfers between devices, body(): lax.all_to_all(chunks.reshape(NCHIP, 1, CH * 128), CHIPS, 0, 0, tiled=True)  5.43 us
    ppermute x1, starting transfers between devices, body(): got = lax.ppermute(own, 'c', CORE)  3.36 us
  transfers between devices with their start and end apart: 12, of which 3 were waited for; matrix products, arithmetic and copies ran while one was open for 1% of the time, Pallas kernels for 16%

profile of v5, /device:TPU:1, one launch (start us, length us, event | category | flops | bytes accessed | tf_op | source)
XLA Modules:
  0.0 98.1 jit_solution(897552726362312556)
XLA Ops:
  0.7 3.0 %shard_map.175 = (f32[5,32,256]{2,1,0:T(8,128)S(1)}, f32[5,32,256]{2,1,0:T(8,128)S(1)}, f32[5,16,256]{2,1,0:T(8,128)S(1)}, f32[5,16,256]{2,1,0:T(8,128)S(1)}, f32[128,128]{1,0:T(8,128)}) custom-call(f32[4,16,32,256]{3,2,1,0:T(8,128)} %refs_3_.1, s32[16,32]{1,0:T(8,128)} %refs_8_.1, s32[16,32]{1,0:T(8,128)} %bitcast.32, s32[1,32]{1,0:T(1,128)} %bitcast.33, ...), custom_call_target="tpu_custom_call" | custom-call | flops 134217728 | bytes 3145728 | tf_op jit(solution)/shard_map/pallas_call | solution.py:62
  3.7 11.5 %all-to-all-start = ((f32[128,1,128]{2,1,0:T(1,128)}), f32[128,1,128]{2,1,0:T(1,128)S(1)}, u32[]{:S(2)}, u32[]{:S(2)}) async-start(f32[128,1,128]{2,1,0:T(1,128)} %bitcast.3), calls=%async_computation | async-start | bytes 131072 | tf_op jit(solution)/shard_map/all_to_all | solution.py:590
  15.2 1.7 %collective-permute-start.2 = (f32[5,32,256]{2,1,0:T(8,128)S(1)}, f32[5,32,256]{2,1,0:T(8,128)S(1)}, u32[]{:S(2)}, u32[]{:S(2)}) collective-permute-start(f32[5,32,256]{2,1,0:T(8,128)S(1)} %get-tuple-element.52), channel_id=1, source_target_pairs={{0,120},{8,16},{16,8},{24,32},{32,24},{40,48},{48,40},{56,64},{64,... | collective-permute-start | bytes 491528 | tf_op jit(solution)/shard_map/ppermute | solution.py:549
  16.9 2.4 %collective-permute-start.3 = (f32[5,32,256]{2,1,0:T(8,128)S(1)}, f32[5,32,256]{2,1,0:T(8,128)S(1)}, u32[]{:S(2)}, u32[]{:S(2)}) collective-permute-start(f32[5,32,256]{2,1,0:T(8,128)S(1)} %get-tuple-element.53), channel_id=1, source_target_pairs={{0,8},{8,0},{16,24},{24,16},{32,40},{40,32},{48,56},{56,48},{64,72... | collective-permute-start | bytes 491528 | tf_op jit(solution)/shard_map/ppermute | solution.py:550
  19.3 0.7 collective-permute-start
  20.0 5.3 %collective-permute-start.1 = (f32[5,16,256]{2,1,0:T(8,128)S(1)}, f32[5,16,256]{2,1,0:T(8,128)S(1)}, u32[]{:S(2)}, u32[]{:S(2)}) collective-permute-start(f32[5,16,256]{2,1,0:T(8,128)S(1)} %get-tuple-element.51), channel_id=1, source_target_pairs={{0,1},{1,0},{2,3},{3,2},{4,5},{5,4},{6,7},{7,6},{8,9},{9,8},{10,11... | collective-permute-start | bytes 245768 | tf_op jit(solution)/shard_map/ppermute | solution.py:548
  25.4 4.3 %shard_map.176 = (f32[512,128]{1,0:T(8,128)S(1)}, f32[512,128]{1,0:T(8,128)S(1)}, bf16[512,128]{1,0:T(8,128)(2,1)S(1)}, bf16[4,256,256]{2,1,0:T(8,128)(2,1)S(1)}...) custom-call(f32[4,4]{1,0:T(4,128)S(1)} %copy-done.3, ...), custom_call_target="tpu_custom_call" | custom-call | flops 4294967296 | bytes 16777216 | tf_op jit(solution)/shard_map/pallas_call | solution.py:62
  29.8 5.9 %shard_map.177 = (f32[4,16,32,256]{3,2,1,0:T(8,128)S(1)}, bf16[4,512,256]{2,1,0:T(8,128)(2,1)S(1)}, bf16[4,512,256]{2,1,0:T(8,128)(2,1)S(1)}, f32[8,128]{1,0:T(8...) custom-call(f32[4,4]{1,0:T(4,128)S(1)} %copy-done.3, ...), custom_call_target="tpu_custom_call" | custom-call | flops 1073741824 | bytes 16777216 | tf_op jit(solution)/shard_map/pallas_call | solution.py:62
  35.7 0.6 collective-permute-start.6
  36.8 0.7 collective-permute-start.4
  37.4 5.8 %collective-permute-start.5 = (f32[4,16,256]{2,1,0:T(8,128)S(1)}, f32[4,16,256]{2,1,0:T(8,128)S(1)}, u32[]{:S(2)}, u32[]{:S(2)}) collective-permute-start(f32[4,16,256]{2,1,0:T(8,128)S(1)} %get-tuple-element.69), channel_id=1, source_target_pairs={{0,1},{1,0},{2,3},{3,2},{4,5},{5,4},{6,7},{7,6},{8,9},{9,8},{10,11... | collective-permute-start | bytes 196616 | tf_op jit(solution)/shard_map/ppermute | solution.py:548
  43.2 2.1 %shard_map.179 = (bf16[4,512,256]{2,1,0:T(8,128)(2,1)S(1)}, bf16[4,512,256]{2,1,0:T(8,128)(2,1)S(1)}, f32[4,512,256]{2,1,0:T(8,128)S(1)}, f32[512,128]{1,0:T(8,128)S(1)}) custom-call(f32[4,4]{1,0:T(4,128)S(1)} %copy-done.3, bf16[4,512,256]{2,1,0:T(8,128)(2,1)S(1)} %bitcast.18, bf16[4,256,256]{2,1,0:T(8,128)(2,1)S(1)} %get-tuple-element.62.refs_16_.turn, ...), custom_call_target="tpu_custom_call" | custom-call | flops 4294967296 | bytes 16777216 | tf_op jit(solution)/shard_map/pallas_call | solution.py:62
  45.2 0.8 shard_map.178.refs_20_.kp
  46.1 4.7 %shard_map.180 = (f32[4,512,256]{2,1,0:T(8,128)}, f32[4,512,256]{2,1,0:T(8,128)}, f32[512,128]{1,0:T(8,128)}, f32[512,128]{1,0:T(8,128)}, f32[520,256]{1,0:T(8,1...) custom-call(f32[4,4]{1,0:T(4,128)S(1)} %copy-done.3, f32[4]{0:T(128)S(1)} %copy-done.5, ...), custom_call_target="tpu_custom_call" | custom-call | flops 1073741824 | bytes 16777216 | tf_op jit(solution)/shard_map/pallas_call | solution.py:62
  50.8 0.6 collective-permute-start.8
  51.9 1.1 %collective-permute-done.8.got = f32[520,256]{1,0:T(8,128)S(1)} collective-permute-done((f32[520,256]{1,0:T(8,128)S(1)}, f32[520,256]{1,0:T(8,128)S(1)}, u32[]{:S(2)}, u32[]{:S(2)}) %collective-permute-start.8) | collective-permute-done | bytes 532512 | tf_op jit(solution)/shard_map/ppermute | solution.py:675
  53.0 0.9 shard_map.182
  53.9 10.3 %all-to-all-start.1 = ((f32[64,1,2176]{2,1,0:T(1,128)}), f32[64,1,2176]{2,1,0:T(1,128)S(1)}, u32[]{:S(2)}, u32[]{:S(2)}) async-start(f32[64,1,2176]{2,1,0:T(1,128)} %bitcast.10), calls=%async_computation.1 | async-start | bytes 1114112 | tf_op jit(solution)/shard_map/all_to_all | solution.py:680
  64.2 7.0 %shard_map.184 = f32[4,512,256]{2,1,0:T(8,128)} custom-call(f32[4,4]{1,0:T(4,128)S(1)} %copy-done.3, f32[4]{0:T(128)S(1)} %copy-done.5, bf16[4,512,256]{2,1,0:T(8,128)(2,1)} %bitcast.17, f32[4,512,256]{2,1,0:T(8,128)} %get-tuple-element.82.m_in, f32[4,512,256]{2,1,0:T(8,128)} %get-tuple-element.83.ge_in, f32[512,128]{1,0:T(8,128)} %get-tuple-element.84.q_in, ...), custom_call_target="tpu_custom_call" | custom-call | flops 1073741824 | bytes 12582912 | tf_op jit(solution)/shard_map/pallas_call | solution.py:661
  71.2 5.4 %all-to-all-done.1 = f32[64,1,2176]{2,1,0:T(1,128)S(1)} async-done(((f32[64,1,2176]{2,1,0:T(1,128)}), f32[64,1,2176]{2,1,0:T(1,128)S(1)}, u32[]{:S(2)}, u32[]{:S(2)}) %all-to-all-start.1) | async-done | bytes 557088 | tf_op jit(solution)/shard_map/all_to_all | solution.py:680
  76.8 15.5 %all_to_all.22 = f32[64,8,256]{2,1,0:T(8,128)S(1)} all-to-all(f32[64,8,256]{2,1,0:T(8,128)S(1)} %get-tuple-element.87), channel_id=1, replica_groups=mesh['zl'=2,'x'=4,'c'=2,'y'=4,'zh'=2] {'zl','x','y','zh'}, dimensions={0} | all-to-all | bytes 1048576 | tf_op jit(solution)/shard_map/all_to_all | solution.py:684
  92.3 3.4 %collective-permute-start.9 = (f32[512,256]{1,0:T(8,128)S(1)}, f32[512,256]{1,0:T(8,128)S(1)}, u32[]{:S(2)}, u32[]{:S(2)}) collective-permute-start(f32[512,256]{1,0:T(8,128)S(1)} %bitcast.21), channel_id=1, source_target_pairs={{0,8},{8,0},{1,9},{9,1},{2,10},{10,2},{3,11},{11,3},{4,12},{12,4},... | collective-permute-start | bytes 1572872 | tf_op jit(solution)/shard_map/ppermute | solution.py:685
  96.1 0.8 shard_map.185._
  97.2 0.8 shard_map.186
  (36 shorter events, 1.9 us)
Async XLA Ops:
  0.6 24.6 %copy-start.4 = (s32[16,32]{1,0:T(8,128)S(1)}, s32[16,32]{1,0:T(8,128)}, u32[]{:S(2)}) copy-start(s32[16,32]{1,0:T(8,128)} %refs_8_.1) | copy-start | bytes 6148
  0.6 24.6 %copy-start.8 = (f32[256]{0:T(256)S(1)}, f32[256]{0:T(256)}, u32[]{:S(2)}) copy-start(f32[256]{0:T(256)} %param.30) | copy-start | bytes 3076
  0.7 24.6 %copy-start.10 = (f32[64]{0:T(128)S(1)}, f32[64]{0:T(128)}, u32[]{:S(2)}) copy-start(f32[64]{0:T(128)} %param.24) | copy-start | bytes 772
  0.7 24.6 %copy-start.9 = (s32[16,32]{1,0:T(8,128)S(1)}, s32[16,32]{1,0:T(8,128)}, u32[]{:S(2)}) copy-start(s32[16,32]{1,0:T(8,128)} %refs_9_.1) | copy-start | bytes 6148
  0.7 24.6 %copy-start.1 = (bf16[4,256,256]{2,1,0:T(8,128)(2,1)S(1)}, bf16[4,256,256]{2,1,0:T(8,128)(2,1)}, u32[]{:S(2)}) copy-start(bf16[4,256,256]{2,1,0:T(8,128)(2,1)} %ker.1) | copy-start | bytes 1572868
  0.7 24.6 %copy-start.3 = (f32[4,4]{1,0:T(4,128)S(1)}, f32[4,4]{1,0:T(4,128)}, u32[]{:S(2)}) copy-start(f32[4,4]{1,0:T(4,128)} %mix.3) | copy-start | bytes 196
  0.7 24.6 %copy-start.5 = (f32[4]{0:T(128)S(1)}, f32[4]{0:T(128)}, u32[]{:S(2)}) copy-start(f32[4]{0:T(128)} %assim.1) | copy-start | bytes 52
  0.7 24.6 %copy-start.6 = (f32[4,256]{1,0:T(4,128)S(1)}, f32[4,256]{1,0:T(4,128)}, u32[]{:S(2)}) copy-start(f32[4,256]{1,0:T(4,128)} %mort.1) | copy-start | bytes 12292
  0.7 24.6 %copy-start.2 = (f32[4,256]{1,0:T(4,128)S(1)}, f32[4,256]{1,0:T(4,128)}, u32[]{:S(2)}) copy-start(f32[4,256]{1,0:T(4,128)} %sel.3) | copy-start | bytes 12292
  3.7 21.6 %all-to-all-start = ((f32[128,1,128]{2,1,0:T(1,128)}), f32[128,1,128]{2,1,0:T(1,128)S(1)}, u32[]{:S(2)}, u32[]{:S(2)}) async-start(f32[128,1,128]{2,1,0:T(1,128)} %bitcast.3), calls=%async_computation | async-start | bytes 131072 | tf_op jit(solution)/shard_map/all_to_all | solution.py:590
  15.2 14.5 %collective-permute-start.2 = (f32[5,32,256]{2,1,0:T(8,128)S(1)}, f32[5,32,256]{2,1,0:T(8,128)S(1)}, u32[]{:S(2)}, u32[]{:S(2)}) collective-permute-start(f32[5,32,256]{2,1,0:T(8,128)S(1)} %get-tuple-element.52), channel_id=1, source_target_pairs={{0,120},{8,16},{16,8},{24,32},{32,24},{40,48},{48,40},{56,64},{64,... | collective-permute-start | bytes 491528 | tf_op jit(solution)/shard_map/ppermute | solution.py:549
  16.9 12.8 %collective-permute-start.3 = (f32[5,32,256]{2,1,0:T(8,128)S(1)}, f32[5,32,256]{2,1,0:T(8,128)S(1)}, u32[]{:S(2)}, u32[]{:S(2)}) collective-permute-start(f32[5,32,256]{2,1,0:T(8,128)S(1)} %get-tuple-element.53), channel_id=1, source_target_pairs={{0,8},{8,0},{16,24},{24,16},{32,40},{40,32},{48,56},{56,48},{64,72... | collective-permute-start | bytes 491528 | tf_op jit(solution)/shard_map/ppermute | solution.py:550
  19.3 10.4 %collective-permute-start = (f32[5,16,256]{2,1,0:T(8,128)S(1)}, f32[5,16,256]{2,1,0:T(8,128)S(1)}, u32[]{:S(2)}, u32[]{:S(2)}) collective-permute-start(f32[5,16,256]{2,1,0:T(8,128)S(1)} %get-tuple-element.50), channel_id=1, source_target_pairs={{1,2},{2,1},{3,4},{4,3},{5,6},{6,5},{9,10},{10,9},{11,12},{12,11},... | collective-permute-start | bytes 245768 | tf_op jit(solution)/shard_map/ppermute | solution.py:547
  20.0 9.7 %collective-permute-start.1 = (f32[5,16,256]{2,1,0:T(8,128)S(1)}, f32[5,16,256]{2,1,0:T(8,128)S(1)}, u32[]{:S(2)}, u32[]{:S(2)}) collective-permute-start(f32[5,16,256]{2,1,0:T(8,128)S(1)} %get-tuple-element.51), channel_id=1, source_target_pairs={{0,1},{1,0},{2,3},{3,2},{4,5},{5,4},{6,7},{7,6},{8,9},{9,8},{10,11... | collective-permute-start | bytes 245768 | tf_op jit(solution)/shard_map/ppermute | solution.py:548
  25.3 4.4 %copy-start.7 = (f32[256]{0:T(256)S(1)}, f32[256]{0:T(256)}, u32[]{:S(2)}) copy-start(f32[256]{0:T(256)} %param.31) | copy-start | bytes 3076
  29.8 13.4 %copy-start = (bf16[4,16,32,256]{3,2,1,0:T(8,128)(2,1)S(1)}, bf16[4,16,32,256]{3,2,1,0:T(8,128)(2,1)}, u32[]{:S(2)}) copy-start(bf16[4,16,32,256]{3,2,1,0:T(8,128)(2,1)} %param.17) | copy-start | bytes 3145732
  35.7 10.3 %collective-permute-start.6 = (f32[4,32,256]{2,1,0:T(8,128)S(1)}, f32[4,32,256]{2,1,0:T(8,128)S(1)}, u32[]{:S(2)}, u32[]{:S(2)}) collective-permute-start(f32[4,32,256]{2,1,0:T(8,128)S(1)} %get-tuple-element.70), channel_id=1, source_target_pairs={{0,120},{8,16},{16,8},{24,32},{32,24},{40,48},{48,40},{56,64},{64,... | collective-permute-start | bytes 393224 | tf_op jit(solution)/shard_map/ppermute | solution.py:549
  36.3 9.8 %collective-permute-start.7 = (f32[4,32,256]{2,1,0:T(8,128)S(1)}, f32[4,32,256]{2,1,0:T(8,128)S(1)}, u32[]{:S(2)}, u32[]{:S(2)}) collective-permute-start(f32[4,32,256]{2,1,0:T(8,128)S(1)} %get-tuple-element.71), channel_id=1, source_target_pairs={{0,8},{8,0},{16,24},{24,16},{32,40},{40,32},{48,56},{56,48},{64,72... | collective-permute-start | bytes 393224 | tf_op jit(solution)/shard_map/ppermute | solution.py:550
  36.8 9.3 %collective-permute-start.4 = (f32[4,16,256]{2,1,0:T(8,128)S(1)}, f32[4,16,256]{2,1,0:T(8,128)S(1)}, u32[]{:S(2)}, u32[]{:S(2)}) collective-permute-start(f32[4,16,256]{2,1,0:T(8,128)S(1)} %get-tuple-element.68), channel_id=1, source_target_pairs={{1,2},{2,1},{3,4},{4,3},{5,6},{6,5},{9,10},{10,9},{11,12},{12,11},... | collective-permute-start | bytes 196616 | tf_op jit(solution)/shard_map/ppermute | solution.py:547
  37.4 8.6 %collective-permute-start.5 = (f32[4,16,256]{2,1,0:T(8,128)S(1)}, f32[4,16,256]{2,1,0:T(8,128)S(1)}, u32[]{:S(2)}, u32[]{:S(2)}) collective-permute-start(f32[4,16,256]{2,1,0:T(8,128)S(1)} %get-tuple-element.69), channel_id=1, source_target_pairs={{0,1},{1,0},{2,3},{3,2},{4,5},{5,4},{6,7},{7,6},{8,9},{9,8},{10,11... | collective-permute-start | bytes 196616 | tf_op jit(solution)/shard_map/ppermute | solution.py:548
  50.8 2.2 %collective-permute-start.8 = (f32[520,256]{1,0:T(8,128)S(1)}, f32[520,256]{1,0:T(8,128)S(1)}, u32[]{:S(2)}, u32[]{:S(2)}) collective-permute-start(f32[520,256]{1,0:T(8,128)S(1)} %get-tuple-element.80.send), channel_id=1, source_target_pairs={{0,8},{8,0},{1,9},{9,1},{2,10},{10,2},{3,11},{11,3},{4,12},{12,4},... | collective-permute-start | bytes 1597448 | tf_op jit(solution)/shard_map/ppermute | solution.py:675
  53.9 22.8 %all-to-all-start.1 = ((f32[64,1,2176]{2,1,0:T(1,128)}), f32[64,1,2176]{2,1,0:T(1,128)S(1)}, u32[]{:S(2)}, u32[]{:S(2)}) async-start(f32[64,1,2176]{2,1,0:T(1,128)} %bitcast.10), calls=%async_computation.1 | async-start | bytes 1114112 | tf_op jit(solution)/shard_map/all_to_all | solution.py:680
  92.3 4.9 %collective-permute-start.9 = (f32[512,256]{1,0:T(8,128)S(1)}, f32[512,256]{1,0:T(8,128)S(1)}, u32[]{:S(2)}, u32[]{:S(2)}) collective-permute-start(f32[512,256]{1,0:T(8,128)S(1)} %bitcast.21), channel_id=1, source_target_pairs={{0,8},{8,0},{1,9},{9,1},{2,10},{10,2},{3,11},{11,3},{4,12},{12,4},... | collective-permute-start | bytes 1572872 | tf_op jit(solution)/shard_map/ppermute | solution.py:685

commit v6 on v5

--- a/solution.py
+++ b/solution.py
@@ -366,7 +366,7 @@
 
 
 def adj_body(*refs):
-    mix, assim, c, tb, ta, lb, la, ocol, ecol, pay, gs, zone, st, feed, gain, ker, turn, sel, wt, spr = refs[:20]
+    mix, assim, c, la, lb, ta, tb, ocol, ecol, pay, gs, zone, st, feed, gain, ker, turn, sel, wt, spr = refs[:20]
     c_out, grm, genc, eff, near, later, ola, olb, ota, otb, opad, pad, m_scr, t_scr, y, catch, hot, hi, lo = refs[20:]
     par_i, par_j = lax.axis_index("c"), lax.axis_index("zh")
     fill(pad, opad, c, la, lb, ta, tb, ocol)
@@ -428,7 +428,7 @@
 
 
 def last_body(*refs):
-    mix, assim, c, tb, ta, lb, la, ocol, ecol, catch, gs, zone, st, prey, eaten, feed, turn, sel, spr, near, kp, eff = refs[:22]
+    mix, assim, c, la, lb, ta, tb, ocol, ecol, catch, gs, zone, st, prey, eaten, feed, turn, sel, spr, near, kp, eff = refs[:22]
     m_hbm, ge_hbm, q_hbm, e_hbm, send, grm, genc, pad, m_scr, ge_scr, y, q_scr, sem = refs[22:]
     core = lax.axis_index("c")
     fill(pad, None, c, la, lb, ta, tb, ocol)
@@ -544,11 +544,12 @@
 
 
 def exchange(la, lb, ta, tb):
-    tb = lax.ppermute(tb, LAT, LAT_B)
-    ta = lax.ppermute(ta, LAT, LAT_A)
-    lb = lax.ppermute(lb, LON, LON_B)
-    la = lax.ppermute(la, LON, LON_A)
-    return la, lb, ta, tb
+    return (
+        lax.ppermute(la, LON, LON_A),
+        lax.ppermute(lb, LON, LON_B),
+        lax.ppermute(ta, LAT, LAT_A),
+        lax.ppermute(tb, LAT, LAT_B),
+    )
 
 
 def body(
@@ -624,7 +625,7 @@
         nbytes=16 * MIB,
         vmem=16,
     )(
-        *(mix, assim, cot, *reversed(rim), ocol, ecol, pay, gs, zone, st, feed, gain),
+        *(mix, assim, cot, *rim, ocol, ecol, pay, gs, zone, st, feed, gain),
         *(kernel, turn, select, wt, spr),
     )
     rim = exchange(*rim)
@@ -652,7 +653,7 @@
         vmem=16,
         out_far=4,
     )(
-        *(mix, assim, cot, *reversed(rim), ocol, ecol, catch, gs, zone, st, prey, eaten, feed),
+        *(mix, assim, cot, *rim, ocol, ecol, catch, gs, zone, st, prey, eaten, feed),
         *(turn, select, spr, near, kp, eff),
     )
     block = pl.BlockSpec((G, R, Z), lambda n: (0, n, 0))

time: 98.5 us -> 98 us (level)
  starting transfers between devices: 43.3 us -> 38.3 us
  waiting for transfers between devices: 6.72 us -> 10.9 us
    ppermute x8, starting transfers between devices: 17.5 us -> 10.9 us  [the longest x2 6.3 us: exchange(): lax.ppermute(ta, LAT, LAT_A)]
    all_to_all x1, waiting for transfers between devices: 0.01 us -> 3.89 us  [body(): pay = lax.all_to_all(pay, ALL, 0, 0, tiled=True)]
    all_to_all x1, starting transfers between devices: 10.3 us -> 11.7 us  [body(): lax.all_to_all(chunks.reshape(NCHIP, 1, CH * 128), CHIPS, 0, 0, tiled=True)]
  transfers between devices with their start and end apart: 12 -> 12, of which waited for: 3 -> 4; matrix products, arithmetic and copies ran while one was open for 1% -> 1% of each run, Pallas kernels for 16% -> 16%
where the time goes in v6:
time: 98 us; the launch traced here: 97.6 us
  starting transfers between devices  38.3 us (39%)
  Pallas kernels  30.9 us (32%)
  blocking collectives  15.8 us (16%)
  waiting for transfers between devices  10.9 us (11%)
  between operations  1.11 us (1%)
    pallas_call x11, Pallas kernels, go(): run(*[in_hbm(a) if not place or n in far else near_core(a) if a.size >= 8...  23.9 us
    all_to_all x1, blocking collectives, body(): own = lax.all_to_all(own, CHIPS, 0, 0, tiled=True).reshape(2 * Z, Z)  15.8 us
    all_to_all x1, starting transfers between devices, body(): lax.all_to_all(chunks.reshape(NCHIP, 1, CH * 128), CHIPS, 0, 0, tiled=True)  11.7 us
    all_to_all x1, starting transfers between devices, body(): pay = lax.all_to_all(pay, ALL, 0, 0, tiled=True)  11.5 us
    pallas_call x1, Pallas kernels, body(): pl.pallas_call(rest_body, grid=(CHUNKS,), out_shape=sds(field), in_specs=...  7.03 us
    ppermute x2, starting transfers between devices, exchange(): lax.ppermute(ta, LAT, LAT_A)  6.3 us
    all_to_all x1, waiting for transfers between devices, body(): lax.all_to_all(chunks.reshape(NCHIP, 1, CH * 128), CHIPS, 0, 0, tiled=True)  5.74 us
    all_to_all x1, waiting for transfers between devices, body(): pay = lax.all_to_all(pay, ALL, 0, 0, tiled=True)  3.89 us
  transfers between devices with their start and end apart: 12, of which 4 were waited for; matrix products, arithmetic and copies ran while one was open for 1% of the time, Pallas kernels for 16%

profile of v6, /device:TPU:1, one launch (start us, length us, event | category | flops | bytes accessed | tf_op | source)
XLA Modules:
  0.0 97.6 jit_solution(5560002118319749227)
XLA Ops:
  0.7 3.0 %shard_map.175 = (f32[5,32,256]{2,1,0:T(8,128)S(1)}, f32[5,32,256]{2,1,0:T(8,128)S(1)}, f32[5,16,256]{2,1,0:T(8,128)S(1)}, f32[5,16,256]{2,1,0:T(8,128)S(1)}, f32[128,128]{1,0:T(8,128)}) custom-call(f32[4,16,32,256]{3,2,1,0:T(8,128)} %refs_3_.1, s32[16,32]{1,0:T(8,128)} %refs_8_.1, s32[16,32]{1,0:T(8,128)} %bitcast.32, s32[1,32]{1,0:T(1,128)} %bitcast.33, ...), custom_call_target="tpu_custom_call" | custom-call | flops 134217728 | bytes 3145728 | tf_op jit(solution)/shard_map/pallas_call | solution.py:62
  3.7 11.5 %all-to-all-start = ((f32[128,1,128]{2,1,0:T(1,128)}), f32[128,1,128]{2,1,0:T(1,128)S(1)}, u32[]{:S(2)}, u32[]{:S(2)}) async-start(f32[128,1,128]{2,1,0:T(1,128)} %bitcast.3), calls=%async_computation | async-start | bytes 131072 | tf_op jit(solution)/shard_map/all_to_all | solution.py:591
  15.2 1.1 %collective-permute-start = (f32[5,32,256]{2,1,0:T(8,128)S(1)}, f32[5,32,256]{2,1,0:T(8,128)S(1)}, u32[]{:S(2)}, u32[]{:S(2)}) collective-permute-start(f32[5,32,256]{2,1,0:T(8,128)S(1)} %get-tuple-element.50), channel_id=1, source_target_pairs={{0,8},{8,0},{16,24},{24,16},{32,40},{40,32},{48,56},{56,48},{64,72... | collective-permute-start | bytes 491528 | tf_op jit(solution)/shard_map/ppermute | solution.py:548
  16.4 0.7 collective-permute-start.1
  17.1 3.1 %collective-permute-start.2 = (f32[5,16,256]{2,1,0:T(8,128)S(1)}, f32[5,16,256]{2,1,0:T(8,128)S(1)}, u32[]{:S(2)}, u32[]{:S(2)}) collective-permute-start(f32[5,16,256]{2,1,0:T(8,128)S(1)} %get-tuple-element.52), channel_id=1, source_target_pairs={{0,1},{1,0},{2,3},{3,2},{4,5},{5,4},{6,7},{7,6},{8,9},{9,8},{10,11... | collective-permute-start | bytes 245768 | tf_op jit(solution)/shard_map/ppermute | solution.py:550
  20.8 3.9 %all-to-all-done = f32[128,1,128]{2,1,0:T(1,128)S(1)} async-done(((f32[128,1,128]{2,1,0:T(1,128)}), f32[128,1,128]{2,1,0:T(1,128)S(1)}, u32[]{:S(2)}, u32[]{:S(2)}) %all-to-all-start) | async-done | bytes 65568 | tf_op jit(solution)/shard_map/all_to_all | solution.py:591
  24.8 4.3 %shard_map.176 = (f32[512,128]{1,0:T(8,128)S(1)}, f32[512,128]{1,0:T(8,128)S(1)}, bf16[512,128]{1,0:T(8,128)(2,1)S(1)}, bf16[4,256,256]{2,1,0:T(8,128)(2,1)S(1)}...) custom-call(f32[4,4]{1,0:T(4,128)S(1)} %copy-done.3, ...), custom_call_target="tpu_custom_call" | custom-call | flops 4294967296 | bytes 16777216 | tf_op jit(solution)/shard_map/pallas_call | solution.py:62
  29.2 5.9 %shard_map.177 = (f32[4,16,32,256]{3,2,1,0:T(8,128)S(1)}, bf16[4,512,256]{2,1,0:T(8,128)(2,1)S(1)}, bf16[4,512,256]{2,1,0:T(8,128)(2,1)S(1)}, f32[8,128]{1,0:T(8...) custom-call(f32[4,4]{1,0:T(4,128)S(1)} %copy-done.3, ...), custom_call_target="tpu_custom_call" | custom-call | flops 1073741824 | bytes 16777216 | tf_op jit(solution)/shard_map/pallas_call | solution.py:62
  35.1 1.1 %collective-permute-start.4 = (f32[4,32,256]{2,1,0:T(8,128)S(1)}, f32[4,32,256]{2,1,0:T(8,128)S(1)}, u32[]{:S(2)}, u32[]{:S(2)}) collective-permute-start(f32[4,32,256]{2,1,0:T(8,128)S(1)} %get-tuple-element.68), channel_id=1, source_target_pairs={{0,8},{8,0},{16,24},{24,16},{32,40},{40,32},{48,56},{56,48},{64,72... | collective-permute-start | bytes 393224 | tf_op jit(solution)/shard_map/ppermute | solution.py:548
  36.4 3.2 %collective-permute-start.6 = (f32[4,16,256]{2,1,0:T(8,128)S(1)}, f32[4,16,256]{2,1,0:T(8,128)S(1)}, u32[]{:S(2)}, u32[]{:S(2)}) collective-permute-start(f32[4,16,256]{2,1,0:T(8,128)S(1)} %get-tuple-element.70), channel_id=1, source_target_pairs={{0,1},{1,0},{2,3},{3,2},{4,5},{5,4},{6,7},{7,6},{8,9},{9,8},{10,11... | collective-permute-start | bytes 196616 | tf_op jit(solution)/shard_map/ppermute | solution.py:550
  39.6 0.8 collective-permute-start.7
  40.4 2.1 %shard_map.179 = (bf16[4,512,256]{2,1,0:T(8,128)(2,1)S(1)}, bf16[4,512,256]{2,1,0:T(8,128)(2,1)S(1)}, f32[4,512,256]{2,1,0:T(8,128)S(1)}, f32[512,128]{1,0:T(8,128)S(1)}) custom-call(f32[4,4]{1,0:T(4,128)S(1)} %copy-done.3, bf16[4,512,256]{2,1,0:T(8,128)(2,1)S(1)} %bitcast.18, bf16[4,256,256]{2,1,0:T(8,128)(2,1)S(1)} %get-tuple-element.62.refs_16_.turn, ...), custom_call_target="tpu_custom_call" | custom-call | flops 4294967296 | bytes 16777216 | tf_op jit(solution)/shard_map/pallas_call | solution.py:62
  42.5 0.8 shard_map.178.refs_20_.kp
  43.3 4.7 %shard_map.180 = (f32[4,512,256]{2,1,0:T(8,128)}, f32[4,512,256]{2,1,0:T(8,128)}, f32[512,128]{1,0:T(8,128)}, f32[512,128]{1,0:T(8,128)}, f32[520,256]{1,0:T(8,1...) custom-call(f32[4,4]{1,0:T(4,128)S(1)} %copy-done.3, f32[4]{0:T(128)S(1)} %copy-done.5, ...), custom_call_target="tpu_custom_call" | custom-call | flops 1073741824 | bytes 16777216 | tf_op jit(solution)/shard_map/pallas_call | solution.py:62
  48.1 1.3 %collective-permute-start.8 = (f32[520,256]{1,0:T(8,128)S(1)}, f32[520,256]{1,0:T(8,128)S(1)}, u32[]{:S(2)}, u32[]{:S(2)}) collective-permute-start(f32[520,256]{1,0:T(8,128)S(1)} %get-tuple-element.80.send), channel_id=1, source_target_pairs={{0,8},{8,0},{1,9},{9,1},{2,10},{10,2},{3,11},{11,3},{4,12},{12,4},... | collective-permute-start | bytes 1597448 | tf_op jit(solution)/shard_map/ppermute | solution.py:676
  49.9 1.1 %collective-permute-done.8.got = f32[520,256]{1,0:T(8,128)S(1)} collective-permute-done((f32[520,256]{1,0:T(8,128)S(1)}, f32[520,256]{1,0:T(8,128)S(1)}, u32[]{:S(2)}, u32[]{:S(2)}) %collective-permute-start.8) | collective-permute-done | bytes 532512 | tf_op jit(solution)/shard_map/ppermute | solution.py:676
  50.9 0.9 shard_map.182
  51.8 11.7 %all-to-all-start.1 = ((f32[64,1,2176]{2,1,0:T(1,128)}), f32[64,1,2176]{2,1,0:T(1,128)S(1)}, u32[]{:S(2)}, u32[]{:S(2)}) async-start(f32[64,1,2176]{2,1,0:T(1,128)} %bitcast.10), calls=%async_computation.1 | async-start | bytes 1114112 | tf_op jit(solution)/shard_map/all_to_all | solution.py:681
  63.5 7.0 %shard_map.184 = f32[4,512,256]{2,1,0:T(8,128)} custom-call(f32[4,4]{1,0:T(4,128)S(1)} %copy-done.3, f32[4]{0:T(128)S(1)} %copy-done.5, bf16[4,512,256]{2,1,0:T(8,128)(2,1)} %bitcast.17, f32[4,512,256]{2,1,0:T(8,128)} %get-tuple-element.82.m_in, f32[4,512,256]{2,1,0:T(8,128)} %get-tuple-element.83.ge_in, f32[512,128]{1,0:T(8,128)} %get-tuple-element.84.q_in, ...), custom_call_target="tpu_custom_call" | custom-call | flops 1073741824 | bytes 12582912 | tf_op jit(solution)/shard_map/pallas_call | solution.py:662
  70.5 5.7 %all-to-all-done.1 = f32[64,1,2176]{2,1,0:T(1,128)S(1)} async-done(((f32[64,1,2176]{2,1,0:T(1,128)}), f32[64,1,2176]{2,1,0:T(1,128)S(1)}, u32[]{:S(2)}, u32[]{:S(2)}) %all-to-all-start.1) | async-done | bytes 557088 | tf_op jit(solution)/shard_map/all_to_all | solution.py:681
  76.4 15.8 %all_to_all.22 = f32[64,8,256]{2,1,0:T(8,128)S(1)} all-to-all(f32[64,8,256]{2,1,0:T(8,128)S(1)} %get-tuple-element.87), channel_id=1, replica_groups=mesh['zl'=2,'x'=4,'c'=2,'y'=4,'zh'=2] {'zl','x','y','zh'}, dimensions={0} | all-to-all | bytes 1048576 | tf_op jit(solution)/shard_map/all_to_all | solution.py:685
  92.1 3.0 %collective-permute-start.9 = (f32[512,256]{1,0:T(8,128)S(1)}, f32[512,256]{1,0:T(8,128)S(1)}, u32[]{:S(2)}, u32[]{:S(2)}) collective-permute-start(f32[512,256]{1,0:T(8,128)S(1)} %bitcast.21), channel_id=1, source_target_pairs={{0,8},{8,0},{1,9},{9,1},{2,10},{10,2},{3,11},{11,3},{4,12},{12,4},... | collective-permute-start | bytes 1572872 | tf_op jit(solution)/shard_map/ppermute | solution.py:686
  95.6 0.8 shard_map.185._
  96.7 0.8 shard_map.186
  (36 shorter events, 2.1 us)
Async XLA Ops:
  0.6 24.1 %copy-start.4 = (s32[16,32]{1,0:T(8,128)S(1)}, s32[16,32]{1,0:T(8,128)}, u32[]{:S(2)}) copy-start(s32[16,32]{1,0:T(8,128)} %refs_8_.1) | copy-start | bytes 6148
  0.6 24.1 %copy-start.8 = (f32[256]{0:T(256)S(1)}, f32[256]{0:T(256)}, u32[]{:S(2)}) copy-start(f32[256]{0:T(256)} %param.30) | copy-start | bytes 3076
  0.7 24.1 %copy-start.10 = (f32[64]{0:T(128)S(1)}, f32[64]{0:T(128)}, u32[]{:S(2)}) copy-start(f32[64]{0:T(128)} %param.24) | copy-start | bytes 772
  0.7 24.1 %copy-start.9 = (s32[16,32]{1,0:T(8,128)S(1)}, s32[16,32]{1,0:T(8,128)}, u32[]{:S(2)}) copy-start(s32[16,32]{1,0:T(8,128)} %refs_9_.1) | copy-start | bytes 6148
  0.7 24.1 %copy-start.1 = (bf16[4,256,256]{2,1,0:T(8,128)(2,1)S(1)}, bf16[4,256,256]{2,1,0:T(8,128)(2,1)}, u32[]{:S(2)}) copy-start(bf16[4,256,256]{2,1,0:T(8,128)(2,1)} %ker.1) | copy-start | bytes 1572868
  0.7 24.1 %copy-start.3 = (f32[4,4]{1,0:T(4,128)S(1)}, f32[4,4]{1,0:T(4,128)}, u32[]{:S(2)}) copy-start(f32[4,4]{1,0:T(4,128)} %mix.3) | copy-start | bytes 196
  0.7 24.1 %copy-start.5 = (f32[4]{0:T(128)S(1)}, f32[4]{0:T(128)}, u32[]{:S(2)}) copy-start(f32[4]{0:T(128)} %assim.1) | copy-start | bytes 52
  0.7 24.1 %copy-start.6 = (f32[4,256]{1,0:T(4,128)S(1)}, f32[4,256]{1,0:T(4,128)}, u32[]{:S(2)}) copy-start(f32[4,256]{1,0:T(4,128)} %mort.1) | copy-start | bytes 12292
  0.7 24.1 %copy-start.2 = (f32[4,256]{1,0:T(4,128)S(1)}, f32[4,256]{1,0:T(4,128)}, u32[]{:S(2)}) copy-start(f32[4,256]{1,0:T(4,128)} %sel.3) | copy-start | bytes 12292
  3.7 21.0 %all-to-all-start = ((f32[128,1,128]{2,1,0:T(1,128)}), f32[128,1,128]{2,1,0:T(1,128)S(1)}, u32[]{:S(2)}, u32[]{:S(2)}) async-start(f32[128,1,128]{2,1,0:T(1,128)} %bitcast.3), calls=%async_computation | async-start | bytes 131072 | tf_op jit(solution)/shard_map/all_to_all | solution.py:591
  15.2 14.0 %collective-permute-start = (f32[5,32,256]{2,1,0:T(8,128)S(1)}, f32[5,32,256]{2,1,0:T(8,128)S(1)}, u32[]{:S(2)}, u32[]{:S(2)}) collective-permute-start(f32[5,32,256]{2,1,0:T(8,128)S(1)} %get-tuple-element.50), channel_id=1, source_target_pairs={{0,8},{8,0},{16,24},{24,16},{32,40},{40,32},{48,56},{56,48},{64,72... | collective-permute-start | bytes 491528 | tf_op jit(solution)/shard_map/ppermute | solution.py:548
  16.4 12.8 %collective-permute-start.1 = (f32[5,32,256]{2,1,0:T(8,128)S(1)}, f32[5,32,256]{2,1,0:T(8,128)S(1)}, u32[]{:S(2)}, u32[]{:S(2)}) collective-permute-start(f32[5,32,256]{2,1,0:T(8,128)S(1)} %get-tuple-element.51), channel_id=1, source_target_pairs={{0,120},{8,16},{16,8},{24,32},{32,24},{40,48},{48,40},{56,64},{64,... | collective-permute-start | bytes 491528 | tf_op jit(solution)/shard_map/ppermute | solution.py:549
  17.1 12.1 %collective-permute-start.2 = (f32[5,16,256]{2,1,0:T(8,128)S(1)}, f32[5,16,256]{2,1,0:T(8,128)S(1)}, u32[]{:S(2)}, u32[]{:S(2)}) collective-permute-start(f32[5,16,256]{2,1,0:T(8,128)S(1)} %get-tuple-element.52), channel_id=1, source_target_pairs={{0,1},{1,0},{2,3},{3,2},{4,5},{5,4},{6,7},{7,6},{8,9},{9,8},{10,11... | collective-permute-start | bytes 245768 | tf_op jit(solution)/shard_map/ppermute | solution.py:550
  20.2 9.0 %collective-permute-start.3 = (f32[5,16,256]{2,1,0:T(8,128)S(1)}, f32[5,16,256]{2,1,0:T(8,128)S(1)}, u32[]{:S(2)}, u32[]{:S(2)}) collective-permute-start(f32[5,16,256]{2,1,0:T(8,128)S(1)} %get-tuple-element.53), channel_id=1, source_target_pairs={{1,2},{2,1},{3,4},{4,3},{5,6},{6,5},{9,10},{10,9},{11,12},{12,11},... | collective-permute-start | bytes 245768 | tf_op jit(solution)/shard_map/ppermute | solution.py:551
  24.8 4.4 %copy-start.7 = (f32[256]{0:T(256)S(1)}, f32[256]{0:T(256)}, u32[]{:S(2)}) copy-start(f32[256]{0:T(256)} %param.31) | copy-start | bytes 3076
  29.2 11.2 %copy-start = (bf16[4,16,32,256]{3,2,1,0:T(8,128)(2,1)S(1)}, bf16[4,16,32,256]{3,2,1,0:T(8,128)(2,1)}, u32[]{:S(2)}) copy-start(bf16[4,16,32,256]{3,2,1,0:T(8,128)(2,1)} %param.17) | copy-start | bytes 3145732
  35.1 8.1 %collective-permute-start.4 = (f32[4,32,256]{2,1,0:T(8,128)S(1)}, f32[4,32,256]{2,1,0:T(8,128)S(1)}, u32[]{:S(2)}, u32[]{:S(2)}) collective-permute-start(f32[4,32,256]{2,1,0:T(8,128)S(1)} %get-tuple-element.68), channel_id=1, source_target_pairs={{0,8},{8,0},{16,24},{24,16},{32,40},{40,32},{48,56},{56,48},{64,72... | collective-permute-start | bytes 393224 | tf_op jit(solution)/shard_map/ppermute | solution.py:548
  36.3 7.0 %collective-permute-start.5 = (f32[4,32,256]{2,1,0:T(8,128)S(1)}, f32[4,32,256]{2,1,0:T(8,128)S(1)}, u32[]{:S(2)}, u32[]{:S(2)}) collective-permute-start(f32[4,32,256]{2,1,0:T(8,128)S(1)} %get-tuple-element.69), channel_id=1, source_target_pairs={{0,120},{8,16},{16,8},{24,32},{32,24},{40,48},{48,40},{56,64},{64,... | collective-permute-start | bytes 393224 | tf_op jit(solution)/shard_map/ppermute | solution.py:549
  36.4 6.9 %collective-permute-start.6 = (f32[4,16,256]{2,1,0:T(8,128)S(1)}, f32[4,16,256]{2,1,0:T(8,128)S(1)}, u32[]{:S(2)}, u32[]{:S(2)}) collective-permute-start(f32[4,16,256]{2,1,0:T(8,128)S(1)} %get-tuple-element.70), channel_id=1, source_target_pairs={{0,1},{1,0},{2,3},{3,2},{4,5},{5,4},{6,7},{7,6},{8,9},{9,8},{10,11... | collective-permute-start | bytes 196616 | tf_op jit(solution)/shard_map/ppermute | solution.py:550
  39.6 3.7 %collective-permute-start.7 = (f32[4,16,256]{2,1,0:T(8,128)S(1)}, f32[4,16,256]{2,1,0:T(8,128)S(1)}, u32[]{:S(2)}, u32[]{:S(2)}) collective-permute-start(f32[4,16,256]{2,1,0:T(8,128)S(1)} %get-tuple-element.71), channel_id=1, source_target_pairs={{1,2},{2,1},{3,4},{4,3},{5,6},{6,5},{9,10},{10,9},{11,12},{12,11},... | collective-permute-start | bytes 196616 | tf_op jit(solution)/shard_map/ppermute | solution.py:551
  48.1 2.9 %collective-permute-start.8 = (f32[520,256]{1,0:T(8,128)S(1)}, f32[520,256]{1,0:T(8,128)S(1)}, u32[]{:S(2)}, u32[]{:S(2)}) collective-permute-start(f32[520,256]{1,0:T(8,128)S(1)} %get-tuple-element.80.send), channel_id=1, source_target_pairs={{0,8},{8,0},{1,9},{9,1},{2,10},{10,2},{3,11},{11,3},{4,12},{12,4},... | collective-permute-start | bytes 1597448 | tf_op jit(solution)/shard_map/ppermute | solution.py:676
  51.8 24.4 %all-to-all-start.1 = ((f32[64,1,2176]{2,1,0:T(1,128)}), f32[64,1,2176]{2,1,0:T(1,128)S(1)}, u32[]{:S(2)}, u32[]{:S(2)}) async-start(f32[64,1,2176]{2,1,0:T(1,128)} %bitcast.10), calls=%async_computation.1 | async-start | bytes 1114112 | tf_op jit(solution)/shard_map/all_to_all | solution.py:681
  92.1 4.5 %collective-permute-start.9 = (f32[512,256]{1,0:T(8,128)S(1)}, f32[512,256]{1,0:T(8,128)S(1)}, u32[]{:S(2)}, u32[]{:S(2)}) collective-permute-start(f32[512,256]{1,0:T(8,128)S(1)} %bitcast.21), channel_id=1, source_target_pairs={{0,8},{8,0},{1,9},{9,1},{2,10},{10,2},{3,11},{11,3},{4,12},{12,4},... | collective-permute-start | bytes 1572872 | tf_op jit(solution)/shard_map/ppermute | solution.py:686

commit v7 on v6

--- a/solution.py
+++ b/solution.py
@@ -681,8 +681,8 @@
     chunks = lax.all_to_all(chunks.reshape(NCHIP, 1, CH * 128), CHIPS, 0, 0, tiled=True)
     chunks = chunks.reshape(NCHIP * CH, 128)
     own, eff = call(sum_body, [vmem((NCHIP, 8, Z)), vmem((1, 128))], [vm()], nbytes=MIB)(chunks)
+    own = lax.all_to_all(own, CHIPS, 0, 0, tiled=True).reshape(2 * Z, Z)
     own, cot = lax.optimization_barrier((own, cot))
-    own = lax.all_to_all(own, CHIPS, 0, 0, tiled=True).reshape(2 * Z, Z)
     got = lax.ppermute(own, "c", CORE)
     whole = [pltpu.HBM((G, Z, Z), F32)]
     sems = [pltpu.SemaphoreType.DMA((2,))]

time: 98 us -> 98 us (level)
  blocking collectives: 15.8 us -> 24.2 us
  starting transfers between devices: 38.3 us -> 31.5 us
  waiting for transfers between devices: 10.9 us -> 9.31 us
    all_to_all x1, blocking collectives: 15.8 us -> 24.2 us  [body(): lax.all_to_all(chunks.reshape(NCHIP, 1, CH * 128), CHIPS, 0, 0, tiled=True)]
    all_to_all x1, starting transfers between devices: 11.7 us -> 4.79 us  [body(): own = lax.all_to_all(own, CHIPS, 0, 0, tiled=True).reshape(2 * Z, Z)]
    all_to_all x1, waiting for transfers between devices: 5.74 us -> 4.14 us  [body(): own = lax.all_to_all(own, CHIPS, 0, 0, tiled=True).reshape(2 * Z, Z)]
where the time goes in v7:
time: 98 us; the launch traced here: 97.6 us
  starting transfers between devices  31.5 us (32%)
  Pallas kernels  30.9 us (32%)
  blocking collectives  24.2 us (25%)
  waiting for transfers between devices  9.31 us (10%)
  between operations  1.11 us (1%)
    all_to_all x1, blocking collectives, body(): lax.all_to_all(chunks.reshape(NCHIP, 1, CH * 128), CHIPS, 0, 0, tiled=True)  24.2 us
    pallas_call x11, Pallas kernels, go(): run(*[in_hbm(a) if not place or n in far else near_core(a) if a.size >= 8...  23.9 us
    all_to_all x1, starting transfers between devices, body(): pay = lax.all_to_all(pay, ALL, 0, 0, tiled=True)  11.5 us
    pallas_call x1, Pallas kernels, body(): pl.pallas_call(rest_body, grid=(CHUNKS,), out_shape=sds(field), in_specs=...  7.03 us
    ppermute x2, starting transfers between devices, exchange(): lax.ppermute(ta, LAT, LAT_A)  6.3 us
    all_to_all x1, starting transfers between devices, body(): own = lax.all_to_all(own, CHIPS, 0, 0, tiled=True).reshape(2 * Z, Z)  4.79 us
    all_to_all x1, waiting for transfers between devices, body(): own = lax.all_to_all(own, CHIPS, 0, 0, tiled=True).reshape(2 * Z, Z)  4.14 us
    all_to_all x1, waiting for transfers between devices, body(): pay = lax.all_to_all(pay, ALL, 0, 0, tiled=True)  3.89 us
  transfers between devices with their start and end apart: 12, of which 4 were waited for; matrix products, arithmetic and copies ran while one was open for 1% of the time, Pallas kernels for 16%

profile of v7, /device:TPU:1, one launch (start us, length us, event | category | flops | bytes accessed | tf_op | source)
XLA Modules:
  0.0 97.6 jit_solution(14816425995753851663)
XLA Ops:
  0.7 3.0 %shard_map.175 = (f32[5,32,256]{2,1,0:T(8,128)S(1)}, f32[5,32,256]{2,1,0:T(8,128)S(1)}, f32[5,16,256]{2,1,0:T(8,128)S(1)}, f32[5,16,256]{2,1,0:T(8,128)S(1)}, f32[128,128]{1,0:T(8,128)}) custom-call(f32[4,16,32,256]{3,2,1,0:T(8,128)} %refs_3_.1, s32[16,32]{1,0:T(8,128)} %refs_8_.1, s32[16,32]{1,0:T(8,128)} %bitcast.33, s32[1,32]{1,0:T(1,128)} %bitcast.34, ...), custom_call_target="tpu_custom_call" | custom-call | flops 134217728 | bytes 3145728 | tf_op jit(solution)/shard_map/pallas_call | solution.py:62
  3.7 11.5 %all-to-all-start = ((f32[128,1,128]{2,1,0:T(1,128)}), f32[128,1,128]{2,1,0:T(1,128)S(1)}, u32[]{:S(2)}, u32[]{:S(2)}) async-start(f32[128,1,128]{2,1,0:T(1,128)} %bitcast.3), calls=%async_computation | async-start | bytes 131072 | tf_op jit(solution)/shard_map/all_to_all | solution.py:591
  15.2 1.1 %collective-permute-start = (f32[5,32,256]{2,1,0:T(8,128)S(1)}, f32[5,32,256]{2,1,0:T(8,128)S(1)}, u32[]{:S(2)}, u32[]{:S(2)}) collective-permute-start(f32[5,32,256]{2,1,0:T(8,128)S(1)} %get-tuple-element.50), channel_id=1, source_target_pairs={{0,8},{8,0},{16,24},{24,16},{32,40},{40,32},{48,56},{56,48},{64,72... | collective-permute-start | bytes 491528 | tf_op jit(solution)/shard_map/ppermute | solution.py:548
  16.4 0.7 collective-permute-start.1
  17.1 3.1 %collective-permute-start.2 = (f32[5,16,256]{2,1,0:T(8,128)S(1)}, f32[5,16,256]{2,1,0:T(8,128)S(1)}, u32[]{:S(2)}, u32[]{:S(2)}) collective-permute-start(f32[5,16,256]{2,1,0:T(8,128)S(1)} %get-tuple-element.52), channel_id=1, source_target_pairs={{0,1},{1,0},{2,3},{3,2},{4,5},{5,4},{6,7},{7,6},{8,9},{9,8},{10,11... | collective-permute-start | bytes 245768 | tf_op jit(solution)/shard_map/ppermute | solution.py:550
  20.8 3.9 %all-to-all-done = f32[128,1,128]{2,1,0:T(1,128)S(1)} async-done(((f32[128,1,128]{2,1,0:T(1,128)}), f32[128,1,128]{2,1,0:T(1,128)S(1)}, u32[]{:S(2)}, u32[]{:S(2)}) %all-to-all-start) | async-done | bytes 65568 | tf_op jit(solution)/shard_map/all_to_all | solution.py:591
  24.8 4.3 %shard_map.176 = (f32[512,128]{1,0:T(8,128)S(1)}, f32[512,128]{1,0:T(8,128)S(1)}, bf16[512,128]{1,0:T(8,128)(2,1)S(1)}, bf16[4,256,256]{2,1,0:T(8,128)(2,1)S(1)}...) custom-call(f32[4,4]{1,0:T(4,128)S(1)} %copy-done.3, ...), custom_call_target="tpu_custom_call" | custom-call | flops 4294967296 | bytes 16777216 | tf_op jit(solution)/shard_map/pallas_call | solution.py:62
  29.2 5.9 %shard_map.177 = (f32[4,16,32,256]{3,2,1,0:T(8,128)S(1)}, bf16[4,512,256]{2,1,0:T(8,128)(2,1)S(1)}, bf16[4,512,256]{2,1,0:T(8,128)(2,1)S(1)}, f32[8,128]{1,0:T(8...) custom-call(f32[4,4]{1,0:T(4,128)S(1)} %copy-done.3, ...), custom_call_target="tpu_custom_call" | custom-call | flops 1073741824 | bytes 16777216 | tf_op jit(solution)/shard_map/pallas_call | solution.py:62
  35.1 1.1 %collective-permute-start.4 = (f32[4,32,256]{2,1,0:T(8,128)S(1)}, f32[4,32,256]{2,1,0:T(8,128)S(1)}, u32[]{:S(2)}, u32[]{:S(2)}) collective-permute-start(f32[4,32,256]{2,1,0:T(8,128)S(1)} %get-tuple-element.68), channel_id=1, source_target_pairs={{0,8},{8,0},{16,24},{24,16},{32,40},{40,32},{48,56},{56,48},{64,72... | collective-permute-start | bytes 393224 | tf_op jit(solution)/shard_map/ppermute | solution.py:548
  36.4 3.2 %collective-permute-start.6 = (f32[4,16,256]{2,1,0:T(8,128)S(1)}, f32[4,16,256]{2,1,0:T(8,128)S(1)}, u32[]{:S(2)}, u32[]{:S(2)}) collective-permute-start(f32[4,16,256]{2,1,0:T(8,128)S(1)} %get-tuple-element.70), channel_id=1, source_target_pairs={{0,1},{1,0},{2,3},{3,2},{4,5},{5,4},{6,7},{7,6},{8,9},{9,8},{10,11... | collective-permute-start | bytes 196616 | tf_op jit(solution)/shard_map/ppermute | solution.py:550
  39.6 0.8 collective-permute-start.7
  40.4 2.1 %shard_map.179 = (bf16[4,512,256]{2,1,0:T(8,128)(2,1)S(1)}, bf16[4,512,256]{2,1,0:T(8,128)(2,1)S(1)}, f32[4,512,256]{2,1,0:T(8,128)S(1)}, f32[512,128]{1,0:T(8,128)S(1)}) custom-call(f32[4,4]{1,0:T(4,128)S(1)} %copy-done.3, bf16[4,512,256]{2,1,0:T(8,128)(2,1)S(1)} %bitcast.18, bf16[4,256,256]{2,1,0:T(8,128)(2,1)S(1)} %get-tuple-element.62.refs_16_.turn, ...), custom_call_target="tpu_custom_call" | custom-call | flops 4294967296 | bytes 16777216 | tf_op jit(solution)/shard_map/pallas_call | solution.py:62
  42.5 0.8 shard_map.178.refs_20_.kp
  43.3 4.7 %shard_map.180 = (f32[4,512,256]{2,1,0:T(8,128)}, f32[4,512,256]{2,1,0:T(8,128)}, f32[512,128]{1,0:T(8,128)}, f32[512,128]{1,0:T(8,128)}, f32[520,256]{1,0:T(8,1...) custom-call(f32[4,4]{1,0:T(4,128)S(1)} %copy-done.3, f32[4]{0:T(128)S(1)} %copy-done.5, ...), custom_call_target="tpu_custom_call" | custom-call | flops 1073741824 | bytes 16777216 | tf_op jit(solution)/shard_map/pallas_call | solution.py:62
  48.1 1.3 %collective-permute-start.8 = (f32[520,256]{1,0:T(8,128)S(1)}, f32[520,256]{1,0:T(8,128)S(1)}, u32[]{:S(2)}, u32[]{:S(2)}) collective-permute-start(f32[520,256]{1,0:T(8,128)S(1)} %get-tuple-element.80.send), channel_id=1, source_target_pairs={{0,8},{8,0},{1,9},{9,1},{2,10},{10,2},{3,11},{11,3},{4,12},{12,4},... | collective-permute-start | bytes 1597448 | tf_op jit(solution)/shard_map/ppermute | solution.py:676
  49.9 1.1 %collective-permute-done.8.got = f32[520,256]{1,0:T(8,128)S(1)} collective-permute-done((f32[520,256]{1,0:T(8,128)S(1)}, f32[520,256]{1,0:T(8,128)S(1)}, u32[]{:S(2)}, u32[]{:S(2)}) %collective-permute-start.8) | collective-permute-done | bytes 532512 | tf_op jit(solution)/shard_map/ppermute | solution.py:676
  51.0 24.2 %all_to_all.22 = f32[64,1,2176]{2,1,0:T(1,128)S(1)} all-to-all(f32[64,1,2176]{2,1,0:T(1,128)S(1)} %bitcast.20), channel_id=1, replica_groups=mesh['zl'=2,'x'=4,'c'=2,'y'=4,'zh'=2] {'zl','x','y','zh'}, dimensions={0} | all-to-all | bytes 1114112 | tf_op jit(solution)/shard_map/all_to_all | solution.py:681
  75.2 0.9 shard_map.183
  76.1 4.8 %all-to-all-start.2 = ((f32[64,8,256]{2,1,0:T(8,128)}), f32[64,8,256]{2,1,0:T(8,128)S(1)}, u32[]{:S(2)}, u32[]{:S(2)}) async-start(f32[64,8,256]{2,1,0:T(8,128)} %get-tuple-element.81), calls=%async_computation.2 | async-start | bytes 1048576 | tf_op jit(solution)/shard_map/all_to_all | solution.py:684
  80.9 7.0 %shard_map.184 = f32[4,512,256]{2,1,0:T(8,128)} custom-call(f32[4,4]{1,0:T(4,128)S(1)} %copy-done.3, f32[4]{0:T(128)S(1)} %copy-done.5, bf16[4,512,256]{2,1,0:T(8,128)(2,1)} %bitcast.17, f32[4,512,256]{2,1,0:T(8,128)} %get-tuple-element.82.m_in, f32[4,512,256]{2,1,0:T(8,128)} %get-tuple-element.83.ge_in, f32[512,128]{1,0:T(8,128)} %get-tuple-element.84.q_in, ...), custom_call_target="tpu_custom_call" | custom-call | flops 1073741824 | bytes 12582912 | tf_op jit(solution)/shard_map/pallas_call | solution.py:662
  88.0 4.1 %all-to-all-done.2 = f32[64,8,256]{2,1,0:T(8,128)S(1)} async-done(((f32[64,8,256]{2,1,0:T(8,128)}), f32[64,8,256]{2,1,0:T(8,128)S(1)}, u32[]{:S(2)}, u32[]{:S(2)}) %all-to-all-start.2) | async-done | bytes 524320 | tf_op jit(solution)/shard_map/all_to_all | solution.py:684
  92.1 3.0 %collective-permute-start.9 = (f32[512,256]{1,0:T(8,128)S(1)}, f32[512,256]{1,0:T(8,128)S(1)}, u32[]{:S(2)}, u32[]{:S(2)}) collective-permute-start(f32[512,256]{1,0:T(8,128)S(1)} %bitcast.22), channel_id=1, source_target_pairs={{0,8},{8,0},{1,9},{9,1},{2,10},{10,2},{3,11},{11,3},{4,12},{12,4},... | collective-permute-start | bytes 1572872 | tf_op jit(solution)/shard_map/ppermute | solution.py:686
  95.6 0.8 shard_map.185._
  96.7 0.8 shard_map.186
  (36 shorter events, 2.1 us)
Async XLA Ops:
  0.6 24.1 %copy-start.4 = (s32[16,32]{1,0:T(8,128)S(1)}, s32[16,32]{1,0:T(8,128)}, u32[]{:S(2)}) copy-start(s32[16,32]{1,0:T(8,128)} %refs_8_.1) | copy-start | bytes 6148
  0.6 24.1 %copy-start.8 = (f32[256]{0:T(256)S(1)}, f32[256]{0:T(256)}, u32[]{:S(2)}) copy-start(f32[256]{0:T(256)} %param.30) | copy-start | bytes 3076
  0.7 24.1 %copy-start.10 = (f32[64]{0:T(128)S(1)}, f32[64]{0:T(128)}, u32[]{:S(2)}) copy-start(f32[64]{0:T(128)} %param.24) | copy-start | bytes 772
  0.7 24.1 %copy-start.9 = (s32[16,32]{1,0:T(8,128)S(1)}, s32[16,32]{1,0:T(8,128)}, u32[]{:S(2)}) copy-start(s32[16,32]{1,0:T(8,128)} %refs_9_.1) | copy-start | bytes 6148
  0.7 24.1 %copy-start.1 = (bf16[4,256,256]{2,1,0:T(8,128)(2,1)S(1)}, bf16[4,256,256]{2,1,0:T(8,128)(2,1)}, u32[]{:S(2)}) copy-start(bf16[4,256,256]{2,1,0:T(8,128)(2,1)} %ker.1) | copy-start | bytes 1572868
  0.7 24.1 %copy-start.3 = (f32[4,4]{1,0:T(4,128)S(1)}, f32[4,4]{1,0:T(4,128)}, u32[]{:S(2)}) copy-start(f32[4,4]{1,0:T(4,128)} %mix.3) | copy-start | bytes 196
  0.7 24.1 %copy-start.5 = (f32[4]{0:T(128)S(1)}, f32[4]{0:T(128)}, u32[]{:S(2)}) copy-start(f32[4]{0:T(128)} %assim.1) | copy-start | bytes 52
  0.7 24.1 %copy-start.6 = (f32[4,256]{1,0:T(4,128)S(1)}, f32[4,256]{1,0:T(4,128)}, u32[]{:S(2)}) copy-start(f32[4,256]{1,0:T(4,128)} %mort.1) | copy-start | bytes 12292
  0.7 24.1 %copy-start.2 = (f32[4,256]{1,0:T(4,128)S(1)}, f32[4,256]{1,0:T(4,128)}, u32[]{:S(2)}) copy-start(f32[4,256]{1,0:T(4,128)} %sel.3) | copy-start | bytes 12292
  3.7 21.0 %all-to-all-start = ((f32[128,1,128]{2,1,0:T(1,128)}), f32[128,1,128]{2,1,0:T(1,128)S(1)}, u32[]{:S(2)}, u32[]{:S(2)}) async-start(f32[128,1,128]{2,1,0:T(1,128)} %bitcast.3), calls=%async_computation | async-start | bytes 131072 | tf_op jit(solution)/shard_map/all_to_all | solution.py:591
  15.2 14.0 %collective-permute-start = (f32[5,32,256]{2,1,0:T(8,128)S(1)}, f32[5,32,256]{2,1,0:T(8,128)S(1)}, u32[]{:S(2)}, u32[]{:S(2)}) collective-permute-start(f32[5,32,256]{2,1,0:T(8,128)S(1)} %get-tuple-element.50), channel_id=1, source_target_pairs={{0,8},{8,0},{16,24},{24,16},{32,40},{40,32},{48,56},{56,48},{64,72... | collective-permute-start | bytes 491528 | tf_op jit(solution)/shard_map/ppermute | solution.py:548
  16.4 12.8 %collective-permute-start.1 = (f32[5,32,256]{2,1,0:T(8,128)S(1)}, f32[5,32,256]{2,1,0:T(8,128)S(1)}, u32[]{:S(2)}, u32[]{:S(2)}) collective-permute-start(f32[5,32,256]{2,1,0:T(8,128)S(1)} %get-tuple-element.51), channel_id=1, source_target_pairs={{0,120},{8,16},{16,8},{24,32},{32,24},{40,48},{48,40},{56,64},{64,... | collective-permute-start | bytes 491528 | tf_op jit(solution)/shard_map/ppermute | solution.py:549
  17.1 12.1 %collective-permute-start.2 = (f32[5,16,256]{2,1,0:T(8,128)S(1)}, f32[5,16,256]{2,1,0:T(8,128)S(1)}, u32[]{:S(2)}, u32[]{:S(2)}) collective-permute-start(f32[5,16,256]{2,1,0:T(8,128)S(1)} %get-tuple-element.52), channel_id=1, source_target_pairs={{0,1},{1,0},{2,3},{3,2},{4,5},{5,4},{6,7},{7,6},{8,9},{9,8},{10,11... | collective-permute-start | bytes 245768 | tf_op jit(solution)/shard_map/ppermute | solution.py:550
  20.2 9.0 %collective-permute-start.3 = (f32[5,16,256]{2,1,0:T(8,128)S(1)}, f32[5,16,256]{2,1,0:T(8,128)S(1)}, u32[]{:S(2)}, u32[]{:S(2)}) collective-permute-start(f32[5,16,256]{2,1,0:T(8,128)S(1)} %get-tuple-element.53), channel_id=1, source_target_pairs={{1,2},{2,1},{3,4},{4,3},{5,6},{6,5},{9,10},{10,9},{11,12},{12,11},... | collective-permute-start | bytes 245768 | tf_op jit(solution)/shard_map/ppermute | solution.py:551
  24.8 4.4 %copy-start.7 = (f32[256]{0:T(256)S(1)}, f32[256]{0:T(256)}, u32[]{:S(2)}) copy-start(f32[256]{0:T(256)} %param.31) | copy-start | bytes 3076
  29.2 11.2 %copy-start = (bf16[4,16,32,256]{3,2,1,0:T(8,128)(2,1)S(1)}, bf16[4,16,32,256]{3,2,1,0:T(8,128)(2,1)}, u32[]{:S(2)}) copy-start(bf16[4,16,32,256]{3,2,1,0:T(8,128)(2,1)} %param.17) | copy-start | bytes 3145732
  35.1 8.1 %collective-permute-start.4 = (f32[4,32,256]{2,1,0:T(8,128)S(1)}, f32[4,32,256]{2,1,0:T(8,128)S(1)}, u32[]{:S(2)}, u32[]{:S(2)}) collective-permute-start(f32[4,32,256]{2,1,0:T(8,128)S(1)} %get-tuple-element.68), channel_id=1, source_target_pairs={{0,8},{8,0},{16,24},{24,16},{32,40},{40,32},{48,56},{56,48},{64,72... | collective-permute-start | bytes 393224 | tf_op jit(solution)/shard_map/ppermute | solution.py:548
  36.3 7.0 %collective-permute-start.5 = (f32[4,32,256]{2,1,0:T(8,128)S(1)}, f32[4,32,256]{2,1,0:T(8,128)S(1)}, u32[]{:S(2)}, u32[]{:S(2)}) collective-permute-start(f32[4,32,256]{2,1,0:T(8,128)S(1)} %get-tuple-element.69), channel_id=1, source_target_pairs={{0,120},{8,16},{16,8},{24,32},{32,24},{40,48},{48,40},{56,64},{64,... | collective-permute-start | bytes 393224 | tf_op jit(solution)/shard_map/ppermute | solution.py:549
  36.4 6.9 %collective-permute-start.6 = (f32[4,16,256]{2,1,0:T(8,128)S(1)}, f32[4,16,256]{2,1,0:T(8,128)S(1)}, u32[]{:S(2)}, u32[]{:S(2)}) collective-permute-start(f32[4,16,256]{2,1,0:T(8,128)S(1)} %get-tuple-element.70), channel_id=1, source_target_pairs={{0,1},{1,0},{2,3},{3,2},{4,5},{5,4},{6,7},{7,6},{8,9},{9,8},{10,11... | collective-permute-start | bytes 196616 | tf_op jit(solution)/shard_map/ppermute | solution.py:550
  39.6 3.7 %collective-permute-start.7 = (f32[4,16,256]{2,1,0:T(8,128)S(1)}, f32[4,16,256]{2,1,0:T(8,128)S(1)}, u32[]{:S(2)}, u32[]{:S(2)}) collective-permute-start(f32[4,16,256]{2,1,0:T(8,128)S(1)} %get-tuple-element.71), channel_id=1, source_target_pairs={{1,2},{2,1},{3,4},{4,3},{5,6},{6,5},{9,10},{10,9},{11,12},{12,11},... | collective-permute-start | bytes 196616 | tf_op jit(solution)/shard_map/ppermute | solution.py:551
  48.1 2.9 %collective-permute-start.8 = (f32[520,256]{1,0:T(8,128)S(1)}, f32[520,256]{1,0:T(8,128)S(1)}, u32[]{:S(2)}, u32[]{:S(2)}) collective-permute-start(f32[520,256]{1,0:T(8,128)S(1)} %get-tuple-element.80.send), channel_id=1, source_target_pairs={{0,8},{8,0},{1,9},{9,1},{2,10},{10,2},{3,11},{11,3},{4,12},{12,4},... | collective-permute-start | bytes 1597448 | tf_op jit(solution)/shard_map/ppermute | solution.py:676
  76.1 16.0 %all-to-all-start.2 = ((f32[64,8,256]{2,1,0:T(8,128)}), f32[64,8,256]{2,1,0:T(8,128)S(1)}, u32[]{:S(2)}, u32[]{:S(2)}) async-start(f32[64,8,256]{2,1,0:T(8,128)} %get-tuple-element.81), calls=%async_computation.2 | async-start | bytes 1048576 | tf_op jit(solution)/shard_map/all_to_all | solution.py:684
  92.1 4.5 %collective-permute-start.9 = (f32[512,256]{1,0:T(8,128)S(1)}, f32[512,256]{1,0:T(8,128)S(1)}, u32[]{:S(2)}, u32[]{:S(2)}) collective-permute-start(f32[512,256]{1,0:T(8,128)S(1)} %bitcast.22), channel_id=1, source_target_pairs={{0,8},{8,0},{1,9},{9,1},{2,10},{10,2},{3,11},{11,3},{4,12},{12,4},... | collective-permute-start | bytes 1572872 | tf_op jit(solution)/shard_map/ppermute | solution.py:686
